TPU v7x, 128 devices: a whole 4x4x4 slice. The times are simulated.
128 devices in a mesh: ctx: 32 (over z, x, y_lo), fsdp: 4 (over y_hi, core).
Axes of the slice: x: 4, y: 4 (y_hi: 2, y_lo: 2; y = y_hi * 2 + y_lo), z: 4, core: 2. Of those that a mesh axis runs over, the one named last changes fastest.
Arguments:
- tokens: bfloat16 [4, 4096, 1088], P('fsdp', 'ctx'), may hold values from -6 to 6
- cotangent: bfloat16 [4, 4096, 1088], P('fsdp', 'ctx'), may hold values from -6 to 6
- ln1_scale: bfloat16 [1088], P('fsdp'), may hold values from 0.5 to 1.5
- ln1_bias: bfloat16 [1088], P('fsdp'), may hold values from -1.5 to 1.5
- w_qkv: bfloat16 [1088, 3264], P('fsdp'), may hold values from -0.1875 to 0.1875
- bias_q: bfloat16 [1088], P('fsdp'), may hold values from -1.5 to 1.5
- bias_v: bfloat16 [1088], P('fsdp'), may hold values from -1.5 to 1.5
- w_out: bfloat16 [1088, 1088], P('fsdp'), may hold values from -3 to 3
- bias_out: bfloat16 [1088], P('fsdp'), may hold values from -1.5 to 1.5
- ln2_scale: bfloat16 [1088], P('fsdp'), may hold values from 0.5 to 1.5
- ln2_bias: bfloat16 [1088], P('fsdp'), may hold values from -1.5 to 1.5
- w_fc: bfloat16 [1088, 4352], P('fsdp'), may hold values from -0.1875 to 0.1875
- bias_fc: bfloat16 [4352], P('fsdp'), may hold values from -1.5 to 1.5
- w_down: bfloat16 [4352, 1088], P('fsdp'), may hold values from -0.09375 to 0.09375
- bias_down: bfloat16 [1088], P('fsdp'), may hold values from -1.5 to 1.5
Outputs:
- outputs: bfloat16 [4, 4096, 1088], P('fsdp', 'ctx')
- grad_tokens: float32 [4, 4096, 1088], P('fsdp', 'ctx')
- d_ln1_scale: float32 [1088], P('fsdp')
- d_ln1_bias: float32 [1088], P('fsdp')
- d_w_qkv: float32 [1088, 3264], P('fsdp')
- d_bias_q: float32 [1088], P('fsdp')
- d_bias_v: float32 [1088], P('fsdp')
- d_w_out: float32 [1088, 1088], P('fsdp')
- d_bias_out: float32 [1088], P('fsdp')
- d_ln2_scale: float32 [1088], P('fsdp')
- d_ln2_bias: float32 [1088], P('fsdp')
- d_w_fc: float32 [1088, 4352], P('fsdp')
- d_bias_fc: float32 [4352], P('fsdp')
- d_w_down: float32 [4352, 1088], P('fsdp')
- d_bias_down: float32 [1088], P('fsdp')
All inputs are finite; a program needn't handle non-finite values.
Results may differ from a plain program's by a relative error of at most 0.025.
Values may be sent and summed in bfloat16 or wider, within the bound.
A program may use at most 256 MiB of HBM per device.

v0:
```python
import math

import jax
import jax.numpy as jnp
from jax import lax
from jax.sharding import PartitionSpec as P

HEAD_DIM = 64


def norm_rows(values, gain_vec, offset):
    centre = values - jnp.mean(values, axis=-1, keepdims=True)
    spread = jnp.mean(centre * centre, axis=-1, keepdims=True)
    return centre * lax.rsqrt(spread + 1e-05) * gain_vec + offset


def gelu_tanh(values):
    return (
        0.5
        * values
        * (1.0 + jnp.tanh(0.7978845608028654 * (values + 0.044715 * values * values * values)))
    )


def dealt_positions(row_count, per_device, first_device, device_count):
    row_ids = jnp.arange(row_count, dtype=jnp.int32)
    device = first_device + row_ids // per_device
    within = row_ids % per_device
    half_size = per_device // 2
    block_id = jnp.where(within < half_size, device, 2 * device_count - 1 - device)
    return block_id * half_size + within % half_size


def block_scores(query_heads, key_heads, query_places, key_places, scaling):
    scores = (
        jnp.einsum("qhd,khd->hqk", query_heads, key_heads, preferred_element_type=jnp.float32)
        * scaling
    )
    allowed = key_places[None, None, :] <= query_places[None, :, None]
    return jnp.where(allowed, scores, -1e30)


def score_grads(
    query_heads,
    grad_heads,
    key_heads,
    value_heads,
    query_places,
    key_places,
    lse_rows,
    delta_rows,
    scaling,
):
    scores = block_scores(query_heads, key_heads, query_places, key_places, scaling)
    probabilities = jnp.exp(scores - lse_rows[..., None])
    grad_probs = jnp.einsum(
        "qhd,khd->hqk", grad_heads, value_heads, preferred_element_type=jnp.float32
    )
    grad_scores = (probabilities * (grad_probs - delta_rows[..., None])).astype(jnp.bfloat16)
    return (probabilities.astype(jnp.bfloat16), grad_scores)


def local(
    tokens,
    cotangent,
    ln1_scale,
    ln1_bias,
    w_qkv,
    bias_q,
    bias_v,
    w_out,
    bias_out,
    ln2_scale,
    ln2_bias,
    w_fc,
    bias_fc,
    w_down,
    bias_down,
):
    ctx_count = lax.axis_size("ctx")
    my_index = lax.axis_index("ctx")
    local_rows = tokens.shape[1]
    model_width = tokens.shape[2]
    seq_length = local_rows * ctx_count
    head_size = HEAD_DIM
    head_count = model_width // head_size
    scaling = 1.0 / math.sqrt(head_size)
    key_block = math.gcd(512, seq_length)
    block_count = seq_length // key_block
    gathered = (
        lax.all_gather(ln1_scale, "fsdp", axis=0, tiled=True),
        lax.all_gather(ln1_bias, "fsdp", axis=0, tiled=True),
        lax.all_gather(w_qkv, "fsdp", axis=0, tiled=True),
        lax.all_gather(bias_q, "fsdp", axis=0, tiled=True),
        lax.all_gather(bias_v, "fsdp", axis=0, tiled=True),
        lax.all_gather(w_out, "fsdp", axis=0, tiled=True),
        lax.all_gather(bias_out, "fsdp", axis=0, tiled=True),
        lax.all_gather(ln2_scale, "fsdp", axis=0, tiled=True),
        lax.all_gather(ln2_bias, "fsdp", axis=0, tiled=True),
        lax.all_gather(w_fc, "fsdp", axis=0, tiled=True),
        lax.all_gather(bias_fc, "fsdp", axis=0, tiled=True),
        lax.all_gather(w_down, "fsdp", axis=0, tiled=True),
        lax.all_gather(bias_down, "fsdp", axis=0, tiled=True),
    )
    (
        g_scale1,
        g_shift1,
        full_qkv,
        full_bq,
        full_bv,
        full_out,
        full_bout,
        g_scale2,
        g_shift2,
        full_fc,
        full_bfc,
        full_down,
        full_bdown,
    ) = gathered
    scale_one = g_scale1.astype(jnp.float32)
    shift_one = g_shift1.astype(jnp.float32)
    scale_two = g_scale2.astype(jnp.float32)
    shift_two = g_shift2.astype(jnp.float32)
    inputs32 = tokens[0].astype(jnp.float32)
    norm_one, norm_one_pull = jax.vjp(norm_rows, inputs32, scale_one, shift_one)
    normed = norm_one.astype(jnp.bfloat16)
    joint_rows = jnp.dot(normed, full_qkv, preferred_element_type=jnp.float32)
    queries = (joint_rows[:, :model_width] + full_bq.astype(jnp.float32)).astype(jnp.bfloat16)
    key_rows = joint_rows[:, model_width : 2 * model_width].astype(jnp.bfloat16)
    value_rows = (joint_rows[:, 2 * model_width :] + full_bv.astype(jnp.float32)).astype(
        jnp.bfloat16
    )
    all_keys, all_values = (
        lax.all_gather(key_rows, "ctx", axis=0, tiled=True),
        lax.all_gather(value_rows, "ctx", axis=0, tiled=True),
    )
    query_places = dealt_positions(local_rows, local_rows, my_index, ctx_count)
    key_places = dealt_positions(seq_length, local_rows, 0, ctx_count)
    heads_q = queries.reshape(local_rows, head_count, head_size)
    keys_blocks = all_keys.reshape(block_count, key_block, head_count, head_size)
    values_blocks = all_values.reshape(block_count, key_block, head_count, head_size)
    places_blocks = key_places.reshape(block_count, key_block)
    key_inputs = (keys_blocks, values_blocks, places_blocks)

    def forward_step(carry, entry):
        run_max, run_sum, accum = carry
        key_heads, value_heads, places_here = entry
        scores = block_scores(heads_q, key_heads, query_places, places_here, scaling)
        new_max = jnp.maximum(run_max, jnp.max(scores, axis=-1))
        factor = jnp.exp(run_max - new_max)
        weights = jnp.exp(scores - new_max[..., None])
        run_sum = run_sum * factor + jnp.sum(weights, axis=-1)
        accum = accum * jnp.transpose(factor)[:, :, None] + jnp.einsum(
            "hqk,khd->qhd",
            weights.astype(jnp.bfloat16),
            value_heads,
            preferred_element_type=jnp.float32,
        )
        return ((new_max, run_sum, accum), None)

    start_max = jnp.full((head_count, local_rows), -1e30, jnp.float32)
    start_sum = jnp.zeros((head_count, local_rows), jnp.float32)
    start_accum = jnp.zeros((local_rows, head_count, head_size), jnp.float32)
    (final_max, final_sum, final_accum), unused = lax.scan(
        forward_step, (start_max, start_sum, start_accum), key_inputs
    )
    lse_rows = final_max + jnp.log(final_sum)
    out_heads = final_accum / jnp.transpose(final_sum)[:, :, None]
    attended = out_heads.reshape(local_rows, model_width).astype(jnp.bfloat16)
    branch = jnp.dot(attended, full_out, preferred_element_type=jnp.float32) + full_bout.astype(
        jnp.float32
    )
    middle = inputs32 + branch
    norm_two, norm_two_pull = jax.vjp(norm_rows, middle, scale_two, shift_two)
    normed2 = norm_two.astype(jnp.bfloat16)
    hidden_pre = jnp.dot(normed2, full_fc, preferred_element_type=jnp.float32) + full_bfc.astype(
        jnp.float32
    )
    gelu_value, gelu_pull = jax.vjp(gelu_tanh, hidden_pre)
    active = gelu_value.astype(jnp.bfloat16)
    out_branch = jnp.dot(active, full_down, preferred_element_type=jnp.float32) + full_bdown.astype(
        jnp.float32
    )
    result = (middle + out_branch).astype(jnp.bfloat16)
    upstream = cotangent[0].astype(jnp.float32)
    grad_branch2 = cotangent[0]
    d_down = jnp.einsum("tf,td->fd", active, grad_branch2, preferred_element_type=jnp.float32)
    d_bdown = jnp.sum(upstream, axis=0)
    grad_active = jnp.einsum(
        "td,fd->tf", grad_branch2, full_down, preferred_element_type=jnp.float32
    )
    grad_hidden = gelu_pull(grad_active)[0].astype(jnp.bfloat16)
    d_fc = jnp.einsum("td,tf->df", normed2, grad_hidden, preferred_element_type=jnp.float32)
    d_bfc = jnp.sum(grad_hidden.astype(jnp.float32), axis=0)
    grad_normed2 = jnp.einsum("tf,df->td", grad_hidden, full_fc, preferred_element_type=jnp.float32)
    grad_mid_part, d_scale2, d_shift2 = norm_two_pull(grad_normed2)
    grad_middle = upstream + grad_mid_part
    grad_branch = grad_middle.astype(jnp.bfloat16)
    d_out = jnp.einsum("td,te->de", attended, grad_branch, preferred_element_type=jnp.float32)
    d_bout = jnp.sum(grad_branch.astype(jnp.float32), axis=0)
    grad_attended = jnp.einsum(
        "te,de->td", grad_branch, full_out, preferred_element_type=jnp.float32
    ).astype(jnp.bfloat16)
    grad_heads = grad_attended.reshape(local_rows, head_count, head_size)
    row_delta = jnp.einsum("qhd,qhd->hq", grad_heads.astype(jnp.float32), out_heads)
    start_query = jnp.zeros((local_rows, head_count, head_size), jnp.float32)

    def main_step(accum, entry):
        key_heads, value_heads, places_here = entry
        low_probs, grad_scores = score_grads(
            heads_q,
            grad_heads,
            key_heads,
            value_heads,
            query_places,
            places_here,
            lse_rows,
            row_delta,
            scaling,
        )
        accum = (
            accum
            + jnp.einsum("hqk,khd->qhd", grad_scores, key_heads, preferred_element_type=jnp.float32)
            * scaling
        )
        grad_keys = (
            jnp.einsum("hqk,qhd->khd", grad_scores, heads_q, preferred_element_type=jnp.float32)
            * scaling
        )
        grad_values = jnp.einsum(
            "hqk,qhd->khd", low_probs, grad_heads, preferred_element_type=jnp.float32
        )
        return (
            accum,
            (
                grad_keys.reshape(key_block, model_width),
                grad_values.reshape(key_block, model_width),
            ),
        )

    grad_query_heads, (key_terms, value_terms) = lax.scan(main_step, start_query, key_inputs)
    key_terms = key_terms.reshape(seq_length, model_width)
    value_terms = value_terms.reshape(seq_length, model_width)
    own_keys, own_values = (
        lax.psum_scatter(
            key_terms.astype(jnp.bfloat16), "ctx", scatter_dimension=0, tiled=True
        ).astype(jnp.float32),
        lax.psum_scatter(
            value_terms.astype(jnp.bfloat16), "ctx", scatter_dimension=0, tiled=True
        ).astype(jnp.float32),
    )
    grad_q16 = grad_query_heads.reshape(local_rows, model_width).astype(jnp.bfloat16)
    grad_k16 = own_keys.astype(jnp.bfloat16)
    grad_v16 = own_values.astype(jnp.bfloat16)
    grad_joint = jnp.concatenate([grad_q16, grad_k16, grad_v16], axis=1)
    d_qkv = jnp.einsum("td,te->de", normed, grad_joint, preferred_element_type=jnp.float32)
    d_bq = jnp.sum(grad_q16.astype(jnp.float32), axis=0)
    d_bv = jnp.sum(grad_v16.astype(jnp.float32), axis=0)
    grad_normed = jnp.einsum("te,de->td", grad_joint, full_qkv, preferred_element_type=jnp.float32)
    grad_in_part, d_scale1, d_shift1 = norm_one_pull(grad_normed)
    grad_inputs = grad_middle + grad_in_part
    shard_terms = (
        lax.psum_scatter(
            d_scale1.astype(jnp.bfloat16), "fsdp", scatter_dimension=0, tiled=True
        ).astype(jnp.float32),
        lax.psum_scatter(
            d_shift1.astype(jnp.bfloat16), "fsdp", scatter_dimension=0, tiled=True
        ).astype(jnp.float32),
        lax.psum_scatter(
            d_qkv.astype(jnp.bfloat16), "fsdp", scatter_dimension=0, tiled=True
        ).astype(jnp.float32),
        lax.psum_scatter(d_bq.astype(jnp.bfloat16), "fsdp", scatter_dimension=0, tiled=True).astype(
            jnp.float32
        ),
        lax.psum_scatter(d_bv.astype(jnp.bfloat16), "fsdp", scatter_dimension=0, tiled=True).astype(
            jnp.float32
        ),
        lax.psum_scatter(
            d_out.astype(jnp.bfloat16), "fsdp", scatter_dimension=0, tiled=True
        ).astype(jnp.float32),
        lax.psum_scatter(
            d_bout.astype(jnp.bfloat16), "fsdp", scatter_dimension=0, tiled=True
        ).astype(jnp.float32),
        lax.psum_scatter(
            d_scale2.astype(jnp.bfloat16), "fsdp", scatter_dimension=0, tiled=True
        ).astype(jnp.float32),
        lax.psum_scatter(
            d_shift2.astype(jnp.bfloat16), "fsdp", scatter_dimension=0, tiled=True
        ).astype(jnp.float32),
        lax.psum_scatter(d_fc.astype(jnp.bfloat16), "fsdp", scatter_dimension=0, tiled=True).astype(
            jnp.float32
        ),
        lax.psum_scatter(
            d_bfc.astype(jnp.bfloat16), "fsdp", scatter_dimension=0, tiled=True
        ).astype(jnp.float32),
        lax.psum_scatter(
            d_down.astype(jnp.bfloat16), "fsdp", scatter_dimension=0, tiled=True
        ).astype(jnp.float32),
        lax.psum_scatter(
            d_bdown.astype(jnp.bfloat16), "fsdp", scatter_dimension=0, tiled=True
        ).astype(jnp.float32),
    )
    totals = (
        lax.psum(shard_terms[0].astype(jnp.bfloat16), "ctx").astype(jnp.float32),
        lax.psum(shard_terms[1].astype(jnp.bfloat16), "ctx").astype(jnp.float32),
        lax.psum(shard_terms[2].astype(jnp.bfloat16), "ctx").astype(jnp.float32),
        lax.psum(shard_terms[3].astype(jnp.bfloat16), "ctx").astype(jnp.float32),
        lax.psum(shard_terms[4].astype(jnp.bfloat16), "ctx").astype(jnp.float32),
        lax.psum(shard_terms[5].astype(jnp.bfloat16), "ctx").astype(jnp.float32),
        lax.psum(shard_terms[6].astype(jnp.bfloat16), "ctx").astype(jnp.float32),
        lax.psum(shard_terms[7].astype(jnp.bfloat16), "ctx").astype(jnp.float32),
        lax.psum(shard_terms[8].astype(jnp.bfloat16), "ctx").astype(jnp.float32),
        lax.psum(shard_terms[9].astype(jnp.bfloat16), "ctx").astype(jnp.float32),
        lax.psum(shard_terms[10].astype(jnp.bfloat16), "ctx").astype(jnp.float32),
        lax.psum(shard_terms[11].astype(jnp.bfloat16), "ctx").astype(jnp.float32),
        lax.psum(shard_terms[12].astype(jnp.bfloat16), "ctx").astype(jnp.float32),
    )
    return (result[None], grad_inputs[None]) + tuple(totals)


def solution(mesh):
    placed = (
        P("fsdp", "ctx", None),
        P("fsdp", "ctx", None),
        P("fsdp"),
        P("fsdp"),
        P("fsdp", None),
        P("fsdp"),
        P("fsdp"),
        P("fsdp", None),
        P("fsdp"),
        P("fsdp"),
        P("fsdp"),
        P("fsdp", None),
        P("fsdp"),
        P("fsdp", None),
        P("fsdp"),
    )
    return jax.shard_map(
        local,
        mesh=mesh,
        in_specs=placed,
        out_specs=(
            P("fsdp", "ctx", None),
            P("fsdp", "ctx", None),
            P("fsdp"),
            P("fsdp"),
            P("fsdp", None),
            P("fsdp"),
            P("fsdp"),
            P("fsdp", None),
            P("fsdp"),
            P("fsdp"),
            P("fsdp"),
            P("fsdp", None),
            P("fsdp"),
            P("fsdp", None),
            P("fsdp"),
        ),
        check_vma=False,
    )
```

profile of v0, /device:TPU:8, one launch (start us, length us, event | category | flops | bytes accessed | tf_op | source)
XLA Modules:
  0.0 1971.2 jit_solution(4137451576188601948)
XLA Ops:
  17.6 16.3 all-reduce.21
  35.3 32.2 %all-gather.7.cloned.1.call-done = bf16[1088,3264]{1,0:T(8,128)(2,1)} async-done(((bf16[272,3264]{1,0:T(8,128)(2,1)}), bf16[1088,3264]{1,0:T(8,128)(2,1)}) %all-gather.7.cloned.1.call-update) | async-done | bytes 7102480 | tf_op jit(solution)/shard_map/all_gather | solution.py:93
  77.9 245.5 %all-gather.9.cloned.1.call-done = bf16[4096,1088]{0,1:T(8,128)(2,1)} async-done(((bf16[128,1088]{0,1:T(8,128)(2,1)}), bf16[4096,1088]{0,1:T(8,128)(2,1)}) %all-gather.9.cloned.1.call-update) | async-done | bytes 8912912 | tf_op jit(solution)/shard_map/all_gather | solution.py:134
  323.4 12.9 copy.78
  336.4 10.2 copy.52
  346.6 226.4 %all-gather.11.cloned.1.call-done = bf16[4096,1088]{0,1:T(8,128)(2,1)} async-done(((bf16[128,1088]{0,1:T(8,128)(2,1)}), bf16[4096,1088]{0,1:T(8,128)(2,1)}) %all-gather.11.cloned.1.call-update) | async-done | bytes 8912912 | tf_op jit(solution)/shard_map/all_gather | solution.py:135
  573.0 13.4 copy.79
  586.4 10.2 copy.53
  596.6 90.0 %while.30 = (s32[]{:T(128)}, f32[17,128]{1,0:T(8,128)S(1)}, f32[17,128]{1,0:T(8,128)S(1)}, f32[128,17,64]{0,2,1:T(8,128)S(1)}, s32[8,512]{1,0:T(8,128)S(1)}, /*i...) while((s32[]{:T(128)}, f32[17,128]{1,0:T(8,128)S(1)}, ...), condition=%wide.region_5.6_spmd.clone, body=%wide.region_2.5_spmd.clone.sunk | while | flops 297968000 | bytes 35224748 | solution.py:164
  696.2 47.4 %all-gather.17.cloned.1.call-done = bf16[4352,1088]{1,0:T(8,128)(2,1)} async-done(((bf16[1088,1088]{1,0:T(8,128)(2,1)}), bf16[4352,1088]{1,0:T(8,128)(2,1)}) %all-gather.17.cloned.1.call-update) | async-done | bytes 9469968 | tf_op jit(solution)/shard_map/all_gather | solution.py:102
  743.6 7.5 fusion.114
  757.2 112.7 %while.31 = (s32[]{:T(128)}, f32[128,17,64]{0,2,1:T(8,128)}, bf16[8,512,1088]{1,2,0:T(8,128)(2,1)}, bf16[8,512,1088]{1,2,0:T(8,128)(2,1)}, bf16[8,512,17,64]{1,3...) while((s32[]{:T(128)}, f32[128,17,64]{0,2,1:T(8,128)}, ...), condition=%wide.region_11.12_spmd.clone, body=%wide.region_10.11_spmd.clone.sunk | while | flops 725773952 | bytes 70419232 | solution.py:241
  869.9 11.9 copy.74
  881.8 11.9 copy.73
  911.1 179.9 %reduce-scatter.21.cloned.1.call-done = bf16[128,1088]{1,0:T(8,128)(2,1)} async-done(((bf16[4096,1088]{1,0:T(8,128)(2,1)}), bf16[128,1088]{1,0:T(8,128)(2,1)}) %reduce-scatter.21.cloned.1.call-update) | async-done | bytes 278544
  1092.1 209.8 %reduce-scatter.19.cloned.1.call-done = bf16[128,1088]{1,0:T(8,128)(2,1)} async-done(((bf16[4096,1088]{1,0:T(8,128)(2,1)}), bf16[128,1088]{1,0:T(8,128)(2,1)}) %reduce-scatter.19.cloned.1.call-update) | async-done | bytes 278544
  1308.3 37.3 %reduce-scatter.13.cloned.1.call-done = bf16[272,1088]{1,0:T(8,128)(2,1)} async-done(((bf16[1088,1088]{1,0:T(8,128)(2,1)}), bf16[272,1088]{1,0:T(8,128)(2,1)}) %reduce-scatter.13.cloned.1.call-update) | async-done | bytes 591888 | tf_op jit(solution)/shard_map/reduce_scatter | solution.py:278
  1345.6 87.8 %reduce-scatter.15.cloned.1.call-done = bf16[272,4352]{1,0:T(8,128)(2,1)} async-done(((bf16[1088,4352]{1,0:T(8,128)(2,1)}), bf16[272,4352]{1,0:T(8,128)(2,1)}) %reduce-scatter.15.cloned.1.call-update) | async-done | bytes 2367504 | tf_op jit(solution)/shard_map/reduce_scatter | solution.py:290
  1433.4 91.6 %reduce-scatter.17.cloned.1.call-done = bf16[1088,1088]{1,0:T(8,128)(2,1)} async-done(((bf16[4352,1088]{1,0:T(8,128)(2,1)}), bf16[1088,1088]{1,0:T(8,128)(2,1)}) %reduce-scatter.17.cloned.1.call-update) | async-done | bytes 2367504 | tf_op jit(solution)/shard_map/reduce_scatter | solution.py:296
  1525.0 73.9 %reduce-scatter.11.cloned.1.call-done = bf16[272,3264]{1,0:T(8,128)(2,1)} async-done(((bf16[1088,3264]{1,0:T(8,128)(2,1)}), bf16[272,3264]{1,0:T(8,128)(2,1)}) %reduce-scatter.11.cloned.1.call-update) | async-done | bytes 1775632 | tf_op jit(solution)/shard_map/reduce_scatter | solution.py:269
  1607.3 18.9 all-reduce.20
  1626.9 156.3 %all-reduce.18 = (bf16[272]{0:T(512)(128)(2,1)S(1)}, bf16[272]{0:T(512)(128)(2,1)S(1)}, bf16[272]{0:T(512)(128)(2,1)S(1)}, bf16[272]{0:T(512)(128)(2,1)S(1)}, bf...) all-reduce(bf16[272]{0:T(512)(128)(2,1)S(1)} %dynamic-slice.10, ...), channel_id=1, replica_groups=mesh['ctx'=32,'fsdp'=4] {'ctx'}, use_global_device_ids=true, to_apply=%region_18.19 | all-reduce | flops 3264 | bytes 13056 | tf_op jit(solution)/shard_map/psum | solution.py:304
  1790.7 8.2 fusion.63
  1798.9 155.1 %all-reduce.24.cloned.1.call-done = (bf16[272,3264]{1,0:T(8,128)(2,1)}, bf16[272,1088]{1,0:T(8,128)(2,1)}, bf16[272,4352]{1,0:T(8,128)(2,1)}, bf16[1088,1088]{1,0:T(8,128)(2,1)}) async-done(((bf16[272,3264]{1,0:T(8,128)(2,1)}, bf16[272,1088]{1,0:T(8,128)(2,1)}, bf16[272,4352]{1,0:T(8,128)(2,1)}, bf16[1088,1088]{1,0:T(8,128)(2,1)}), (bf16[272,3264]{1,0:T(8,128)(2,1)}, bf16[272,1088]{1,0:T(8,128)(2,1)}, ...) | async-done | bytes 7102480 | tf_op jit(solution)/shard_map/psum | solution.py:306
  (413 shorter events, 287.5 us)
Async XLA Ops:
  7.2 60.3 %all-gather.7.cloned.1.call-start = ((), (), s32[]{:S(2)}) async-start(), calls=%async_computation.6 | async-start | bytes 9052160 | tf_op jit(solution)/shard_map/all_gather | solution.py:93
  7.9 315.5 %all-gather.9.cloned.1.call-start = ((), (), s32[]{:S(2)}) async-start(), calls=%async_computation.7 | async-start | bytes 9191424 | tf_op jit(solution)/shard_map/all_gather | solution.py:134
  33.9 39.9 %copy-start.30 = (f32[1088]{0:T(1024)}, f32[1088]{0:T(1024)S(1)}, u32[]{:S(2)}) copy-start(f32[1088]{0:T(1024)S(1)} %convert_element_type.204) | copy-start | bytes 13060
  33.9 39.9 %copy-start.26 = (f32[1088]{0:T(1024)}, f32[1088]{0:T(1024)S(1)}, u32[]{:S(2)}) copy-start(f32[1088]{0:T(1024)S(1)} %convert_element_type.203) | copy-start | bytes 13060
  35.1 38.8 %copy-start.32 = (f32[128]{0:T(128)}, f32[128]{0:T(128)S(1)}, u32[]{:S(2)}) copy-start(f32[128]{0:T(128)S(1)} %broadcast_multiply_fusion.1) | copy-start | bytes 1540
  35.2 38.6 %copy-start.37 = (f32[128]{0:T(128)}, f32[128]{0:T(128)S(1)}, u32[]{:S(2)}) copy-start(f32[128]{0:T(128)S(1)} %fusion.80) | copy-start | bytes 1540
  35.3 38.6 %copy-start.34 = (f32[128]{0:T(128)}, f32[128]{0:T(128)S(1)}, u32[]{:S(2)}) copy-start(f32[128]{0:T(128)S(1)} %fusion.100) | copy-start | bytes 1540
  74.6 498.4 %all-gather.11.cloned.1.call-start = ((), (), s32[]{:S(2)}) async-start(), calls=%async_computation.8 | async-start | bytes 9191424 | tf_op jit(solution)/shard_map/all_gather | solution.py:135
  75.8 611.0 %all-gather.13.cloned.1.call-start = ((), (), s32[]{:S(2)}) async-start(), calls=%async_computation.9 | async-start | bytes 3133440 | tf_op jit(solution)/shard_map/all_gather | solution.py:96
  76.3 614.4 %all-gather.15.cloned.1.call-start = ((), (), s32[]{:S(2)}) async-start(), calls=%async_computation.10 | async-start | bytes 11837440 | tf_op jit(solution)/shard_map/all_gather | solution.py:100
  76.9 666.7 %all-gather.17.cloned.1.call-start = ((), (), s32[]{:S(2)}) async-start(), calls=%async_computation.11 | async-start | bytes 12533760 | tf_op jit(solution)/shard_map/all_gather | solution.py:102
  77.5 1013.4 %reduce-scatter.21.cloned.1.call-start = ((), (), s32[]{:S(2)}) async-start(), calls=%async_computation.17 | async-start | bytes 9732096
  696.2 54.9 %copy-start.6 = (f32[128,4352]{1,0:T(8,128)}, f32[128,4352]{1,0:T(8,128)S(1)}, u32[]{:S(2)}) copy-start(f32[128,4352]{1,0:T(8,128)S(1)} %convolution_add_fusion) | copy-start | bytes 6684676
  881.8 420.2 %reduce-scatter.19.cloned.1.call-start = ((), (), s32[]{:S(2)}) async-start(), calls=%async_computation.16 | async-start | bytes 9732096
  893.8 451.8 %reduce-scatter.13.cloned.1.call-start = ((), (), s32[]{:S(2)}) async-start(), calls=%async_computation.13 | async-start | bytes 3133440 | tf_op jit(solution)/shard_map/reduce_scatter | solution.py:278
  897.1 536.3 %reduce-scatter.15.cloned.1.call-start = ((), (), s32[]{:S(2)}) async-start(), calls=%async_computation.14 | async-start | bytes 11837440 | tf_op jit(solution)/shard_map/reduce_scatter | solution.py:290
  902.7 622.2 %reduce-scatter.17.cloned.1.call-start = ((), (), s32[]{:S(2)}) async-start(), calls=%async_computation.15 | async-start | bytes 12533760 | tf_op jit(solution)/shard_map/reduce_scatter | solution.py:296
  909.8 393.3 %copy-start.27 = (f32[1088]{0:T(1024)S(1)}, f32[1088]{0:T(1024)}, u32[]{:S(2)}) copy-start(f32[1088]{0:T(1024)} %copy-done.26) | copy-start | bytes 13060
  909.8 393.3 %copy-start.31 = (f32[1088]{0:T(1024)S(1)}, f32[1088]{0:T(1024)}, u32[]{:S(2)}) copy-start(f32[1088]{0:T(1024)} %copy-done.30) | copy-start | bytes 13060
  909.8 393.3 %copy-start.33 = (f32[128]{0:T(128)S(1)}, f32[128]{0:T(128)}, u32[]{:S(2)}) copy-start(f32[128]{0:T(128)} %copy-done.32) | copy-start | bytes 1540
  909.8 393.3 %copy-start.35 = (f32[128]{0:T(128)S(1)}, f32[128]{0:T(128)}, u32[]{:S(2)}) copy-start(f32[128]{0:T(128)} %copy-done.34) | copy-start | bytes 1540
  909.8 689.1 %reduce-scatter.11.cloned.1.call-start = ((), (), s32[]{:S(2)}) async-start(), calls=%async_computation.12 | async-start | bytes 9052160 | tf_op jit(solution)/shard_map/reduce_scatter | solution.py:269
  1308.3 645.7 %all-reduce.24.cloned.1.call-start = ((), (), s32[]{:S(2)}) async-start(), calls=%async_computation.18 | async-start | bytes 14622720 | tf_op jit(solution)/shard_map/psum | solution.py:306
  1606.1 184.6 %copy-start.8 = (f32[128,4352]{1,0:T(8,128)S(1)}, f32[128,4352]{1,0:T(8,128)}, u32[]{:S(2)}) copy-start(f32[128,4352]{1,0:T(8,128)} %copy-done.6) | copy-start | bytes 6684676
  (63 other events, 205.9 us)
Sparse Core Ops, SparseCore 0:
  9.7 57.7 all-gather.6
  74.7 248.6 all-gather.8
  325.6 247.3 all-gather.10
  574.5 27.0 all-gather.12
  603.1 67.8 all-gather.14
  672.5 71.0 all-gather.16
  881.9 208.9 reduce-scatter.20
  1093.4 208.5 reduce-scatter.18
  1305.2 40.3 reduce-scatter.12
  1348.4 84.9 reduce-scatter.14
  1436.3 88.6 reduce-scatter.16
  1527.7 71.1 reduce-scatter.10
  1601.7 352.2 all-reduce.23
where the time goes:
time: 1980 us; the launch traced here: 1970 us
  waiting for transfers between devices  1390 us (70%)
  matrix products  214 us (11%)
  blocking collectives  191 us (10%)
  local copies, waits for them, and re-layouts  105 us (5%)
  other arithmetic  51.5 us (3%)
    unnamed x15, waiting for transfers between devices  392 us
    all_gather x1, waiting for transfers between devices, local(): lax.all_gather(key_rows, 'ctx', axis=0, tiled=True)  246 us
    all_gather x1, waiting for transfers between devices, local(): lax.all_gather(value_rows, 'ctx', axis=0, tiled=True)  226 us
    psum x1, blocking collectives, local(): lax.psum(shard_terms[0].astype(jnp.bfloat16), 'ctx').astype(jnp.float32)  156 us
    psum x1, waiting for transfers between devices, local(): lax.psum(shard_terms[2].astype(jnp.bfloat16), 'ctx').astype(jnp.float32)  155 us
    reduce_scatter x1, waiting for transfers between devices, local(): lax.psum_scatter(d_down.astype(jnp.bfloat16), 'fsdp', scatter_dimension=0...  91.6 us
    unnamed x104, local copies, waits for them, and re-layouts  88.1 us
    reduce_scatter x1, waiting for transfers between devices, local(): lax.psum_scatter(d_fc.astype(jnp.bfloat16), 'fsdp', scatter_dimension=0,...  87.8 us
  transfers between devices with their start and end apart: 13, of which 11 were waited for; matrix products, arithmetic and copies ran while one was open for 11% of the time, Pallas kernels for 0%

commit v1 on v0

--- a/solution.py
+++ b/solution.py
@@ -1,11 +1,395 @@
+import functools
 import math
 
 import jax
 import jax.numpy as jnp
 from jax import lax
+from jax.experimental import pallas as pl
+from jax.experimental.pallas import tpu as pltpu
 from jax.sharding import PartitionSpec as P
 
+MESH = pl.DeviceIdType.MESH
 HEAD_DIM = 64
+HEADS = 17
+BLOCK = 64
+STEP = 512
+
+
+def head_place(head, core):
+    return jnp.where(head < 16, 2 * head + core, 1 - core)
+
+
+def held_head(place, core):
+    own = lax.rem(place, 2) == core
+    head = jnp.where(own, place // 2, 16)
+    return own | (place == 1 - core), head
+
+
+def greet_ctx(me, count):
+    barrier = pltpu.get_barrier_semaphore()
+
+    def greet(step, carry):
+        pl.semaphore_signal(
+            barrier, inc=1, device_id={"ctx": lax.rem(me + step, count)}, device_id_type=MESH
+        )
+        return carry
+
+    lax.fori_loop(1, count, greet, 0)
+    pl.semaphore_wait(barrier, count - 1)
+
+
+def rows_of(place, half, count):
+    block = place if half == 0 else 2 * count - 1 - place
+    return pl.ds(pl.multiple_of(block * BLOCK, BLOCK), BLOCK)
+
+
+def spread_kernel(count, x_ref, out_ref, send_sem, recv_sem, own_sem):
+    me = lax.axis_index("ctx")
+    core = lax.rem(lax.axis_index("fsdp"), 2)
+    has, _ = held_head(me, core)
+    greet_ctx(me, count)
+
+    def remote(head, source, half):
+        return pltpu.make_async_remote_copy(
+            src_ref=x_ref.at[head, pl.ds(half * BLOCK, BLOCK)],
+            dst_ref=out_ref.at[rows_of(source, half, count)],
+            send_sem=send_sem.at[head, half],
+            recv_sem=recv_sem.at[source, half],
+            device_id={"ctx": head_place(head, core)},
+            device_id_type=MESH,
+        )
+
+    def own(head, half):
+        return pltpu.make_async_copy(
+            x_ref.at[head, pl.ds(half * BLOCK, BLOCK)],
+            out_ref.at[rows_of(me, half, count)],
+            own_sem.at[half],
+        )
+
+    def send(head, carry):
+        target = head_place(head, core)
+        for half in range(2):
+
+            @pl.when(target != me)
+            def _():
+                remote(head, me, half).start()
+
+            @pl.when(target == me)
+            def _():
+                own(head, half).start()
+
+        return carry
+
+    lax.fori_loop(0, HEADS, send, 0)
+
+    def sent(head, carry):
+        target = head_place(head, core)
+        for half in range(2):
+
+            @pl.when(target != me)
+            def _():
+                remote(head, me, half).wait_send()
+
+            @pl.when(target == me)
+            def _():
+                own(head, half).wait()
+
+        return carry
+
+    lax.fori_loop(0, HEADS, sent, 0)
+
+    @pl.when(has)
+    def _():
+        def arrived(source, carry):
+            for half in range(2):
+
+                @pl.when(source != me)
+                def _():
+                    remote(0, source, half).wait_recv()
+
+            return carry
+
+        lax.fori_loop(0, count, arrived, 0)
+
+
+def collect_kernel(count, y_ref, out_ref, send_sem, recv_sem, own_sem):
+    me = lax.axis_index("ctx")
+    core = lax.rem(lax.axis_index("fsdp"), 2)
+    has, mine = held_head(me, core)
+    greet_ctx(me, count)
+
+    def remote(head, target, half):
+        return pltpu.make_async_remote_copy(
+            src_ref=y_ref.at[rows_of(target, half, count)],
+            dst_ref=out_ref.at[head, pl.ds(half * BLOCK, BLOCK)],
+            send_sem=send_sem.at[target, half],
+            recv_sem=recv_sem.at[head, half],
+            device_id={"ctx": target},
+            device_id_type=MESH,
+        )
+
+    def own(half):
+        return pltpu.make_async_copy(
+            y_ref.at[rows_of(me, half, count)],
+            out_ref.at[mine, pl.ds(half * BLOCK, BLOCK)],
+            own_sem.at[half],
+        )
+
+    @pl.when(has)
+    def _():
+        def send(step, carry):
+            target = lax.rem(me + step, count)
+            for half in range(2):
+                remote(mine, target, half).start()
+            return carry
+
+        lax.fori_loop(1, count, send, 0)
+        for half in range(2):
+            own(half).start()
+
+        def sent(step, carry):
+            target = lax.rem(me + step, count)
+            for half in range(2):
+                remote(mine, target, half).wait_send()
+            return carry
+
+        lax.fori_loop(1, count, sent, 0)
+        for half in range(2):
+            own(half).wait()
+
+    def arrived(head, carry):
+        for half in range(2):
+
+            @pl.when(head_place(head, core) != me)
+            def _():
+                remote(head, 0, half).wait_recv()
+
+        return carry
+
+    lax.fori_loop(0, HEADS, arrived, 0)
+
+
+def spread_heads(packed, count, collective):
+    width = packed.shape[2]
+    return pl.pallas_call(
+        functools.partial(spread_kernel, count),
+        out_shape=jax.ShapeDtypeStruct((2 * BLOCK * count, width), packed.dtype),
+        in_specs=[pl.BlockSpec(memory_space=pl.ANY)],
+        out_specs=pl.BlockSpec(memory_space=pl.ANY),
+        scratch_shapes=[
+            pltpu.SemaphoreType.DMA((HEADS, 2)),
+            pltpu.SemaphoreType.DMA((count, 2)),
+            pltpu.SemaphoreType.DMA((2,)),
+        ],
+        compiler_params=pltpu.CompilerParams(collective_id=collective, has_side_effects=True),
+        cost_estimate=pl.CostEstimate(flops=0, bytes_accessed=4 << 20, transcendentals=0),
+    )(packed)
+
+
+def collect_heads(rows, count, collective):
+    width = rows.shape[1]
+    return pl.pallas_call(
+        functools.partial(collect_kernel, count),
+        out_shape=jax.ShapeDtypeStruct((HEADS, 2 * BLOCK, width), rows.dtype),
+        in_specs=[pl.BlockSpec(memory_space=pl.ANY)],
+        out_specs=pl.BlockSpec(memory_space=pl.ANY),
+        scratch_shapes=[
+            pltpu.SemaphoreType.DMA((count, 2)),
+            pltpu.SemaphoreType.DMA((HEADS, 2)),
+            pltpu.SemaphoreType.DMA((2,)),
+        ],
+        compiler_params=pltpu.CompilerParams(collective_id=collective, has_side_effects=True),
+        cost_estimate=pl.CostEstimate(flops=0, bytes_accessed=4 << 20, transcendentals=0),
+    )(rows)
+
+
+def dot_nt(left, right):
+    return lax.dot_general(
+        left, right, (((1,), (1,)), ((), ())), preferred_element_type=jnp.float32
+    )
+
+
+def dot_nn(left, right):
+    return jnp.dot(left, right, preferred_element_type=jnp.float32)
+
+
+def causal(scores):
+    keys = lax.broadcasted_iota(jnp.int32, scores.shape, 0)
+    asks = lax.broadcasted_iota(jnp.int32, scores.shape, 1)
+    return keys <= asks
+
+
+def attend_forward(x_ref, out_ref, wide_ref, lse_ref, q_ref, k_ref, vt_ref):
+    has, _ = held_head(lax.axis_index("ctx"), lax.rem(lax.axis_index("fsdp"), 2))
+    blocks = x_ref.shape[0] // STEP
+
+    @pl.when(has)
+    def _():
+        def prepare(at, carry):
+            rows = pl.ds(pl.multiple_of(at * STEP, STEP), STEP)
+            q_ref[rows, :] = x_ref[rows, 0:64] * jnp.bfloat16(0.125)
+            k_ref[rows, :] = x_ref[rows, 64:128]
+            vt_ref[:, rows] = x_ref[rows, 128:256].T[0:64, :]
+            return carry
+
+        lax.fori_loop(0, blocks, prepare, 0)
+
+        def one_block(at, carry):
+            asks = pl.ds(pl.multiple_of(at * STEP, STEP), STEP)
+            query = q_ref[asks, :]
+
+            def update(state, place, masked):
+                top, total, accum = state
+                keys = pl.ds(pl.multiple_of(place * STEP, STEP), STEP)
+                scores = dot_nt(k_ref[keys, :], query)
+                if masked:
+                    scores = jnp.where(causal(scores), scores, -1e30)
+                new_top = jnp.maximum(top, jnp.max(scores, axis=0, keepdims=True))
+                factor = jnp.exp(top - new_top)
+                weights = jnp.exp(scores - new_top)
+                total = total * factor + jnp.sum(weights, axis=0, keepdims=True)
+                accum = accum * factor + dot_nn(vt_ref[:, keys], weights.astype(jnp.bfloat16))
+                return new_top, total, accum
+
+            state = (
+                jnp.full((1, STEP), -1e30, jnp.float32),
+                jnp.zeros((1, STEP), jnp.float32),
+                jnp.zeros((64, STEP), jnp.float32),
+            )
+            state = update(state, at, True)
+            state = lax.fori_loop(0, at, lambda place, held: update(held, place, False), state)
+            top, total, accum = state
+            result = accum / total
+            wide_ref[:, asks] = result
+            lse_ref[:, asks] = top + jnp.log(total)
+            full = jnp.concatenate([result, jnp.zeros_like(result)], axis=0)
+            out_ref[asks, :] = full.T.astype(jnp.bfloat16)
+            return carry
+
+        lax.fori_loop(0, blocks, one_block, 0)
+
+
+def attend_backward(
+    x_ref, g_ref, wide_ref, lse_ref, out_ref, q_ref, k_ref, kt_ref, v_ref, go_ref, dq_ref, delta_ref
+):
+    has, _ = held_head(lax.axis_index("ctx"), lax.rem(lax.axis_index("fsdp"), 2))
+    blocks = x_ref.shape[0] // STEP
+
+    @pl.when(has)
+    def _():
+        def prepare(at, carry):
+            rows = pl.ds(pl.multiple_of(at * STEP, STEP), STEP)
+            q_ref[rows, :] = x_ref[rows, 0:64] * jnp.bfloat16(0.125)
+            k_ref[rows, :] = x_ref[rows, 64:128]
+            kt_ref[:, rows] = x_ref[rows, 0:128].T[64:128, :]
+            v_ref[rows, :] = x_ref[rows, 128:192]
+            go_ref[rows, :] = g_ref[rows, 0:64]
+            turned = g_ref[rows, :].T[0:64, :].astype(jnp.float32)
+            delta_ref[:, rows] = jnp.sum(turned * wide_ref[:, rows], axis=0, keepdims=True)
+            dq_ref[:, rows] = jnp.zeros((64, STEP), jnp.float32)
+            return carry
+
+        lax.fori_loop(0, blocks, prepare, 0)
+
+        def one_block(place, carry):
+            keys = pl.ds(pl.multiple_of(place * STEP, STEP), STEP)
+            key = k_ref[keys, :]
+            turned_key = kt_ref[:, keys]
+            value = v_ref[keys, :]
+
+            def update(state, at, masked):
+                grad_key, grad_value = state
+                asks = pl.ds(pl.multiple_of(at * STEP, STEP), STEP)
+                query = q_ref[asks, :]
+                grad = go_ref[asks, :]
+                probs = jnp.exp(dot_nt(key, query) - lse_ref[:, asks])
+                if masked:
+                    probs = jnp.where(causal(probs), probs, 0.0)
+                grad_probs = dot_nt(value, grad)
+                grad_scores = (probs * (grad_probs - delta_ref[:, asks])).astype(jnp.bfloat16)
+                grad_value = grad_value + dot_nn(probs.astype(jnp.bfloat16), grad)
+                grad_key = grad_key + dot_nn(grad_scores, query)
+                dq_ref[:, asks] += dot_nn(turned_key, grad_scores)
+                return grad_key, grad_value
+
+            state = (jnp.zeros((STEP, 64), jnp.float32), jnp.zeros((STEP, 64), jnp.float32))
+            state = update(state, place, True)
+            grad_key, grad_value = lax.fori_loop(
+                place + 1, blocks, lambda at, held: update(held, at, False), state
+            )
+            out_ref[keys, 64:128] = grad_key.astype(jnp.bfloat16)
+            out_ref[keys, 128:192] = grad_value.astype(jnp.bfloat16)
+            return carry
+
+        lax.fori_loop(0, blocks, one_block, 0)
+
+        def finish(at, carry):
+            rows = pl.ds(pl.multiple_of(at * STEP, STEP), STEP)
+            half = dq_ref[:, rows] * 0.125
+            full = jnp.concatenate([half, jnp.zeros_like(half)], axis=0).T
+            out_ref[rows, 0:64] = full[:, 0:64].astype(jnp.bfloat16)
+            return carry
+
+        lax.fori_loop(0, blocks, finish, 0)
+
+
+def run_forward(rows):
+    length = rows.shape[0]
+    return pl.pallas_call(
+        attend_forward,
+        out_shape=(
+            jax.ShapeDtypeStruct((length, 128), jnp.bfloat16),
+            jax.ShapeDtypeStruct((64, length), jnp.float32),
+            jax.ShapeDtypeStruct((1, length), jnp.float32),
+        ),
+        scratch_shapes=[
+            pltpu.VMEM((length, 64), jnp.bfloat16),
+            pltpu.VMEM((length, 64), jnp.bfloat16),
+            pltpu.VMEM((64, length), jnp.bfloat16),
+        ],
+        compiler_params=pltpu.CompilerParams(vmem_limit_bytes=40 << 20),
+        cost_estimate=pl.CostEstimate(
+            flops=2 * length * length * 64,
+            bytes_accessed=length * 512 * 2,
+            transcendentals=length * length // 2,
+        ),
+    )(rows)
+
+
+def run_backward(rows, grads, wide, lse):
+    length = rows.shape[0]
+    return pl.pallas_call(
+        attend_backward,
+        out_shape=jax.ShapeDtypeStruct((length, 256), jnp.bfloat16),
+        scratch_shapes=[
+            pltpu.VMEM((length, 64), jnp.bfloat16),
+            pltpu.VMEM((length, 64), jnp.bfloat16),
+            pltpu.VMEM((64, length), jnp.bfloat16),
+            pltpu.VMEM((length, 64), jnp.bfloat16),
+            pltpu.VMEM((length, 64), jnp.bfloat16),
+            pltpu.VMEM((64, length), jnp.float32),
+            pltpu.VMEM((1, length), jnp.float32),
+        ],
+        compiler_params=pltpu.CompilerParams(vmem_limit_bytes=40 << 20),
+        cost_estimate=pl.CostEstimate(
+            flops=5 * length * length * 64,
+            bytes_accessed=length * 512 * 3,
+            transcendentals=length * length // 2,
+        ),
+    )(rows, grads, wide, lse)
+
+
+def pack_heads(*parts):
+    rows = parts[0].shape[0]
+    turned = [part.reshape(rows, HEADS, HEAD_DIM) for part in parts]
+    if len(parts) % 2:
+        turned.append(jnp.zeros((rows, HEADS, HEAD_DIM), parts[0].dtype))
+    return jnp.transpose(jnp.concatenate(turned, axis=2), (1, 0, 2))
+
+
+def unpack_heads(packed, at):
+    part = packed[:, :, at * HEAD_DIM : (at + 1) * HEAD_DIM]
+    return jnp.transpose(part, (1, 0, 2)).reshape(part.shape[1], HEADS * HEAD_DIM)
 
 
 def norm_rows(values, gain_vec, offset):
@@ -20,44 +404,6 @@
         * values
         * (1.0 + jnp.tanh(0.7978845608028654 * (values + 0.044715 * values * values * values)))
     )
-
-
-def dealt_positions(row_count, per_device, first_device, device_count):
-    row_ids = jnp.arange(row_count, dtype=jnp.int32)
-    device = first_device + row_ids // per_device
-    within = row_ids % per_device
-    half_size = per_device // 2
-    block_id = jnp.where(within < half_size, device, 2 * device_count - 1 - device)
-    return block_id * half_size + within % half_size
-
-
-def block_scores(query_heads, key_heads, query_places, key_places, scaling):
-    scores = (
-        jnp.einsum("qhd,khd->hqk", query_heads, key_heads, preferred_element_type=jnp.float32)
-        * scaling
-    )
-    allowed = key_places[None, None, :] <= query_places[None, :, None]
-    return jnp.where(allowed, scores, -1e30)
-
-
-def score_grads(
-    query_heads,
-    grad_heads,
-    key_heads,
-    value_heads,
-    query_places,
-    key_places,
-    lse_rows,
-    delta_rows,
-    scaling,
-):
-    scores = block_scores(query_heads, key_heads, query_places, key_places, scaling)
-    probabilities = jnp.exp(scores - lse_rows[..., None])
-    grad_probs = jnp.einsum(
-        "qhd,khd->hqk", grad_heads, value_heads, preferred_element_type=jnp.float32
-    )
-    grad_scores = (probabilities * (grad_probs - delta_rows[..., None])).astype(jnp.bfloat16)
-    return (probabilities.astype(jnp.bfloat16), grad_scores)
 
 
 def local(
@@ -78,15 +424,7 @@
     bias_down,
 ):
     ctx_count = lax.axis_size("ctx")
-    my_index = lax.axis_index("ctx")
-    local_rows = tokens.shape[1]
     model_width = tokens.shape[2]
-    seq_length = local_rows * ctx_count
-    head_size = HEAD_DIM
-    head_count = model_width // head_size
-    scaling = 1.0 / math.sqrt(head_size)
-    key_block = math.gcd(512, seq_length)
-    block_count = seq_length // key_block
     gathered = (
         lax.all_gather(ln1_scale, "fsdp", axis=0, tiled=True),
         lax.all_gather(ln1_bias, "fsdp", axis=0, tiled=True),
@@ -130,43 +468,9 @@
     value_rows = (joint_rows[:, 2 * model_width :] + full_bv.astype(jnp.float32)).astype(
         jnp.bfloat16
     )
-    all_keys, all_values = (
-        lax.all_gather(key_rows, "ctx", axis=0, tiled=True),
-        lax.all_gather(value_rows, "ctx", axis=0, tiled=True),
-    )
-    query_places = dealt_positions(local_rows, local_rows, my_index, ctx_count)
-    key_places = dealt_positions(seq_length, local_rows, 0, ctx_count)
-    heads_q = queries.reshape(local_rows, head_count, head_size)
-    keys_blocks = all_keys.reshape(block_count, key_block, head_count, head_size)
-    values_blocks = all_values.reshape(block_count, key_block, head_count, head_size)
-    places_blocks = key_places.reshape(block_count, key_block)
-    key_inputs = (keys_blocks, values_blocks, places_blocks)
-
-    def forward_step(carry, entry):
-        run_max, run_sum, accum = carry
-        key_heads, value_heads, places_here = entry
-        scores = block_scores(heads_q, key_heads, query_places, places_here, scaling)
-        new_max = jnp.maximum(run_max, jnp.max(scores, axis=-1))
-        factor = jnp.exp(run_max - new_max)
-        weights = jnp.exp(scores - new_max[..., None])
-        run_sum = run_sum * factor + jnp.sum(weights, axis=-1)
-        accum = accum * jnp.transpose(factor)[:, :, None] + jnp.einsum(
-            "hqk,khd->qhd",
-            weights.astype(jnp.bfloat16),
-            value_heads,
-            preferred_element_type=jnp.float32,
-        )
-        return ((new_max, run_sum, accum), None)
-
-    start_max = jnp.full((head_count, local_rows), -1e30, jnp.float32)
-    start_sum = jnp.zeros((head_count, local_rows), jnp.float32)
-    start_accum = jnp.zeros((local_rows, head_count, head_size), jnp.float32)
-    (final_max, final_sum, final_accum), unused = lax.scan(
-        forward_step, (start_max, start_sum, start_accum), key_inputs
-    )
-    lse_rows = final_max + jnp.log(final_sum)
-    out_heads = final_accum / jnp.transpose(final_sum)[:, :, None]
-    attended = out_heads.reshape(local_rows, model_width).astype(jnp.bfloat16)
+    head_rows = spread_heads(pack_heads(queries, key_rows, value_rows), ctx_count, 1)
+    out_rows, wide_out, lse_rows = run_forward(head_rows)
+    attended = unpack_heads(collect_heads(out_rows, ctx_count, 2), 0)
     branch = jnp.dot(attended, full_out, preferred_element_type=jnp.float32) + full_bout.astype(
         jnp.float32
     )
@@ -201,57 +505,12 @@
     grad_attended = jnp.einsum(
         "te,de->td", grad_branch, full_out, preferred_element_type=jnp.float32
     ).astype(jnp.bfloat16)
-    grad_heads = grad_attended.reshape(local_rows, head_count, head_size)
-    row_delta = jnp.einsum("qhd,qhd->hq", grad_heads.astype(jnp.float32), out_heads)
-    start_query = jnp.zeros((local_rows, head_count, head_size), jnp.float32)
-
-    def main_step(accum, entry):
-        key_heads, value_heads, places_here = entry
-        low_probs, grad_scores = score_grads(
-            heads_q,
-            grad_heads,
-            key_heads,
-            value_heads,
-            query_places,
-            places_here,
-            lse_rows,
-            row_delta,
-            scaling,
-        )
-        accum = (
-            accum
-            + jnp.einsum("hqk,khd->qhd", grad_scores, key_heads, preferred_element_type=jnp.float32)
-            * scaling
-        )
-        grad_keys = (
-            jnp.einsum("hqk,qhd->khd", grad_scores, heads_q, preferred_element_type=jnp.float32)
-            * scaling
-        )
-        grad_values = jnp.einsum(
-            "hqk,qhd->khd", low_probs, grad_heads, preferred_element_type=jnp.float32
-        )
-        return (
-            accum,
-            (
-                grad_keys.reshape(key_block, model_width),
-                grad_values.reshape(key_block, model_width),
-            ),
-        )
-
-    grad_query_heads, (key_terms, value_terms) = lax.scan(main_step, start_query, key_inputs)
-    key_terms = key_terms.reshape(seq_length, model_width)
-    value_terms = value_terms.reshape(seq_length, model_width)
-    own_keys, own_values = (
-        lax.psum_scatter(
-            key_terms.astype(jnp.bfloat16), "ctx", scatter_dimension=0, tiled=True
-        ).astype(jnp.float32),
-        lax.psum_scatter(
-            value_terms.astype(jnp.bfloat16), "ctx", scatter_dimension=0, tiled=True
-        ).astype(jnp.float32),
-    )
-    grad_q16 = grad_query_heads.reshape(local_rows, model_width).astype(jnp.bfloat16)
-    grad_k16 = own_keys.astype(jnp.bfloat16)
-    grad_v16 = own_values.astype(jnp.bfloat16)
+    grad_rows = spread_heads(pack_heads(grad_attended, jnp.zeros_like(grad_attended)), ctx_count, 3)
+    joint_rows_grad = run_backward(head_rows, grad_rows, wide_out, lse_rows)
+    packed_grads = collect_heads(joint_rows_grad, ctx_count, 4)
+    grad_q16 = unpack_heads(packed_grads, 0)
+    grad_k16 = unpack_heads(packed_grads, 1)
+    grad_v16 = unpack_heads(packed_grads, 2)
     grad_joint = jnp.concatenate([grad_q16, grad_k16, grad_v16], axis=1)
     d_qkv = jnp.einsum("td,te->de", normed, grad_joint, preferred_element_type=jnp.float32)
     d_bq = jnp.sum(grad_q16.astype(jnp.float32), axis=0)

time: 1980 us -> 1010 us (0.51)
  waiting for transfers between devices: 1390 us -> 529 us
  Pallas kernels: 0 us -> 156 us
  matrix products: 214 us -> 63.2 us
  local copies, waits for them, and re-layouts: 105 us -> 22.9 us
  other arithmetic: 51.5 us -> 21.4 us
    all_gather x2 -> x0, waiting for transfers between devices: 472 us -> none  [the longest x1 246 us: local(): lax.all_gather(key_rows, 'ctx', axis=0, tiled=True)]
    unnamed x15 -> x9, waiting for transfers between devices: 392 us -> 2.66 us
    pallas_call x0 -> x6, Pallas kernels: none -> 156 us  [the longest x2 53.3 us: spread_heads(): pl.pallas_call(functools.partial(spread_kernel, count), out_shape=jax.Sha...]
    dot_general x56 -> x0, matrix products: 155 us -> none  [the longest x16 52.2 us: block_scores(): jnp.einsum('qhd,khd->hqk', query_heads, key_heads, preferred_element_type...]
    unnamed x104 -> x102, local copies, waits for them, and re-layouts: 88.1 us -> 13.6 us
    reduce_scatter x1, waiting for transfers between devices: 37.3 us -> 0.02 us  [local(): lax.psum_scatter(d_out.astype(jnp.bfloat16), 'fsdp', scatter_dimension=0,...]
    all_gather x1, waiting for transfers between devices: 0.02 us -> 32 us  [local(): lax.all_gather(w_fc, 'fsdp', axis=0, tiled=True)]
    reduce_sum x9 -> x0, other arithmetic: 27.6 us -> none  [the longest x8 27.4 us: forward_step(): run_sum = run_sum * factor + jnp.sum(weights, axis=-1)]
  transfers between devices with their start and end apart: 13 -> 9, of which waited for: 11 -> 7; matrix products, arithmetic and copies ran while one was open for 11% -> 7% of each run, Pallas kernels for 0% -> 16%
where the time goes in v1:
time: 1010 us; the launch traced here: 1000 us
  waiting for transfers between devices  529 us (52%)
  blocking collectives  191 us (19%)
  Pallas kernels  156 us (15%)
  matrix products  63.2 us (6%)
  local copies, waits for them, and re-layouts  22.9 us (2%)
  other arithmetic  21.4 us (2%)
  between operations  17.6 us (2%)
    psum x1, blocking collectives, local(): lax.psum(shard_terms[0].astype(jnp.bfloat16), 'ctx').astype(jnp.float32)  156 us
    psum x1, waiting for transfers between devices, local(): lax.psum(shard_terms[2].astype(jnp.bfloat16), 'ctx').astype(jnp.float32)  156 us
    reduce_scatter x1, waiting for transfers between devices, local(): lax.psum_scatter(d_down.astype(jnp.bfloat16), 'fsdp', scatter_dimension=0...  91.4 us
    reduce_scatter x1, waiting for transfers between devices, local(): lax.psum_scatter(d_fc.astype(jnp.bfloat16), 'fsdp', scatter_dimension=0,...  87.7 us
    all_gather x1, waiting for transfers between devices, local(): lax.all_gather(w_down, 'fsdp', axis=0, tiled=True)  65 us
    reduce_scatter x1, waiting for transfers between devices, local(): lax.psum_scatter(d_qkv.astype(jnp.bfloat16), 'fsdp', scatter_dimension=0,...  57.7 us
    pallas_call x2, Pallas kernels, spread_heads(): pl.pallas_call(functools.partial(spread_kernel, count), out_shape=jax.Sha...  53.3 us
    pallas_call x2, Pallas kernels, collect_heads(): pl.pallas_call(functools.partial(collect_kernel, count), out_shape=jax.Sh...  43.5 us
  transfers between devices with their start and end apart: 9, of which 7 were waited for; matrix products, arithmetic and copies ran while one was open for 7% of the time, Pallas kernels for 16%

profile of v1, /device:TPU:8, one launch (start us, length us, event | category | flops | bytes accessed | tf_op | source)
XLA Modules:
  0.0 1001.5 jit_solution(7219400053756964108)
XLA Ops:
  14.1 16.1 %all-reduce.22 = (bf16[1088]{0:T(1024)(128)(2,1)S(1)}, bf16[1088]{0:T(1024)(128)(2,1)S(1)}, bf16[1088]{0:T(1024)(128)(2,1)S(1)}, bf16[1088]{0:T(1024)(128)(2,1)S...) all-reduce(bf16[1088]{0:T(1024)(128)(2,1)S(1)} %dynamic-update-slic, ...), channel_id=1, replica_groups=mesh['ctx'=32,'fsdp'=4] {'fsdp'}, use_global_device_ids=true, to_apply=%add.2 | all-reduce | flops 11968 | bytes 47872
  30.7 36.5 %all-gather.5.cloned.1.call-done = bf16[1088,3264]{1,0:T(8,128)(2,1)} async-done(((bf16[272,3264]{1,0:T(8,128)(2,1)}), bf16[1088,3264]{1,0:T(8,128)(2,1)}) %all-gather.5.cloned.1.call-update) | async-done | bytes 7102480 | tf_op jit(solution)/shard_map/all_gather | solution.py:431
  67.2 6.4 fusion.39
  76.6 32.4 %shard_map.262.x_ref = bf16[4096,256]{1,0:T(8,128)(2,1)} custom-call(bf16[17,128,256]{2,1,0:T(8,128)(2,1)} %maximum_bitcast_fusion.x_ref), custom_call_target="tpu_custom_call" | custom-call | bytes 4194304 | tf_op jit(solution)/shard_map/pallas_call | solution.py:174
  110.6 25.4 %shard_map.263 = (bf16[4096,128]{1,0:T(8,128)(2,1)S(1)}, f32[64,4096]{1,0:T(8,128)S(1)}, f32[1,4096]{1,0:T(1,128)S(1)}) custom-call(bf16[4096,256]{1,0:T(8,128)(2,1)S(1)} %copy-done), custom_call_target="tpu_custom_call" | custom-call | flops 2147483648 | bytes 4194304 | tf_op jit(solution)/shard_map/pallas_call | solution.py:338
  137.0 18.7 %shard_map.264 = bf16[17,128,128]{2,1,0:T(8,128)(2,1)} custom-call(bf16[4096,128]{1,0:T(8,128)(2,1)} %copy-done.4), custom_call_target="tpu_custom_call" | custom-call | bytes 4194304 | tf_op jit(solution)/shard_map/pallas_call | solution.py:191
  160.1 32.0 %all-gather.9.cloned.1.call-done = bf16[1088,4352]{1,0:T(8,128)(2,1)} async-done(((bf16[272,4352]{1,0:T(8,128)(2,1)}), bf16[1088,4352]{1,0:T(8,128)(2,1)}) %all-gather.9.cloned.1.call-update) | async-done | bytes 9469968 | tf_op jit(solution)/shard_map/all_gather | solution.py:438
  192.2 6.8 convolution_add_fusion
  199.0 65.0 %all-gather.11.cloned.1.call-done = bf16[4352,1088]{1,0:T(8,128)(2,1)} async-done(((bf16[1088,1088]{1,0:T(8,128)(2,1)}), bf16[4352,1088]{1,0:T(8,128)(2,1)}) %all-gather.11.cloned.1.call-update) | async-done | bytes 9469968 | tf_op jit(solution)/shard_map/all_gather | solution.py:440
  264.0 8.1 fusion.47
  286.0 21.0 %shard_map.265.g_ref = bf16[4096,128]{1,0:T(8,128)(2,1)} custom-call(bf16[17,128,128]{2,1,0:T(8,128)(2,1)} %pad_bitcast_fusion.x_ref), custom_call_target="tpu_custom_call" | custom-call | bytes 4194304 | tf_op jit(solution)/shard_map/pallas_call | solution.py:174
  308.2 34.2 %shard_map.266.y_ref = bf16[4096,256]{1,0:T(8,128)(2,1)S(1)} custom-call(bf16[4096,256]{1,0:T(8,128)(2,1)S(1)} %copy-done.1, bf16[4096,128]{1,0:T(8,128)(2,1)S(1)} %copy-done.3, f32[64,4096]{1,0:T(8,128)S(1)} %get-tuple-element.19.wide_ref, f32[1,4096]{1,0:T(1,128)S(1)} %get-tuple-element.20.lse_ref), custom_call_target="tpu_custom_call" | custom-call | flops 5368709120 | bytes 6291456 | tf_op jit(solution)/shard_map/pallas_call | solution.py:361
  343.7 24.8 %shard_map.267 = bf16[17,128,256]{2,1,0:T(8,128)(2,1)} custom-call(bf16[4096,256]{1,0:T(8,128)(2,1)} %copy-done.2), custom_call_target="tpu_custom_call" | custom-call | bytes 4194304 | tf_op jit(solution)/shard_map/pallas_call | solution.py:191
  371.0 5.2 convolution_convert_fusion.2
  377.6 5.5 convolution_convert_fusion.1
  384.7 6.7 convolution_convert_fusion
  391.6 57.7 %reduce-scatter.5.cloned.1.call-done = bf16[272,3264]{1,0:T(8,128)(2,1)} async-done(((bf16[1088,3264]{1,0:T(8,128)(2,1)}), bf16[272,3264]{1,0:T(8,128)(2,1)}) %reduce-scatter.5.cloned.1.call-update) | async-done | bytes 1775632 | tf_op jit(solution)/shard_map/reduce_scatter | solution.py:528
  449.3 87.7 %reduce-scatter.9.cloned.1.call-done = bf16[272,4352]{1,0:T(8,128)(2,1)} async-done(((bf16[1088,4352]{1,0:T(8,128)(2,1)}), bf16[272,4352]{1,0:T(8,128)(2,1)}) %reduce-scatter.9.cloned.1.call-update) | async-done | bytes 2367504 | tf_op jit(solution)/shard_map/reduce_scatter | solution.py:549
  537.0 91.4 %reduce-scatter.11.cloned.1.call-done = bf16[1088,1088]{1,0:T(8,128)(2,1)} async-done(((bf16[4352,1088]{1,0:T(8,128)(2,1)}), bf16[1088,1088]{1,0:T(8,128)(2,1)}) %reduce-scatter.11.cloned.1.call-update) | async-done | bytes 2367504 | tf_op jit(solution)/shard_map/reduce_scatter | solution.py:555
  630.7 5.2 fusion.41
  637.1 18.9 %all-reduce.21 = (bf16[1088]{0:T(1024)(128)(2,1)S(1)}, bf16[1088]{0:T(1024)(128)(2,1)S(1)}, bf16[1088]{0:T(1024)(128)(2,1)S(1)}, bf16[1088]{0:T(1024)(128)(2,1)S...) all-reduce(bf16[1088]{0:T(1024)(128)(2,1)S(1)} %dynamic-update-slic, ...), channel_id=1, replica_groups=mesh['ctx'=32,'fsdp'=4] {'fsdp'}, use_global_device_ids=true, to_apply=%add.9 | all-reduce | flops 14144 | bytes 56576
  656.8 156.3 %all-reduce.19 = (bf16[272]{0:T(512)(128)(2,1)S(1)}, bf16[272]{0:T(512)(128)(2,1)S(1)}, bf16[272]{0:T(512)(128)(2,1)S(1)}, bf16[272]{0:T(512)(128)(2,1)S(1)}, bf...) all-reduce(bf16[272]{0:T(512)(128)(2,1)S(1)} %dynamic-slice.10, ...), channel_id=1, replica_groups=mesh['ctx'=32,'fsdp'=4] {'ctx'}, use_global_device_ids=true, to_apply=%region_10.0 | all-reduce | flops 3264 | bytes 13056 | tf_op jit(solution)/shard_map/psum | solution.py:563
  820.6 8.2 fusion.3
  828.8 155.6 %all-reduce.25.cloned.1.call-done = (bf16[272,3264]{1,0:T(8,128)(2,1)}, bf16[272,1088]{1,0:T(8,128)(2,1)}, bf16[272,4352]{1,0:T(8,128)(2,1)}, bf16[1088,1088]{1,0:T(8,128)(2,1)}) async-done(((bf16[272,3264]{1,0:T(8,128)(2,1)}, bf16[272,1088]{1,0:T(8,128)(2,1)}, bf16[272,4352]{1,0:T(8,128)(2,1)}, bf16[1088,1088]{1,0:T(8,128)(2,1)}), (bf16[272,3264]{1,0:T(8,128)(2,1)}, bf16[272,1088]{1,0:T(8,128)(2,1)}, ...) | async-done | bytes 7102480 | tf_op jit(solution)/shard_map/psum | solution.py:565
  (183 shorter events, 58.4 us)
Async XLA Ops:
  7.2 60.0 %all-gather.5.cloned.1.call-start = ((), (), s32[]{:S(2)}) async-start(), calls=%async_computation.4 | async-start | bytes 9052160 | tf_op jit(solution)/shard_map/all_gather | solution.py:431
  7.9 149.1 %all-gather.7.cloned.1.call-start = ((), (), s32[]{:S(2)}) async-start(), calls=%async_computation.5 | async-start | bytes 3133440 | tf_op jit(solution)/shard_map/all_gather | solution.py:434
  8.7 4.1 copy-start.32
  8.7 4.4 copy-start.33
  8.7 4.6 copy-start.34
  8.7 4.8 copy-start.35
  8.7 5.1 copy-start.27
  8.8 21.6 %copy-start.8 = (bf16[1,128,1088]{1,2,0:T(8,128)(2,1)S(1)}, bf16[1,128,1088]{1,2,0:T(8,128)(2,1)}, u32[]{:S(2)}) copy-start(bf16[1,128,1088]{1,2,0:T(8,128)(2,1)} %param.15) | copy-start | bytes 835588
  8.8 183.4 %all-gather.9.cloned.1.call-start = ((), (), s32[]{:S(2)}) async-start(), calls=%async_computation.6 | async-start | bytes 11837440 | tf_op jit(solution)/shard_map/all_gather | solution.py:438
  9.5 254.5 %all-gather.11.cloned.1.call-start = ((), (), s32[]{:S(2)}) async-start(), calls=%async_computation.7 | async-start | bytes 12533760 | tf_op jit(solution)/shard_map/all_gather | solution.py:440
  10.1 381.5 %reduce-scatter.7.cloned.1.call-start = ((), (), s32[]{:S(2)}) async-start(), calls=%async_computation.9 | async-start | bytes 3133440 | tf_op jit(solution)/shard_map/reduce_scatter | solution.py:537
  159.9 115.0 %copy-start.6 = (f32[128,1088]{0,1:T(8,128)}, f32[128,1088]{0,1:T(8,128)S(1)}, u32[]{:S(2)}) copy-start(f32[128,1088]{0,1:T(8,128)S(1)} %get-tuple-element.73) | copy-start | bytes 1671172
  160.1 103.8 %copy-start.15 = (bf16[1,128,1088]{1,2,0:T(8,128)(2,1)S(1)}, bf16[1,128,1088]{1,2,0:T(8,128)(2,1)}, u32[]{:S(2)}) copy-start(bf16[1,128,1088]{1,2,0:T(8,128)(2,1)} %param.16) | copy-start | bytes 835588
  264.0 8.1 copy-start.5
  278.5 170.8 %reduce-scatter.5.cloned.1.call-start = ((), (), s32[]{:S(2)}) async-start(), calls=%async_computation.8 | async-start | bytes 9052160 | tf_op jit(solution)/shard_map/reduce_scatter | solution.py:528
  281.8 25.2 %copy-start.1 = (bf16[4096,256]{1,0:T(8,128)(2,1)S(1)}, bf16[4096,256]{1,0:T(8,128)(2,1)}, u32[]{:S(2)}) copy-start(bf16[4096,256]{1,0:T(8,128)(2,1)} %shard_map.262.x_ref) | copy-start | bytes 6291460
  370.5 5.7 copy-start.20
  370.7 5.5 copy-start.22
  371.0 5.2 copy-start.24
  376.3 160.7 %reduce-scatter.9.cloned.1.call-start = ((), (), s32[]{:S(2)}) async-start(), calls=%async_computation.10 | async-start | bytes 11837440 | tf_op jit(solution)/shard_map/reduce_scatter | solution.py:549
  383.1 245.2 %reduce-scatter.11.cloned.1.call-start = ((), (), s32[]{:S(2)}) async-start(), calls=%async_computation.11 | async-start | bytes 12533760 | tf_op jit(solution)/shard_map/reduce_scatter | solution.py:555
  391.5 592.8 %all-reduce.25.cloned.1.call-start = ((), (), s32[]{:S(2)}) async-start(), calls=%async_computation.12 | async-start | bytes 14622720 | tf_op jit(solution)/shard_map/psum | solution.py:565
  635.9 184.7 %copy-start.11 = (f32[128,4352]{1,0:T(8,128)S(1)}, f32[128,4352]{1,0:T(8,128)}, u32[]{:S(2)}) copy-start(f32[128,4352]{1,0:T(8,128)} %convolution_add_fusion) | copy-start | bytes 6684676
  984.3 4.8 copy-start.18
  (22 other events, 44.8 us)
Sparse Core Ops, SparseCore 0:
  9.7 57.4 all-gather.4
  68.9 44.7 all-gather.6
  115.4 76.7 all-gather.8
  193.7 70.2 all-gather.10
  278.6 40.2 reduce-scatter.6
  376.4 72.8 reduce-scatter.4
  452.0 84.9 reduce-scatter.8
  539.7 88.6 reduce-scatter.10
  631.1 353.1 all-reduce.24

commit v2 on v1

--- a/solution.py
+++ b/solution.py
@@ -392,6 +392,394 @@
     return jnp.transpose(part, (1, 0, 2)).reshape(part.shape[1], HEADS * HEAD_DIM)
 
 
+UNITS = 17
+PIECE = 6528
+TAIL = 896
+
+
+def places():
+    ctx = lax.axis_index("ctx")
+    fsdp = lax.axis_index("fsdp")
+    return ctx // 8, lax.rem(ctx // 2, 4), lax.rem(ctx, 2), fsdp // 2, lax.rem(fsdp, 2)
+
+
+def device_at(z, x, y_low, y_high, core):
+    return (z * 8 + x * 2 + y_low, y_high * 2 + core)
+
+
+def z_peer(step):
+    z, x, y_low, y_high, core = places()
+    return device_at(lax.rem(z + step, 4), x, y_low, y_high, core)
+
+
+def x_peer(step):
+    z, x, y_low, y_high, core = places()
+    return device_at(z, lax.rem(x + step, 4), y_low, y_high, core)
+
+
+def near_peer():
+    z, x, y_low, y_high, core = places()
+    return device_at(z, x, 1 - y_low, y_high, core)
+
+
+def cross_peer():
+    z, x, y_low, y_high, core = places()
+    return device_at(z, x, 1 - y_low, 1 - y_high, core)
+
+
+def far_peer():
+    z, x, y_low, y_high, core = places()
+    return device_at(z, x, y_low, 1 - y_high, core)
+
+
+def twin_peer():
+    z, x, y_low, y_high, core = places()
+    return device_at(z, x, y_low, y_high, 1 - core)
+
+
+def ring_peers():
+    return [z_peer(step) for step in (1, 2, 3)] + [x_peer(step) for step in (1, 2, 3)]
+
+
+def greet(peers):
+    barrier = pltpu.get_barrier_semaphore()
+    for peer in peers:
+        pl.semaphore_signal(barrier, inc=1, device_id=peer, device_id_type=MESH)
+    pl.semaphore_wait(barrier, len(peers))
+
+
+class Sender:
+    def __init__(self, send_sem, recv_sem):
+        self.send_sem = send_sem
+        self.recv_sem = recv_sem
+        self.used = 0
+        self.started = []
+
+    def push(self, source, target, peer):
+        copy = pltpu.make_async_remote_copy(
+            src_ref=source,
+            dst_ref=target,
+            send_sem=self.send_sem.at[self.used],
+            recv_sem=self.recv_sem.at[self.used],
+            device_id=peer,
+            device_id_type=MESH,
+        )
+        self.used += 1
+        copy.start()
+        self.started.append(copy)
+        return copy
+
+    def finish(self):
+        for copy in self.started:
+            copy.wait_send()
+
+
+GATHER_COPIES = 4 * 19 + 3
+
+
+def gather_kernel(*refs):
+    sources, small = refs[0:4], refs[4]
+    targets, small_out = refs[5:9], refs[9]
+    own_sem, send_sem, recv_sem = refs[10:13]
+    z, x, y_low, y_high, core = places()
+    mine = y_high * 2 + core
+    cross = (1 - y_high) * 2 + core
+    other = y_high * 2 + 1 - core
+    other_cross = (1 - y_high) * 2 + 1 - core
+    greet(ring_peers() + [cross_peer(), far_peer(), twin_peer()] + [far_twin()])
+    sender = Sender(send_sem, recv_sem)
+    starts = ((2 * z, 2), (8 + 2 * x, 2), (16, 1))
+    owns = []
+    for at in range(4):
+        owns.append(pltpu.make_async_copy(sources[at], targets[at].at[mine], own_sem.at[at]))
+    owns.append(pltpu.make_async_copy(small, small_out.at[mine], own_sem.at[4]))
+    small_in = [
+        sender.push(small, small_out.at[mine], twin_peer()),
+        sender.push(small, small_out.at[mine], far_peer()),
+        sender.push(small, small_out.at[mine], far_twin()),
+    ]
+    crossed = []
+    for at in range(4):
+        crossed.append(
+            [
+                sender.push(
+                    sources[at].at[pl.ds(start, size)],
+                    targets[at].at[mine, pl.ds(start, size)],
+                    cross_peer(),
+                )
+                for start, size in starts
+            ]
+        )
+    for own in owns:
+        own.start()
+    twin_in = []
+    for at in range(4):
+        twin_in.append(sender.push(sources[at], targets[at].at[mine], twin_peer()))
+    ringed = []
+    for at in range(4):
+        here = []
+        for part, (start, size) in enumerate(starts):
+            crossed[at][part].wait_recv()
+            piece = targets[at].at[cross, pl.ds(start, size)]
+            for step in (1, 3, 2):
+                if part < 2:
+                    peer = z_peer(step) if part == 0 else x_peer(step)
+                    here.append((part, step, sender.push(piece, piece, peer)))
+            twin_in.append(sender.push(piece, piece, twin_peer()))
+        ringed.append(here)
+    for at in range(4):
+        for part, step, copy in ringed[at]:
+            copy.wait_recv()
+            if part == 0:
+                start = 2 * lax.rem(z - step + 4, 4)
+            else:
+                start = 8 + 2 * lax.rem(x - step + 4, 4)
+            piece = targets[at].at[cross, pl.ds(start, 2)]
+            twin_in.append(sender.push(piece, piece, twin_peer()))
+    for copy in small_in:
+        copy.wait_recv()
+    for copy in twin_in:
+        copy.wait_recv()
+    for own in owns:
+        own.wait()
+    sender.finish()
+
+
+def far_twin():
+    z, x, y_low, y_high, core = places()
+    return device_at(z, x, y_low, 1 - y_high, 1 - core)
+
+
+def gather_weights(parts, small, collective):
+    shapes = [jax.ShapeDtypeStruct((4,) + part.shape, part.dtype) for part in parts + [small]]
+    return pl.pallas_call(
+        gather_kernel,
+        out_shape=shapes,
+        in_specs=[pl.BlockSpec(memory_space=pl.ANY)] * 5,
+        out_specs=[pl.BlockSpec(memory_space=pl.ANY)] * 5,
+        scratch_shapes=[
+            pltpu.SemaphoreType.DMA((5,)),
+            pltpu.SemaphoreType.DMA((GATHER_COPIES,)),
+            pltpu.SemaphoreType.DMA((GATHER_COPIES,)),
+        ],
+        compiler_params=pltpu.CompilerParams(collective_id=collective, has_side_effects=True),
+        cost_estimate=pl.CostEstimate(flops=0, bytes_accessed=60 << 20, transcendentals=0),
+    )(*parts, small)
+
+
+def first_kernel(*refs):
+    parts, tail = refs[0:4], refs[4]
+    by_z, by_x, tail_out = refs[5:9], refs[9:13], refs[13]
+    send_sem, recv_sem = refs[14:16]
+    z, x, y_low, y_high, core = places()
+    greet(ring_peers())
+    sender = Sender(send_sem, recv_sem)
+    for step in (2, 1, 3):
+        to_z, to_x = lax.rem(z + step, 4), lax.rem(x + step, 4)
+        for at in range(4):
+            sender.push(
+                parts[at].at[:, pl.ds(2 * to_z, 2)], by_z[at].at[step - 1], z_peer(step)
+            )
+            sender.push(
+                parts[at].at[:, pl.ds(8 + 2 * to_x, 2)], by_x[at].at[step - 1], x_peer(step)
+            )
+        sender.push(tail.at[:, to_z], tail_out.at[step - 1], z_peer(step))
+    for copy in sender.started:
+        copy.wait_recv()
+    sender.finish()
+
+
+def first_exchange(parts, tail, collective):
+    shapes = [
+        jax.ShapeDtypeStruct((3, 2, 2) + part.shape[2:], part.dtype) for part in parts + parts
+    ]
+    shapes.append(jax.ShapeDtypeStruct((3, 2, 4, 16, TAIL), tail.dtype))
+    results = pl.pallas_call(
+        first_kernel,
+        out_shape=shapes,
+        in_specs=[pl.BlockSpec(memory_space=pl.ANY)] * 5,
+        out_specs=[pl.BlockSpec(memory_space=pl.ANY)] * 9,
+        scratch_shapes=[pltpu.SemaphoreType.DMA((27,)), pltpu.SemaphoreType.DMA((27,))],
+        compiler_params=pltpu.CompilerParams(collective_id=collective, has_side_effects=True),
+        cost_estimate=pl.CostEstimate(flops=0, bytes_accessed=40 << 20, transcendentals=0),
+    )(*parts, tail)
+    return results[0:4], results[4:8], results[8]
+
+
+LAST_COPIES = 9 + 3 + 9 + 36
+
+
+def last_kernel(
+    tz_ref,
+    tx_ref,
+    td_ref,
+    gz_ref,
+    gx_ref,
+    gd_ref,
+    rz_ref,
+    rx_ref,
+    rd_ref,
+    sum_ref,
+    in_ref,
+    total_ref,
+    own_sem,
+    send_sem,
+    recv_sem,
+):
+    z, x, y_low, y_high, core = places()
+    greet(ring_peers() + [near_peer(), cross_peer(), far_peer()])
+    sender = Sender(send_sem, recv_sem)
+    spans = ((0, PIECE), (PIECE, PIECE), (2 * PIECE, TAIL))
+    chunk = 1088
+    for step in (2, 1, 3):
+        to_z, to_x = lax.rem(z + step, 4), lax.rem(x + step, 4)
+        sender.push(tz_ref.at[to_x], rz_ref.at[step - 1], x_peer(step))
+        sender.push(tx_ref.at[to_z], rx_ref.at[step - 1], z_peer(step))
+        sender.push(td_ref.at[to_x], rd_ref.at[step - 1], x_peer(step))
+    for copy in sender.started:
+        copy.wait_recv()
+
+    groups = ((tz_ref, x, rz_ref), (tx_ref, z, rx_ref), (td_ref, x, rd_ref))
+    for (terms, mine, others), (start, size) in zip(groups, spans):
+        for low in range(0, size, PIECE // 3):
+            high = min(low + PIECE // 3, size)
+            total = terms[mine, :, :, low:high].astype(jnp.float32)
+            for step in range(3):
+                total = total + others[step, :, :, low:high].astype(jnp.float32)
+            sum_ref[:, :, start + low : start + high] = total.astype(jnp.bfloat16)
+
+    met = [
+        sender.push(sum_ref.at[0], in_ref.at[0], near_peer()),
+        sender.push(sum_ref.at[1], in_ref.at[1], cross_peer()),
+        sender.push(sum_ref.at[1], in_ref.at[2], far_peer()),
+    ]
+    for copy in met:
+        copy.wait_recv()
+    for start, size in spans:
+        for low in range(start, start + size, PIECE // 3):
+            high = min(low + PIECE // 3, start + size)
+            near = sum_ref[0, :, low:high].astype(jnp.float32) + in_ref[0, :, low:high].astype(
+                jnp.float32
+            )
+            away = in_ref[1, :, low:high].astype(jnp.float32) + in_ref[2, :, low:high].astype(
+                jnp.float32
+            )
+            total_ref[:, low:high] = (near + away).astype(jnp.bfloat16)
+
+    pieces = [total_ref.at[:, pl.ds(start, size)] for start, size in spans]
+    firsts = (gz_ref.at[z, x], gx_ref.at[x, z], gd_ref.at[z, x])
+    owns = [
+        pltpu.make_async_copy(pieces[at], firsts[at], own_sem.at[at]) for at in range(3)
+    ]
+    for own in owns:
+        own.start()
+    passed = []
+    for step in (1, 3, 2):
+        for at in range(3):
+            peer = z_peer(step) if at == 1 else x_peer(step)
+            passed.append((at, step, sender.push(pieces[at], firsts[at], peer)))
+    ends = []
+    for step in (1, 3, 2):
+        for at in range(3):
+            peer = x_peer(step) if at == 1 else z_peer(step)
+            ends.append(sender.push(pieces[at], firsts[at], peer))
+    for at, step, copy in passed:
+        copy.wait_recv()
+        from_x, from_z = lax.rem(x - step + 4, 4), lax.rem(z - step + 4, 4)
+        place = (gz_ref.at[z, from_x], gx_ref.at[x, from_z], gd_ref.at[z, from_x])[at]
+        for other in (1, 3, 2):
+            peer = x_peer(other) if at == 1 else z_peer(other)
+            ends.append(sender.push(place, place, peer))
+    for copy in ends:
+        copy.wait_recv()
+    for own in owns:
+        own.wait()
+    sender.finish()
+
+
+def last_exchange(tz, tx, td, collective):
+    return pl.pallas_call(
+        last_kernel,
+        out_shape=(
+            jax.ShapeDtypeStruct((4, 4, 16, PIECE), jnp.bfloat16),
+            jax.ShapeDtypeStruct((4, 4, 16, PIECE), jnp.bfloat16),
+            jax.ShapeDtypeStruct((4, 4, 16, TAIL), jnp.bfloat16),
+        ),
+        in_specs=[pl.BlockSpec(memory_space=pltpu.VMEM)] * 3,
+        out_specs=[pl.BlockSpec(memory_space=pl.ANY)] * 3,
+        scratch_shapes=[
+            pltpu.VMEM((3, 2, 16, PIECE), jnp.bfloat16),
+            pltpu.VMEM((3, 2, 16, PIECE), jnp.bfloat16),
+            pltpu.VMEM((3, 2, 16, TAIL), jnp.bfloat16),
+            pltpu.VMEM((2, 16, 2 * PIECE + TAIL), jnp.bfloat16),
+            pltpu.VMEM((3, 16, 2 * PIECE + TAIL), jnp.bfloat16),
+            pltpu.VMEM((16, 2 * PIECE + TAIL), jnp.bfloat16),
+            pltpu.SemaphoreType.DMA((3,)),
+            pltpu.SemaphoreType.DMA((LAST_COPIES,)),
+            pltpu.SemaphoreType.DMA((LAST_COPIES,)),
+        ],
+        compiler_params=pltpu.CompilerParams(
+            collective_id=collective, has_side_effects=True, vmem_limit_bytes=40 << 20
+        ),
+        cost_estimate=pl.CostEstimate(flops=0, bytes_accessed=16 << 20, transcendentals=0),
+    )(tz, tx, td)
+
+
+def flat_units(parts):
+    lead = parts[0].shape[:-2]
+    down = parts[3].reshape(lead + (4, 16, 1088))
+    down = jnp.moveaxis(down, -3, -2).reshape(lead + (16, 4352))
+    return jnp.concatenate([parts[0], parts[1], parts[2], down], axis=-1)
+
+
+def wide_units(flat):
+    lead = flat.shape[:-2]
+    down = flat[..., 8704:].reshape(lead + (16, 4, 1088))
+    down = jnp.moveaxis(down, -2, -3).reshape(lead + (64, 1088))
+    return flat[..., :3264], flat[..., 3264:4352], flat[..., 4352:8704], down
+
+
+def reduce_grads(parts, small, collective):
+    z, x, y_low, y_high, core = places()
+    parts = [part.reshape(2, UNITS, part.shape[1] // UNITS, part.shape[2]) for part in parts]
+    last = flat_units([part[:, 16] for part in parts])
+    extra = jnp.pad(small, ((0, 0), (0, 16 * 1280 - small.shape[1]))).reshape(2, 16, 1280)
+    tail = jnp.concatenate([last, extra.astype(jnp.bfloat16)], axis=-1)
+    tail = jnp.transpose(tail.reshape(2, 16, 4, 4, TAIL), (0, 2, 3, 1, 4))
+    by_z, by_x, by_tail = first_exchange(parts, tail, collective)
+
+    def added(own, others):
+        total = own.astype(jnp.float32)
+        for step in range(3):
+            total = total + others[step].astype(jnp.float32)
+        return total.astype(jnp.bfloat16)
+
+    def first_sum(start, others):
+        sums = []
+        for part, other in zip(parts, others):
+            size = (2, 2) + part.shape[2:]
+            sums.append(added(lax.dynamic_slice(part, (0, start, 0, 0), size), other))
+        flat = flat_units(sums).reshape(2, 2, 16, 2, PIECE)
+        return jnp.transpose(flat, (1, 3, 0, 2, 4)).reshape(4, 2, 16, PIECE)
+
+    tz = first_sum(2 * z, by_z)
+    tx = first_sum(8 + 2 * x, by_x)
+    td = added(lax.dynamic_index_in_dim(tail, z, 1, keepdims=False), by_tail)
+    gz, gx, gd = last_exchange(tz, tx, jnp.transpose(td, (1, 0, 2, 3)), collective + 1)
+
+    def units(whole):
+        turned = jnp.transpose(whole.reshape(8, 2, 16, PIECE), (0, 2, 1, 3))
+        return turned.reshape(8, 16, 2 * PIECE)
+
+    tail_all = jnp.transpose(gd, (2, 0, 1, 3)).reshape(1, 16, 16 * TAIL)
+    flat = jnp.concatenate([units(gz), units(gx), tail_all[:, :, : 2 * PIECE]], axis=0)
+    outs = wide_units(flat)
+    widths = [(272, 3264), (272, 1088), (272, 4352), (1088, 1088)]
+    outs = [out.reshape(shape).astype(jnp.float32) for out, shape in zip(outs, widths)]
+    extras = tail_all[0, :, 2 * PIECE :].reshape(-1)[:3264].astype(jnp.float32)
+    return outs, extras
+
+
 def norm_rows(values, gain_vec, offset):
     centre = values - jnp.mean(values, axis=-1, keepdims=True)
     spread = jnp.mean(centre * centre, axis=-1, keepdims=True)
@@ -425,36 +813,62 @@
 ):
     ctx_count = lax.axis_size("ctx")
     model_width = tokens.shape[2]
-    gathered = (
-        lax.all_gather(ln1_scale, "fsdp", axis=0, tiled=True),
-        lax.all_gather(ln1_bias, "fsdp", axis=0, tiled=True),
-        lax.all_gather(w_qkv, "fsdp", axis=0, tiled=True),
-        lax.all_gather(bias_q, "fsdp", axis=0, tiled=True),
-        lax.all_gather(bias_v, "fsdp", axis=0, tiled=True),
-        lax.all_gather(w_out, "fsdp", axis=0, tiled=True),
-        lax.all_gather(bias_out, "fsdp", axis=0, tiled=True),
-        lax.all_gather(ln2_scale, "fsdp", axis=0, tiled=True),
-        lax.all_gather(ln2_bias, "fsdp", axis=0, tiled=True),
-        lax.all_gather(w_fc, "fsdp", axis=0, tiled=True),
-        lax.all_gather(bias_fc, "fsdp", axis=0, tiled=True),
-        lax.all_gather(w_down, "fsdp", axis=0, tiled=True),
-        lax.all_gather(bias_down, "fsdp", axis=0, tiled=True),
+    vectors = (
+        ln1_scale,
+        ln1_bias,
+        bias_q,
+        bias_v,
+        bias_out,
+        ln2_scale,
+        ln2_bias,
+        bias_down,
+        bias_fc,
     )
-    (
-        g_scale1,
-        g_shift1,
-        full_qkv,
-        full_bq,
-        full_bv,
-        full_out,
-        full_bout,
-        g_scale2,
-        g_shift2,
-        full_fc,
-        full_bfc,
-        full_down,
-        full_bdown,
-    ) = gathered
+    small = jnp.pad(jnp.concatenate(vectors), (0, 4096 - 3264)).reshape(16, 256)
+    own_parts = [
+        part.reshape(UNITS, part.shape[0] // UNITS, part.shape[1])
+        for part in (w_qkv, w_out, w_fc, w_down)
+    ]
+    full_qkv, full_out, full_fc, full_down, full_small = gather_weights(own_parts, small, 5)
+    full_qkv = full_qkv.reshape(1088, 3264)
+    full_out = full_out.reshape(1088, 1088)
+    full_fc = full_fc.reshape(1088, 4352)
+    full_down = full_down.reshape(4352, 1088)
+    full_small = full_small.reshape(4, 4096)
+    (g_scale1, g_shift1, full_bq, full_bv, full_bout, g_scale2, g_shift2, full_bdown) = [
+        full_small[:, at * 272 : (at + 1) * 272].reshape(1088) for at in range(8)
+    ]
+    full_bfc = full_small[:, 2176:3264].reshape(4352)
+    z, x, y_low, y_high, core = places()
+
+    def swap(values):
+        return lax.ppermute(values, "fsdp", [(0, 1), (1, 0), (2, 3), (3, 2)])
+
+    def split(values):
+        quarters = values.reshape(values.shape[0], 2, 2, -1)
+        first, second = quarters[:, :, 0], quarters[:, :, 1]
+        keep = jnp.where(core == 0, first, second)
+        give = jnp.where(core == 0, second, first)
+        keep = jnp.where(y_high == 0, keep, keep[:, ::-1])
+        give = jnp.where(y_high == 0, give, give[:, ::-1])
+        return keep.reshape(values.shape[0], -1), give.reshape(values.shape[0], -1)
+
+    def left_rows(values):
+        keep, give = split(values)
+        return jnp.concatenate([keep, swap(give)], axis=0)
+
+    def right_rows(values):
+        return jnp.concatenate([values, swap(values)], axis=0)
+
+    def weight_terms(left, right):
+        terms = lax.dot_general(
+            left_rows(left),
+            right_rows(right),
+            (((0,), (0,)), ((), ())),
+            preferred_element_type=jnp.float32,
+        ).astype(jnp.bfloat16)
+        return terms.reshape(2, terms.shape[0] // 2, terms.shape[1])
+
     scale_one = g_scale1.astype(jnp.float32)
     shift_one = g_shift1.astype(jnp.float32)
     scale_two = g_scale2.astype(jnp.float32)
@@ -488,19 +902,19 @@
     result = (middle + out_branch).astype(jnp.bfloat16)
     upstream = cotangent[0].astype(jnp.float32)
     grad_branch2 = cotangent[0]
-    d_down = jnp.einsum("tf,td->fd", active, grad_branch2, preferred_element_type=jnp.float32)
+    d_down = weight_terms(active, grad_branch2)
     d_bdown = jnp.sum(upstream, axis=0)
     grad_active = jnp.einsum(
         "td,fd->tf", grad_branch2, full_down, preferred_element_type=jnp.float32
     )
     grad_hidden = gelu_pull(grad_active)[0].astype(jnp.bfloat16)
-    d_fc = jnp.einsum("td,tf->df", normed2, grad_hidden, preferred_element_type=jnp.float32)
+    d_fc = weight_terms(normed2, grad_hidden)
     d_bfc = jnp.sum(grad_hidden.astype(jnp.float32), axis=0)
     grad_normed2 = jnp.einsum("tf,df->td", grad_hidden, full_fc, preferred_element_type=jnp.float32)
     grad_mid_part, d_scale2, d_shift2 = norm_two_pull(grad_normed2)
     grad_middle = upstream + grad_mid_part
     grad_branch = grad_middle.astype(jnp.bfloat16)
-    d_out = jnp.einsum("td,te->de", attended, grad_branch, preferred_element_type=jnp.float32)
+    d_out = weight_terms(attended, grad_branch)
     d_bout = jnp.sum(grad_branch.astype(jnp.float32), axis=0)
     grad_attended = jnp.einsum(
         "te,de->td", grad_branch, full_out, preferred_element_type=jnp.float32
@@ -512,69 +926,38 @@
     grad_k16 = unpack_heads(packed_grads, 1)
     grad_v16 = unpack_heads(packed_grads, 2)
     grad_joint = jnp.concatenate([grad_q16, grad_k16, grad_v16], axis=1)
-    d_qkv = jnp.einsum("td,te->de", normed, grad_joint, preferred_element_type=jnp.float32)
+    d_qkv = weight_terms(normed, grad_joint)
     d_bq = jnp.sum(grad_q16.astype(jnp.float32), axis=0)
     d_bv = jnp.sum(grad_v16.astype(jnp.float32), axis=0)
     grad_normed = jnp.einsum("te,de->td", grad_joint, full_qkv, preferred_element_type=jnp.float32)
     grad_in_part, d_scale1, d_shift1 = norm_one_pull(grad_normed)
     grad_inputs = grad_middle + grad_in_part
-    shard_terms = (
-        lax.psum_scatter(
-            d_scale1.astype(jnp.bfloat16), "fsdp", scatter_dimension=0, tiled=True
-        ).astype(jnp.float32),
-        lax.psum_scatter(
-            d_shift1.astype(jnp.bfloat16), "fsdp", scatter_dimension=0, tiled=True
-        ).astype(jnp.float32),
-        lax.psum_scatter(
-            d_qkv.astype(jnp.bfloat16), "fsdp", scatter_dimension=0, tiled=True
-        ).astype(jnp.float32),
-        lax.psum_scatter(d_bq.astype(jnp.bfloat16), "fsdp", scatter_dimension=0, tiled=True).astype(
-            jnp.float32
-        ),
-        lax.psum_scatter(d_bv.astype(jnp.bfloat16), "fsdp", scatter_dimension=0, tiled=True).astype(
-            jnp.float32
-        ),
-        lax.psum_scatter(
-            d_out.astype(jnp.bfloat16), "fsdp", scatter_dimension=0, tiled=True
-        ).astype(jnp.float32),
-        lax.psum_scatter(
-            d_bout.astype(jnp.bfloat16), "fsdp", scatter_dimension=0, tiled=True
-        ).astype(jnp.float32),
-        lax.psum_scatter(
-            d_scale2.astype(jnp.bfloat16), "fsdp", scatter_dimension=0, tiled=True
-        ).astype(jnp.float32),
-        lax.psum_scatter(
-            d_shift2.astype(jnp.bfloat16), "fsdp", scatter_dimension=0, tiled=True
-        ).astype(jnp.float32),
-        lax.psum_scatter(d_fc.astype(jnp.bfloat16), "fsdp", scatter_dimension=0, tiled=True).astype(
-            jnp.float32
-        ),
-        lax.psum_scatter(
-            d_bfc.astype(jnp.bfloat16), "fsdp", scatter_dimension=0, tiled=True
-        ).astype(jnp.float32),
-        lax.psum_scatter(
-            d_down.astype(jnp.bfloat16), "fsdp", scatter_dimension=0, tiled=True
-        ).astype(jnp.float32),
-        lax.psum_scatter(
-            d_bdown.astype(jnp.bfloat16), "fsdp", scatter_dimension=0, tiled=True
-        ).astype(jnp.float32),
+    narrow = (d_scale1, d_shift1, d_bq, d_bv, d_bout, d_scale2, d_shift2, d_bdown, d_bfc)
+    sums = jnp.concatenate([vector.reshape(4, -1) for vector in narrow], axis=1)
+    keep, give = split(sums.reshape(1, -1))
+    sums = (keep + swap(give)).reshape(2, 3264)
+    (t_qkv, t_out, t_fc, t_down), extras = reduce_grads((d_qkv, d_out, d_fc, d_down), sums, 6)
+    (t_scale1, t_shift1, t_bq, t_bv, t_bout, t_scale2, t_shift2, t_bdown) = [
+        extras[at * 272 : (at + 1) * 272] for at in range(8)
+    ]
+    t_bfc = extras[2176:]
+    return (
+        result[None],
+        grad_inputs[None],
+        t_scale1,
+        t_shift1,
+        t_qkv,
+        t_bq,
+        t_bv,
+        t_out,
+        t_bout,
+        t_scale2,
+        t_shift2,
+        t_fc,
+        t_bfc,
+        t_down,
+        t_bdown,
     )
-    totals = (
-        lax.psum(shard_terms[0].astype(jnp.bfloat16), "ctx").astype(jnp.float32),
-        lax.psum(shard_terms[1].astype(jnp.bfloat16), "ctx").astype(jnp.float32),
-        lax.psum(shard_terms[2].astype(jnp.bfloat16), "ctx").astype(jnp.float32),
-        lax.psum(shard_terms[3].astype(jnp.bfloat16), "ctx").astype(jnp.float32),
-        lax.psum(shard_terms[4].astype(jnp.bfloat16), "ctx").astype(jnp.float32),
-        lax.psum(shard_terms[5].astype(jnp.bfloat16), "ctx").astype(jnp.float32),
-        lax.psum(shard_terms[6].astype(jnp.bfloat16), "ctx").astype(jnp.float32),
-        lax.psum(shard_terms[7].astype(jnp.bfloat16), "ctx").astype(jnp.float32),
-        lax.psum(shard_terms[8].astype(jnp.bfloat16), "ctx").astype(jnp.float32),
-        lax.psum(shard_terms[9].astype(jnp.bfloat16), "ctx").astype(jnp.float32),
-        lax.psum(shard_terms[10].astype(jnp.bfloat16), "ctx").astype(jnp.float32),
-        lax.psum(shard_terms[11].astype(jnp.bfloat16), "ctx").astype(jnp.float32),
-        lax.psum(shard_terms[12].astype(jnp.bfloat16), "ctx").astype(jnp.float32),
-    )
-    return (result[None], grad_inputs[None]) + tuple(totals)
 
 
 def solution(mesh):

time: 1010 us -> 779 us (0.77)
  waiting for transfers between devices: 529 us -> 0.09 us
  Pallas kernels: 156 us -> 569 us
  blocking collectives: 191 us -> 0 us
  local copies, waits for them, and re-layouts: 22.9 us -> 101 us
  other arithmetic: 21.4 us -> 37.2 us
  between operations: 17.6 us -> 1.97 us
    pallas_call x0 -> x3, Pallas kernels: none -> 417 us  [the longest x1 228 us: gather_weights(): pl.pallas_call(gather_kernel, out_shape=shapes, in_specs=[pl.BlockSpec(me...]
    reduce_scatter x4 -> x0, waiting for transfers between devices: 237 us -> none  [the longest x1 91.4 us: local(): lax.psum_scatter(d_down.astype(jnp.bfloat16), 'fsdp', scatter_dimension=0...]
    psum x1 -> x0, blocking collectives: 156 us -> none  [local(): lax.psum(shard_terms[0].astype(jnp.bfloat16), 'ctx').astype(jnp.float32)]
    psum x1 -> x0, waiting for transfers between devices: 156 us -> none  [local(): lax.psum(shard_terms[2].astype(jnp.bfloat16), 'ctx').astype(jnp.float32)]
    all_gather x4 -> x0, waiting for transfers between devices: 134 us -> none  [the longest x1 65 us: local(): lax.all_gather(w_down, 'fsdp', axis=0, tiled=True)]
    reshape x0 -> x18, local copies, waits for them, and re-layouts: none -> 35.9 us  [the longest x2 16.4 us: units(): return turned.reshape(8, 16, 2 * PIECE)]
    unnamed x2 -> x0, blocking collectives: 34.9 us -> none
    convert_element_type x0 -> x17, local copies, waits for them, and re-layouts: none -> 22.5 us  [the longest x2 12.1 us: reduce_grads(): out.reshape(shape).astype(jnp.float32)]
  transfers between devices with their start and end apart: 9 -> 9, of which waited for: 7 -> 1; matrix products, arithmetic and copies ran while one was open for 7% -> 7% of each run, Pallas kernels for 16% -> 11%
where the time goes in v2:
time: 779 us; the launch traced here: 769 us
  Pallas kernels  569 us (73%)
  local copies, waits for them, and re-layouts  101 us (13%)
  matrix products  56.7 us (7%)
  other arithmetic  37.2 us (5%)
    pallas_call x1, Pallas kernels, gather_weights(): pl.pallas_call(gather_kernel, out_shape=shapes, in_specs=[pl.BlockSpec(me...  228 us
    pallas_call x1, Pallas kernels, last_exchange(): pl.pallas_call(last_kernel, out_shape=(jax.ShapeDtypeStruct((4, 4, 16, PI...  99.9 us
    pallas_call x1, Pallas kernels, first_exchange(): pl.pallas_call(first_kernel, out_shape=shapes, in_specs=[pl.BlockSpec(mem...  89 us
    pallas_call x2, Pallas kernels, spread_heads(): pl.pallas_call(functools.partial(spread_kernel, count), out_shape=jax.Sha...  52.3 us
    pallas_call x2, Pallas kernels, collect_heads(): pl.pallas_call(functools.partial(collect_kernel, count), out_shape=jax.Sh...  40.2 us
    pallas_call x1, Pallas kernels, run_backward(): pl.pallas_call(attend_backward, out_shape=jax.ShapeDtypeStruct((length, 2...  34 us
    pallas_call x1, Pallas kernels, run_forward(): pl.pallas_call(attend_forward, out_shape=(jax.ShapeDtypeStruct((length, 1...  25.4 us
    reshape x2, local copies, waits for them, and re-layouts, units(): return turned.reshape(8, 16, 2 * PIECE)  16.4 us
  transfers between devices with their start and end apart: 9, of which 1 were waited for; matrix products, arithmetic and copies ran while one was open for 7% of the time, Pallas kernels for 11%

profile of v2, /device:TPU:8, one launch (start us, length us, event | category | flops | bytes accessed | tf_op | source)
XLA Modules:
  0.0 768.8 jit_solution(12226031561496145833)
XLA Ops:
  0.6 6.3 concatenate.70
  7.6 228.5 %shard_map.262 = (bf16[4,17,16,3264]{3,2,1,0:T(8,128)(2,1)}, bf16[4,17,16,1088]{3,2,1,0:T(8,128)(2,1)}, bf16[4,17,16,4352]{3,2,1,0:T(8,128)(2,1)}, bf16[4,17,64,1088]{3,2,1,0:T(8,128)(2,1)}, bf16[4,16,256]{2,1,0:T(8,128)(2,1)}) custom-call(bf16[17,16,3264]{2,1,0:T(8,128)(2,1)} %bitcast.345, bf16[17,16,1088]{2,1,0:T(8,128)(2,1)} %bitcast.359, ...), custom_call_target="tpu_custom_call" | custom-call | bytes 62914560 | tf_op jit(solution)/shard_map/pallas_call | solution.py:555
  237.7 6.4 fusion.46
  247.2 31.7 %shard_map.263.x_ref = bf16[4096,256]{1,0:T(8,128)(2,1)} custom-call(bf16[17,128,256]{2,1,0:T(8,128)(2,1)} %maximum_bitcast_fusion.x_ref), custom_call_target="tpu_custom_call" | custom-call | bytes 4194304 | tf_op jit(solution)/shard_map/pallas_call | solution.py:174
  280.5 25.4 %shard_map.264 = (bf16[4096,128]{1,0:T(8,128)(2,1)S(1)}, f32[64,4096]{1,0:T(8,128)S(1)}, f32[1,4096]{1,0:T(1,128)S(1)}) custom-call(bf16[4096,256]{1,0:T(8,128)(2,1)S(1)} %copy-done.3), custom_call_target="tpu_custom_call" | custom-call | flops 2147483648 | bytes 4194304 | tf_op jit(solution)/shard_map/pallas_call | solution.py:338
  306.9 13.8 %shard_map.265 = bf16[17,128,128]{2,1,0:T(8,128)(2,1)} custom-call(bf16[4096,128]{1,0:T(8,128)(2,1)} %copy-done.7), custom_call_target="tpu_custom_call" | custom-call | bytes 4194304 | tf_op jit(solution)/shard_map/pallas_call | solution.py:191
  325.8 7.1 multiply_convert_fusion
  332.8 10.1 %convert_reduce_fusion = (f32[4352]{0:T(1024)S(1)}, bf16[128,4352]{1,0:T(8,128)(2,1)}) fusion(f32[128,4352]{1,0:T(8,128)S(1)} %get-tuple-element.109, bf16[4352,1088]{1,0:T(8,128)(2,1)} %bitcast.319, bf16[1,128,1088]{1,2,0:T(8,128)(2,1)S(1)} %copy-done.27), kind=kOutput, calls=%fused_computation.31 | convolution fusion | flops 1226632960 | bytes 13108224 | tf_op jit(solution)/shard_map/td,fd->tf/dot_general | solution.py:907
  343.0 4.0 multiply_reduce_fusion
  355.6 20.6 %shard_map.266.g_ref = bf16[4096,128]{1,0:T(8,128)(2,1)} custom-call(bf16[17,128,128]{2,1,0:T(8,128)(2,1)} %pad_bitcast_fusion.x_ref), custom_call_target="tpu_custom_call" | custom-call | bytes 4194304 | tf_op jit(solution)/shard_map/pallas_call | solution.py:174
  377.5 34.0 %shard_map.267.y_ref = bf16[4096,256]{1,0:T(8,128)(2,1)S(1)} custom-call(bf16[4096,256]{1,0:T(8,128)(2,1)S(1)} %copy-done.4, bf16[4096,128]{1,0:T(8,128)(2,1)S(1)} %copy-done.6, f32[64,4096]{1,0:T(8,128)S(1)} %get-tuple-element.41.wide_ref, f32[1,4096]{1,0:T(1,128)S(1)} %get-tuple-element.42.lse_ref), custom_call_target="tpu_custom_call" | custom-call | flops 5368709120 | bytes 6291456 | tf_op jit(solution)/shard_map/pallas_call | solution.py:361
  412.8 26.4 %shard_map.268 = bf16[17,128,256]{2,1,0:T(8,128)(2,1)} custom-call(bf16[4096,256]{1,0:T(8,128)(2,1)} %copy-done.5), custom_call_target="tpu_custom_call" | custom-call | bytes 4194304 | tf_op jit(solution)/shard_map/pallas_call | solution.py:191
  444.0 5.2 fusion.77
  453.2 7.6 fusion.3
  472.5 8.3 %copy.106 = bf16[2176,1088]{1,0:T(8,128)(2,1)} copy(bf16[2176,1088]{0,1:T(8,128)(2,1)} %convolution_convert_fusion) | data formatting | bytes 9469952 | tf_op jit(solution)/shard_map/convert_element_type | solution.py:869
  494.0 89.0 %shard_map.269 = (bf16[3,2,2,16,3264]{4,3,2,1,0:T(8,128)(2,1)}, bf16[3,2,2,16,1088]{4,3,2,1,0:T(8,128)(2,1)}, bf16[3,2,2,16,4352]{4,3,2,1,0:T(8,128)(2,1)}, bf16...) custom-call(bf16[2,17,16,3264]{3,2,1,0:T(8,128)(2,1)} %bitcast.324, ...), custom_call_target="tpu_custom_call" | custom-call | bytes 41943040 | tf_op jit(solution)/shard_map/pallas_call | solution.py:597
  607.0 99.9 %shard_map.270 = (bf16[4,4,16,6528]{3,2,1,0:T(8,128)(2,1)S(1)}, bf16[4,4,16,6528]{3,2,1,0:T(8,128)(2,1)S(1)}, bf16[4,4,16,896]{3,2,1,0:T(8,128)(2,1)S(1)}) custom-call(bf16[4,2,16,6528]{3,2,1,0:T(8,128)(2,1)S(1)} %bitcast.300, bf16[4,2,16,6528]{3,2,1,0:T(8,128)(2,1)S(1)} %bitcast.301, bf16[4,2,16,896]{3,2,1,0:T(8,128)(2,1)S(1)} %fusion.61.td_ref), custom_call_target="tpu_custom_call" | custom-call | bytes 16777216 | tf_op jit(solution)/shard_map/pallas_call | solution.py:701
  711.8 6.2 copy.148
  718.1 8.2 %reshape.571 = bf16[8,16,13056]{2,1,0:T(8,128)(2,1)} reshape(bf16[8,16,2,6528]{3,2,1,0:T(2,128)(2,1)} %bitcast.317) | data formatting | bytes 6684672 | tf_op jit(solution)/shard_map/reshape | solution.py:772
  726.3 4.3 copy.149
  730.6 8.2 %reshape.569 = bf16[8,16,13056]{2,1,0:T(8,128)(2,1)} reshape(bf16[8,16,2,6528]{3,2,1,0:T(2,128)(2,1)} %bitcast.318) | data formatting | bytes 6684672 | tf_op jit(solution)/shard_map/reshape | solution.py:772
  738.8 3.8 pad_maximum_fusion
  756.5 6.9 reshape.616
  763.4 5.1 copy.124
  (265 shorter events, 99.7 us)
Async XLA Ops:
  7.6 229.6 %copy-start.14 = (bf16[1,128,1088]{1,2,0:T(8,128)(2,1)S(1)}, bf16[1,128,1088]{1,2,0:T(8,128)(2,1)}, u32[]{:S(2)}) copy-start(bf16[1,128,1088]{1,2,0:T(8,128)(2,1)} %param.15) | copy-start | bytes 835588
  237.3 212.2 %copy-start.47 = (f32[128]{0:T(128)}, f32[128]{0:T(128)S(1)}, u32[]{:S(2)}) copy-start(f32[128]{0:T(128)S(1)} %broadcast_multiply_fusion.1) | copy-start | bytes 1540
  237.5 212.0 %copy-start.49 = (f32[128]{0:T(128)}, f32[128]{0:T(128)S(1)}, u32[]{:S(2)}) copy-start(f32[128]{0:T(128)S(1)} %fusion.69) | copy-start | bytes 1540
  325.2 21.9 %copy-start.11 = (f32[128,1088]{0,1:T(8,128)}, f32[128,1088]{0,1:T(8,128)S(1)}, u32[]{:S(2)}) copy-start(f32[128,1088]{0,1:T(8,128)S(1)} %get-tuple-element.107) | copy-start | bytes 1671172
  325.8 17.2 %slice-start = ((s8[9469952]{0:T(1024)(128)(4,1)}), s8[4194304]{0:T(1024)(128)(4,1)S(1)}, s32[]{:S(2)}) async-start(s8[9469952]{0:T(1024)(128)(4,1)} %bitcast.306), calls=%async_computation | async-start | bytes 8388608
  332.8 10.1 %slice-start.1 = ((s8[9469952]{0:T(1024)(128)(4,1)}), s8[4194304]{0:T(1024)(128)(4,1)S(1)}, s32[]{:S(2)}) async-start(s8[9469952]{0:T(1024)(128)(4,1)} %bitcast.306), calls=%async_computation.1 | async-start | bytes 8388608
  332.8 10.1 %slice-start.2 = ((s8[9469952]{0:T(1024)(128)(4,1)}), s8[1081344]{0:T(1024)(128)(4,1)S(1)}, s32[]{:S(2)}) async-start(s8[9469952]{0:T(1024)(128)(4,1)} %bitcast.306), calls=%async_computation.2 | async-start | bytes 2162688
  342.9 141.8 %collective-permute-start.5 = (bf16[128,4352]{1,0:T(8,128)(2,1)}, bf16[128,4352]{1,0:T(8,128)(2,1)}, u32[]{:S(2)}, u32[]{:S(2)}) collective-permute-start(bf16[128,4352]{1,0:T(8,128)(2,1)} %get-tuple-element.113), channel_id=1, source_target_pairs={{0,1},{1,0},{2,3},{3,2},{4,5},{5,4},{6,7},{7,6},{8,9},{9,8},{10,11... | collective-permute-start | bytes 3342344 | tf_op jit(solution)/shard_map/ppermute | solution.py:845
  348.1 118.2 %collective-permute-start.3 = (bf16[128,1088]{0,1:T(8,128)(2,1)}, bf16[128,1088]{0,1:T(8,128)(2,1)}, u32[]{:S(2)}, u32[]{:S(2)}) collective-permute-start(bf16[128,1088]{0,1:T(8,128)(2,1)} %get-tuple-element.65), channel_id=1, source_target_pairs={{0,1},{1,0},{2,3},{3,2},{4,5},{5,4},{6,7},{7,6},{8,9},{9,8},{10,11... | collective-permute-start | bytes 835592 | tf_op jit(solution)/shard_map/ppermute | solution.py:845
  351.5 24.7 %copy-start.4 = (bf16[4096,256]{1,0:T(8,128)(2,1)S(1)}, bf16[4096,256]{1,0:T(8,128)(2,1)}, u32[]{:S(2)}) copy-start(bf16[4096,256]{1,0:T(8,128)(2,1)} %shard_map.263.x_ref) | copy-start | bytes 6291460
  442.8 39.5 %collective-permute-start.1 = (bf16[128,3264]{0,1:T(8,128)(2,1)}, bf16[128,3264]{0,1:T(8,128)(2,1)}, u32[]{:S(2)}, u32[]{:S(2)}) collective-permute-start(bf16[128,3264]{0,1:T(8,128)(2,1)} %pad_maximum_fusion.1), channel_id=1, source_target_pairs={{0,1},{1,0},{2,3},{3,2},{4,5},{5,4},{6,7},{7,6},{8,9},{9,8},{10,11... | collective-permute-start | bytes 2506760 | tf_op jit(solution)/shard_map/ppermute | solution.py:845
  443.5 22.6 %collective-permute-start.2 = (bf16[128,544]{0,1:T(8,128)(2,1)}, bf16[128,544]{0,1:T(8,128)(2,1)}, u32[]{:S(2)}, u32[]{:S(2)}) collective-permute-start(bf16[128,544]{0,1:T(8,128)(2,1)} %bitcast.41), channel_id=1, source_target_pairs={{0,1},{1,0},{2,3},{3,2},{4,5},{5,4},{6,7},{7,6},{8,9},{9,8},{10,11... | collective-permute-start | bytes 417800 | tf_op jit(solution)/shard_map/ppermute | solution.py:845
  451.4 13.9 %collective-permute-start.8 = (f32[1,6528]{1,0:T(1,128)S(1)}, f32[1,6528]{1,0:T(1,128)S(1)}, u32[]{:S(2)}, u32[]{:S(2)}) collective-permute-start(f32[1,6528]{1,0:T(1,128)S(1)} %reshape.556), channel_id=1, source_target_pairs={{0,1},{1,0},{2,3},{3,2},{4,5},{5,4},{6,7},{7,6},{8,9},{9,8},{10,11... | collective-permute-start | bytes 78344 | tf_op jit(solution)/shard_map/ppermute | solution.py:845
  453.2 7.7 %copy-start.32 = (f32[128,1088]{0,1:T(8,128)S(1)}, f32[128,1088]{0,1:T(8,128)}, u32[]{:S(2)}) copy-start(f32[128,1088]{0,1:T(8,128)} %copy-done.31) | copy-start | bytes 1671172
  465.3 16.9 %collective-permute-start = (bf16[128,544]{0,1:T(8,128)(2,1)}, bf16[128,544]{0,1:T(8,128)(2,1)}, u32[]{:S(2)}, u32[]{:S(2)}) collective-permute-start(bf16[128,544]{0,1:T(8,128)(2,1)} %bitcast.32), channel_id=1, source_target_pairs={{0,1},{1,0},{2,3},{3,2},{4,5},{5,4},{6,7},{7,6},{8,9},{9,8},{10,11... | collective-permute-start | bytes 417800 | tf_op jit(solution)/shard_map/ppermute | solution.py:845
  466.1 2.7 collective-permute-start.6
  466.3 2.2 collective-permute-start.7
  468.5 16.2 %collective-permute-start.4 = (bf16[128,544]{0,1:T(8,128)(2,1)S(1)}, bf16[128,544]{0,1:T(8,128)(2,1)}, u32[]{:S(2)}, u32[]{:S(2)}) collective-permute-start(bf16[128,544]{0,1:T(8,128)(2,1)S(1)} %bitcast.366), channel_id=1, source_target_pairs={{0,1},{1,0},{2,3},{3,2},{4,5},{5,4},{6,7},{7,6},{8,9},{9,8},{10,11... | collective-permute-start | bytes 417800 | tf_op jit(solution)/shard_map/ppermute | solution.py:845
  472.5 9.7 %copy-start.39 = (bf16[128,17,64]{0,2,1:T(8,128)(2,1)S(1)}, bf16[128,17,64]{0,2,1:T(8,128)(2,1)}, u32[]{:S(2)}) copy-start(bf16[128,17,64]{0,2,1:T(8,128)(2,1)} %copy-done.38) | copy-start | bytes 835588
  472.5 9.7 %copy-start.41 = (bf16[128,17,64]{0,2,1:T(8,128)(2,1)S(1)}, bf16[128,17,64]{0,2,1:T(8,128)(2,1)}, u32[]{:S(2)}) copy-start(bf16[128,17,64]{0,2,1:T(8,128)(2,1)} %copy-done.40) | copy-start | bytes 835588
  472.5 9.7 %copy-start.43 = (bf16[128,17,64]{0,2,1:T(8,128)(2,1)S(1)}, bf16[128,17,64]{0,2,1:T(8,128)(2,1)}, u32[]{:S(2)}) copy-start(bf16[128,17,64]{0,2,1:T(8,128)(2,1)} %copy-done.42) | copy-start | bytes 835588
  492.8 90.2 %copy-start.19 = (bf16[2,16,4,4,896]{4,3,2,1,0:T(4,128)(2,1)}, bf16[2,16,4,4,896]{4,3,2,1,0:T(4,128)(2,1)S(1)}, u32[]{:S(2)}) copy-start(bf16[2,16,4,4,896]{4,3,2,1,0:T(4,128)(2,1)S(1)} %reshape.558) | copy-start | bytes 2752516
  718.1 8.2 %copy-start.1 = (bf16[4,4,16,6528]{3,2,1,0:T(8,128)(2,1)S(1)}, bf16[4,4,16,6528]{3,2,1,0:T(8,128)(2,1)}, u32[]{:S(2)}) copy-start(bf16[4,4,16,6528]{3,2,1,0:T(8,128)(2,1)} %copy-done) | copy-start | bytes 10027012
  730.6 8.2 %copy-start.9 = (bf16[8,16,13056]{2,1,0:T(8,128)(2,1)S(1)}, bf16[8,16,13056]{2,1,0:T(8,128)(2,1)}, u32[]{:S(2)}) copy-start(bf16[8,16,13056]{2,1,0:T(8,128)(2,1)} %reshape.571) | copy-start | bytes 10027012
  (43 other events, 160.4 us)

commit v3 on v2

--- a/solution.py
+++ b/solution.py
@@ -270,10 +270,33 @@
 
 
 def attend_backward(
-    x_ref, g_ref, wide_ref, lse_ref, out_ref, q_ref, k_ref, kt_ref, v_ref, go_ref, dq_ref, delta_ref
+    x_ref,
+    g_ref,
+    wide_ref,
+    lse_ref,
+    fc_ref,
+    down_ref,
+    out_ref,
+    fc_z_ref,
+    down_z_ref,
+    fc_x_ref,
+    down_x_ref,
+    q_ref,
+    k_ref,
+    kt_ref,
+    v_ref,
+    go_ref,
+    dq_ref,
+    delta_ref,
+    send_sem,
+    recv_sem,
 ):
     has, _ = held_head(lax.axis_index("ctx"), lax.rem(lax.axis_index("fsdp"), 2))
     blocks = x_ref.shape[0] // STEP
+    greet(ring_peers())
+    sender = Sender(send_sem, recv_sem)
+    push_rings(sender, down_ref, down_z_ref, down_x_ref)
+    push_rings(sender, fc_ref, fc_z_ref, fc_x_ref)
 
     @pl.when(has)
     def _():
@@ -331,6 +354,10 @@
             return carry
 
         lax.fori_loop(0, blocks, finish, 0)
+
+    for copy in sender.started:
+        copy.wait_recv()
+    sender.finish()
 
 
 def run_forward(rows):
@@ -356,11 +383,19 @@
     )(rows)
 
 
-def run_backward(rows, grads, wide, lse):
+def run_backward(rows, grads, wide, lse, fc, down, collective):
     length = rows.shape[0]
-    return pl.pallas_call(
+    inside = pl.BlockSpec(memory_space=pltpu.VMEM)
+    outside = pl.BlockSpec(memory_space=pl.ANY)
+    received = [
+        jax.ShapeDtypeStruct((3, 2, 2) + part.shape[2:], part.dtype)
+        for part in (fc, down, fc, down)
+    ]
+    results = pl.pallas_call(
         attend_backward,
-        out_shape=jax.ShapeDtypeStruct((length, 256), jnp.bfloat16),
+        out_shape=[jax.ShapeDtypeStruct((length, 256), jnp.bfloat16)] + received,
+        in_specs=[inside] * 4 + [outside] * 2,
+        out_specs=[inside] + [outside] * 4,
         scratch_shapes=[
             pltpu.VMEM((length, 64), jnp.bfloat16),
             pltpu.VMEM((length, 64), jnp.bfloat16),
@@ -369,14 +404,19 @@
             pltpu.VMEM((length, 64), jnp.bfloat16),
             pltpu.VMEM((64, length), jnp.float32),
             pltpu.VMEM((1, length), jnp.float32),
+            pltpu.SemaphoreType.DMA((12,)),
+            pltpu.SemaphoreType.DMA((12,)),
         ],
-        compiler_params=pltpu.CompilerParams(vmem_limit_bytes=40 << 20),
+        compiler_params=pltpu.CompilerParams(
+            collective_id=collective, has_side_effects=True, vmem_limit_bytes=40 << 20
+        ),
         cost_estimate=pl.CostEstimate(
             flops=5 * length * length * 64,
             bytes_accessed=length * 512 * 3,
             transcendentals=length * length // 2,
         ),
-    )(rows, grads, wide, lse)
+    )(rows, grads, wide, lse, fc, down)
+    return results[0], results[1:3], results[3:5]
 
 
 def pack_heads(*parts):
@@ -393,8 +433,9 @@
 
 
 UNITS = 17
-PIECE = 6528
 TAIL = 896
+SHAPES = ((16, 4352), (16, 4352), (64, 1088))
+PIECES = ((16, 2176), (16, 2176), (32, 1088))
 
 
 def places():
@@ -435,6 +476,11 @@
 def twin_peer():
     z, x, y_low, y_high, core = places()
     return device_at(z, x, y_low, y_high, 1 - core)
+
+
+def far_twin():
+    z, x, y_low, y_high, core = places()
+    return device_at(z, x, y_low, 1 - y_high, 1 - core)
 
 
 def ring_peers():
@@ -474,310 +520,385 @@
             copy.wait_send()
 
 
-GATHER_COPIES = 4 * 19 + 3
+class Mover:
+    def __init__(self, sem):
+        self.sem = sem
+        self.used = 0
+
+    def move(self, source, target):
+        copy = pltpu.make_async_copy(source, target, self.sem.at[self.used])
+        self.used += 1
+        copy.start()
+        return copy
+
+
+GATHER_COPIES = 4 * 35 + 3
 
 
 def gather_kernel(*refs):
     sources, small = refs[0:4], refs[4]
     targets, small_out = refs[5:9], refs[9]
-    own_sem, send_sem, recv_sem = refs[10:13]
+    holds, small_hold = refs[10:14], refs[14]
+    own_sem, send_sem, recv_sem = refs[15:18]
     z, x, y_low, y_high, core = places()
     mine = y_high * 2 + core
     cross = (1 - y_high) * 2 + core
-    other = y_high * 2 + 1 - core
-    other_cross = (1 - y_high) * 2 + 1 - core
-    greet(ring_peers() + [cross_peer(), far_peer(), twin_peer()] + [far_twin()])
+    mover = Mover(own_sem)
+    loads = [mover.move(sources[at], holds[at]) for at in range(4)]
+    loads.append(mover.move(small, small_hold))
+    greet(ring_peers() + [near_peer(), cross_peer(), far_peer(), twin_peer(), far_twin()])
     sender = Sender(send_sem, recv_sem)
-    starts = ((2 * z, 2), (8 + 2 * x, 2), (16, 1))
-    owns = []
-    for at in range(4):
-        owns.append(pltpu.make_async_copy(sources[at], targets[at].at[mine], own_sem.at[at]))
-    owns.append(pltpu.make_async_copy(small, small_out.at[mine], own_sem.at[4]))
-    small_in = [
+    firsts = (2 * z + y_low, 8 + 2 * x + y_low, 16)
+    others = (2 * z + 1 - y_low, 8 + 2 * x + 1 - y_low)
+    arrivals = [
         sender.push(small, small_out.at[mine], twin_peer()),
         sender.push(small, small_out.at[mine], far_peer()),
         sender.push(small, small_out.at[mine], far_twin()),
     ]
-    crossed = []
+    crossed = [
+        [
+            sender.push(sources[at].at[unit], targets[at].at[mine, unit], cross_peer())
+            for unit in others + (16,)
+        ]
+        for at in range(4)
+    ]
     for at in range(4):
-        crossed.append(
-            [
-                sender.push(
-                    sources[at].at[pl.ds(start, size)],
-                    targets[at].at[mine, pl.ds(start, size)],
-                    cross_peer(),
-                )
-                for start, size in starts
-            ]
-        )
-    for own in owns:
-        own.start()
-    twin_in = []
+        arrivals.append(sender.push(sources[at], targets[at].at[mine], twin_peer()))
+    owns = []
     for at in range(4):
-        twin_in.append(sender.push(sources[at], targets[at].at[mine], twin_peer()))
-    ringed = []
+        loads[at].wait()
+        owns.append(mover.move(holds[at], targets[at].at[mine]))
+    loads[4].wait()
+    owns.append(mover.move(small_hold, small_out.at[mine]))
+
+    def ring(at, part, unit, kept):
+        piece = targets[at].at[cross, unit]
+        for step in (1, 3, 2):
+            peer = z_peer(step) if part == 0 else x_peer(step)
+            kept.append((at, part, step, sender.push(piece, piece, peer)))
+
+    first_ring, second_ring = [], []
+
+    def second(at, nears):
+        for part in range(2):
+            nears[part].wait_recv()
+            ring(at, part, others[part], second_ring)
+            piece = targets[at].at[cross, others[part]]
+            arrivals.append(sender.push(piece, piece, twin_peer()))
+
+    waiting = None
     for at in range(4):
-        here = []
-        for part, (start, size) in enumerate(starts):
+        nears = []
+        for part in range(3):
             crossed[at][part].wait_recv()
-            piece = targets[at].at[cross, pl.ds(start, size)]
-            for step in (1, 3, 2):
-                if part < 2:
-                    peer = z_peer(step) if part == 0 else x_peer(step)
-                    here.append((part, step, sender.push(piece, piece, peer)))
-            twin_in.append(sender.push(piece, piece, twin_peer()))
-        ringed.append(here)
+            piece = targets[at].at[cross, firsts[part]]
+            if part < 2:
+                nears.append(sender.push(piece, piece, near_peer()))
+                ring(at, part, firsts[part], first_ring)
+            arrivals.append(sender.push(piece, piece, twin_peer()))
+        if waiting is not None:
+            second(*waiting)
+        waiting = (at, nears)
+    second(*waiting)
+
     for at in range(4):
-        for part, step, copy in ringed[at]:
-            copy.wait_recv()
-            if part == 0:
-                start = 2 * lax.rem(z - step + 4, 4)
-            else:
-                start = 8 + 2 * lax.rem(x - step + 4, 4)
-            piece = targets[at].at[cross, pl.ds(start, 2)]
-            twin_in.append(sender.push(piece, piece, twin_peer()))
-    for copy in small_in:
-        copy.wait_recv()
-    for copy in twin_in:
+        for kept, base in ((first_ring, y_low), (second_ring, 1 - y_low)):
+            for where, part, step, copy in kept:
+                if where != at:
+                    continue
+                copy.wait_recv()
+                if part == 0:
+                    unit = 2 * lax.rem(z - step + 4, 4) + base
+                else:
+                    unit = 8 + 2 * lax.rem(x - step + 4, 4) + base
+                piece = targets[at].at[cross, unit]
+                arrivals.append(sender.push(piece, piece, twin_peer()))
+    for copy in arrivals:
         copy.wait_recv()
     for own in owns:
         own.wait()
     sender.finish()
 
 
-def far_twin():
-    z, x, y_low, y_high, core = places()
-    return device_at(z, x, y_low, 1 - y_high, 1 - core)
-
-
 def gather_weights(parts, small, collective):
-    shapes = [jax.ShapeDtypeStruct((4,) + part.shape, part.dtype) for part in parts + [small]]
+    whole = list(parts) + [small]
+    shapes = [jax.ShapeDtypeStruct((4,) + part.shape, part.dtype) for part in whole]
     return pl.pallas_call(
         gather_kernel,
         out_shape=shapes,
         in_specs=[pl.BlockSpec(memory_space=pl.ANY)] * 5,
         out_specs=[pl.BlockSpec(memory_space=pl.ANY)] * 5,
-        scratch_shapes=[
-            pltpu.SemaphoreType.DMA((5,)),
+        scratch_shapes=[pltpu.VMEM(part.shape, part.dtype) for part in whole]
+        + [
+            pltpu.SemaphoreType.DMA((10,)),
             pltpu.SemaphoreType.DMA((GATHER_COPIES,)),
             pltpu.SemaphoreType.DMA((GATHER_COPIES,)),
         ],
-        compiler_params=pltpu.CompilerParams(collective_id=collective, has_side_effects=True),
+        compiler_params=pltpu.CompilerParams(
+            collective_id=collective, has_side_effects=True, vmem_limit_bytes=24 << 20
+        ),
         cost_estimate=pl.CostEstimate(flops=0, bytes_accessed=60 << 20, transcendentals=0),
-    )(*parts, small)
-
-
-def first_kernel(*refs):
-    parts, tail = refs[0:4], refs[4]
-    by_z, by_x, tail_out = refs[5:9], refs[9:13], refs[13]
-    send_sem, recv_sem = refs[14:16]
+    )(*whole)
+
+
+def push_rings(sender, terms, by_z, by_x):
     z, x, y_low, y_high, core = places()
-    greet(ring_peers())
-    sender = Sender(send_sem, recv_sem)
+    copies = []
     for step in (2, 1, 3):
         to_z, to_x = lax.rem(z + step, 4), lax.rem(x + step, 4)
-        for at in range(4):
-            sender.push(
-                parts[at].at[:, pl.ds(2 * to_z, 2)], by_z[at].at[step - 1], z_peer(step)
-            )
-            sender.push(
-                parts[at].at[:, pl.ds(8 + 2 * to_x, 2)], by_x[at].at[step - 1], x_peer(step)
-            )
-        sender.push(tail.at[:, to_z], tail_out.at[step - 1], z_peer(step))
-    for copy in sender.started:
-        copy.wait_recv()
-    sender.finish()
-
-
-def first_exchange(parts, tail, collective):
-    shapes = [
-        jax.ShapeDtypeStruct((3, 2, 2) + part.shape[2:], part.dtype) for part in parts + parts
+        copies.append(
+            sender.push(terms.at[:, pl.ds(2 * to_z, 2)], by_z.at[step - 1], z_peer(step))
+        )
+        copies.append(
+            sender.push(terms.at[:, pl.ds(8 + 2 * to_x, 2)], by_x.at[step - 1], x_peer(step))
+        )
+    return copies
+
+
+def widen(values):
+    return values.astype(jnp.float32)
+
+
+def halves(values, group):
+    if group == 2:
+        return values[0:32], values[32:64]
+    return values[:, 0:2176], values[:, 2176:4352]
+
+
+LAST_COPIES = 6 + 3 * (6 + 3 + 6 + 6 + 18) + 3 + 3 + 3 + 3 + 3 + 9
+
+
+def last_kernel(*refs):
+    terms, tail = refs[0:3], refs[3]
+    far_z, far_x = (None,) + refs[4:6], (None,) + refs[6:8]
+    totals, small_out = refs[8:11], refs[11]
+    scratch = refs[12:]
+    own, by, parted, met, merged, landed, summed = [
+        scratch[3 * at : 3 * at + 3] for at in range(7)
     ]
-    shapes.append(jax.ShapeDtypeStruct((3, 2, 4, 16, TAIL), tail.dtype))
-    results = pl.pallas_call(
-        first_kernel,
-        out_shape=shapes,
-        in_specs=[pl.BlockSpec(memory_space=pl.ANY)] * 5,
-        out_specs=[pl.BlockSpec(memory_space=pl.ANY)] * 9,
-        scratch_shapes=[pltpu.SemaphoreType.DMA((27,)), pltpu.SemaphoreType.DMA((27,))],
-        compiler_params=pltpu.CompilerParams(collective_id=collective, has_side_effects=True),
-        cost_estimate=pl.CostEstimate(flops=0, bytes_accessed=40 << 20, transcendentals=0),
-    )(*parts, tail)
-    return results[0:4], results[4:8], results[8]
-
-
-LAST_COPIES = 9 + 3 + 9 + 36
-
-
-def last_kernel(
-    tz_ref,
-    tx_ref,
-    td_ref,
-    gz_ref,
-    gx_ref,
-    gd_ref,
-    rz_ref,
-    rx_ref,
-    rd_ref,
-    sum_ref,
-    in_ref,
-    total_ref,
-    own_sem,
-    send_sem,
-    recv_sem,
-):
+    own_t, by_t, parted_t, met_t, merged_t, landed_t, summed_t, whole_t = scratch[21:29]
+    units, small_unit = scratch[29:32], scratch[32]
+    own_sem, send_sem, recv_sem = scratch[33:36]
     z, x, y_low, y_high, core = places()
+    mover = Mover(own_sem)
+    order = (2, 1, 0)
+    loads = {}
+    for group in order:
+        loads[group] = [
+            mover.move(terms[group].at[:, pl.ds(2 * z, 2)], own[group].at[0]),
+            mover.move(terms[group].at[:, pl.ds(8 + 2 * x, 2)], own[group].at[1]),
+        ]
+        if group > 0:
+            loads[group].append(mover.move(far_z[group], by[group].at[0]))
+            loads[group].append(mover.move(far_x[group], by[group].at[1]))
+    load_tail = mover.move(tail.at[:, z], own_t)
     greet(ring_peers() + [near_peer(), cross_peer(), far_peer()])
     sender = Sender(send_sem, recv_sem)
-    spans = ((0, PIECE), (PIECE, PIECE), (2 * PIECE, TAIL))
-    chunk = 1088
-    for step in (2, 1, 3):
-        to_z, to_x = lax.rem(z + step, 4), lax.rem(x + step, 4)
-        sender.push(tz_ref.at[to_x], rz_ref.at[step - 1], x_peer(step))
-        sender.push(tx_ref.at[to_z], rx_ref.at[step - 1], z_peer(step))
-        sender.push(td_ref.at[to_x], rd_ref.at[step - 1], x_peer(step))
-    for copy in sender.started:
+    first = push_rings(sender, terms[0], by[0].at[0], by[0].at[1])
+    first_t = [
+        sender.push(tail.at[:, lax.rem(z + step, 4)], by_t.at[step - 1], z_peer(step))
+        for step in (2, 1, 3)
+    ]
+
+    second = {}
+    for group in order:
+        for load in loads[group]:
+            load.wait()
+        if group == 0:
+            for copy in first:
+                copy.wait_recv()
+        second[group] = []
+        for ring in range(2):
+            for unit in range(2):
+                for side in range(2):
+                    total = widen(own[group][ring, side, unit])
+                    for step in range(3):
+                        total = total + widen(by[group][ring, step, side, unit])
+                    pair = halves(total.astype(jnp.bfloat16), group)
+                    parted[group][ring, 2 * unit, side] = pair[0]
+                    parted[group][ring, 2 * unit + 1, side] = pair[1]
+            for step in (2, 1, 3):
+                place = lax.rem(x + step, 4) if ring == 0 else lax.rem(z + step, 4)
+                peer = x_peer(step) if ring == 0 else z_peer(step)
+                second[group].append(
+                    sender.push(
+                        parted[group].at[ring, place], met[group].at[ring, step - 1], peer
+                    )
+                )
+    load_tail.wait()
+    for copy in first_t:
         copy.wait_recv()
-
-    groups = ((tz_ref, x, rz_ref), (tx_ref, z, rx_ref), (td_ref, x, rd_ref))
-    for (terms, mine, others), (start, size) in zip(groups, spans):
-        for low in range(0, size, PIECE // 3):
-            high = min(low + PIECE // 3, size)
-            total = terms[mine, :, :, low:high].astype(jnp.float32)
+    for place in range(4):
+        total = widen(own_t[:, place])
+        for step in range(3):
+            total = total + widen(by_t[step, :, place])
+        parted_t[place] = total.astype(jnp.bfloat16)
+    second_t = [
+        sender.push(parted_t.at[lax.rem(x + step, 4)], met_t.at[step - 1], x_peer(step))
+        for step in (2, 1, 3)
+    ]
+
+    def across(source, target):
+        return [
+            sender.push(source.at[0], target.at[0], near_peer()),
+            sender.push(source.at[1], target.at[1], cross_peer()),
+            sender.push(source.at[1], target.at[2], far_peer()),
+        ]
+
+    third = {}
+    for group in order:
+        for copy in second[group]:
+            copy.wait_recv()
+        for ring in range(2):
+            total = widen(parted[group][ring, x if ring == 0 else z])
             for step in range(3):
-                total = total + others[step, :, :, low:high].astype(jnp.float32)
-            sum_ref[:, :, start + low : start + high] = total.astype(jnp.bfloat16)
-
-    met = [
-        sender.push(sum_ref.at[0], in_ref.at[0], near_peer()),
-        sender.push(sum_ref.at[1], in_ref.at[1], cross_peer()),
-        sender.push(sum_ref.at[1], in_ref.at[2], far_peer()),
-    ]
-    for copy in met:
+                total = total + widen(met[group][ring, step])
+            merged[group][:, ring] = total.astype(jnp.bfloat16)
+        third[group] = across(merged[group], landed[group])
+    for copy in second_t:
         copy.wait_recv()
-    for start, size in spans:
-        for low in range(start, start + size, PIECE // 3):
-            high = min(low + PIECE // 3, start + size)
-            near = sum_ref[0, :, low:high].astype(jnp.float32) + in_ref[0, :, low:high].astype(
-                jnp.float32
-            )
-            away = in_ref[1, :, low:high].astype(jnp.float32) + in_ref[2, :, low:high].astype(
-                jnp.float32
-            )
-            total_ref[:, low:high] = (near + away).astype(jnp.bfloat16)
-
-    pieces = [total_ref.at[:, pl.ds(start, size)] for start, size in spans]
-    firsts = (gz_ref.at[z, x], gx_ref.at[x, z], gd_ref.at[z, x])
-    owns = [
-        pltpu.make_async_copy(pieces[at], firsts[at], own_sem.at[at]) for at in range(3)
-    ]
-    for own in owns:
-        own.start()
-    passed = []
+    total = widen(parted_t[x])
+    for step in range(3):
+        total = total + widen(met_t[step])
+    merged_t[...] = total.astype(jnp.bfloat16)
+    third_t = across(merged_t, landed_t)
+
+    def spot(group, ring, at_z, at_x):
+        unit = 2 * at_z + at_x // 2 if ring == 0 else 8 + 2 * at_x + at_z // 2
+        half = lax.rem(at_x, 2) if ring == 0 else lax.rem(at_z, 2)
+        if group == 2:
+            return totals[group].at[unit, pl.ds(pl.multiple_of(half * 32, 32), 32)]
+        return totals[group].at[unit, :, pl.ds(pl.multiple_of(half * 2176, 128), 2176)]
+
+    passed, ends, owns = [], [], []
+    for group in order:
+        for copy in third[group]:
+            copy.wait_recv()
+        near = widen(merged[group][0]) + widen(landed[group][0])
+        away = widen(landed[group][1]) + widen(landed[group][2])
+        summed[group][...] = (near + away).astype(jnp.bfloat16)
+        for ring in range(2):
+            place = spot(group, ring, z, x)
+            piece = summed[group].at[ring]
+            owns.append(mover.move(piece, place))
+            for step in (1, 3, 2):
+                peer = x_peer(step) if ring == 0 else z_peer(step)
+                passed.append((group, ring, step, sender.push(piece, place, peer)))
+            for step in (1, 3, 2):
+                peer = z_peer(step) if ring == 0 else x_peer(step)
+                ends.append(sender.push(piece, place, peer))
+    for copy in third_t:
+        copy.wait_recv()
+    near = widen(merged_t[0]) + widen(landed_t[0])
+    away = widen(landed_t[1]) + widen(landed_t[2])
+    summed_t[...] = (near + away).astype(jnp.bfloat16)
+    owns.append(mover.move(summed_t, whole_t.at[z, x]))
     for step in (1, 3, 2):
-        for at in range(3):
-            peer = z_peer(step) if at == 1 else x_peer(step)
-            passed.append((at, step, sender.push(pieces[at], firsts[at], peer)))
-    ends = []
+        passed.append((3, 0, step, sender.push(summed_t, whole_t.at[z, x], x_peer(step))))
     for step in (1, 3, 2):
-        for at in range(3):
-            peer = x_peer(step) if at == 1 else z_peer(step)
-            ends.append(sender.push(pieces[at], firsts[at], peer))
-    for at, step, copy in passed:
+        ends.append(sender.push(summed_t, whole_t.at[z, x], z_peer(step)))
+
+    for group, ring, step, copy in passed:
         copy.wait_recv()
-        from_x, from_z = lax.rem(x - step + 4, 4), lax.rem(z - step + 4, 4)
-        place = (gz_ref.at[z, from_x], gx_ref.at[x, from_z], gd_ref.at[z, from_x])[at]
+        if group == 3:
+            place = whole_t.at[z, lax.rem(x - step + 4, 4)]
+        elif ring == 0:
+            place = spot(group, ring, z, lax.rem(x - step + 4, 4))
+        else:
+            place = spot(group, ring, lax.rem(z - step + 4, 4), x)
         for other in (1, 3, 2):
-            peer = x_peer(other) if at == 1 else z_peer(other)
+            peer = z_peer(other) if ring == 0 else x_peer(other)
             ends.append(sender.push(place, place, peer))
     for copy in ends:
         copy.wait_recv()
-    for own in owns:
-        own.wait()
+    for copy in owns:
+        copy.wait()
+
+    def tile(at):
+        return whole_t[at // 28, at // 7 % 4, :, 128 * (at % 7) : 128 * (at % 7 + 1)]
+
+    for at in range(34):
+        units[0][:, 128 * at : 128 * (at + 1)] = tile(at)
+        units[1][:, 128 * at : 128 * (at + 1)] = tile(34 + at)
+    for row in range(4):
+        for at in range(9):
+            width = min(128, 1088 - 128 * at)
+            units[2][16 * row : 16 * row + 16, 128 * at : 128 * at + width] = tile(
+                68 + 9 * row + at
+            )[:, :width]
+    for at in range(8):
+        small_unit[:, 128 * at : 128 * (at + 1)] = tile(104 + at)
+    lasts = [mover.move(units[group], totals[group].at[16]) for group in range(3)]
+    lasts.append(mover.move(small_unit, small_out))
+    for copy in lasts:
+        copy.wait()
     sender.finish()
 
 
-def last_exchange(tz, tx, td, collective):
+def last_exchange(terms, tail, far_z, far_x, collective):
+    low = jnp.bfloat16
+
+    def each(make):
+        return [pltpu.VMEM(make(*pair), low) for pair in zip(SHAPES, PIECES)]
+
+    scratch = (
+        each(lambda unit, piece: (2, 2, 2) + unit)
+        + each(lambda unit, piece: (2, 3, 2, 2) + unit)
+        + each(lambda unit, piece: (2, 4, 2) + piece)
+        + each(lambda unit, piece: (2, 3, 2) + piece)
+        + each(lambda unit, piece: (2, 2) + piece)
+        + each(lambda unit, piece: (3, 2) + piece)
+        + each(lambda unit, piece: (2,) + piece)
+        + [
+            pltpu.VMEM((2, 4, 16, TAIL), low),
+            pltpu.VMEM((3, 2, 4, 16, TAIL), low),
+            pltpu.VMEM((4, 2, 16, TAIL), low),
+            pltpu.VMEM((3, 2, 16, TAIL), low),
+            pltpu.VMEM((2, 16, TAIL), low),
+            pltpu.VMEM((3, 16, TAIL), low),
+            pltpu.VMEM((16, TAIL), low),
+            pltpu.VMEM((4, 4, 16, TAIL), low),
+        ]
+        + each(lambda unit, piece: unit)
+        + [
+            pltpu.VMEM((16, 1024), low),
+            pltpu.SemaphoreType.DMA((24,)),
+            pltpu.SemaphoreType.DMA((LAST_COPIES,)),
+            pltpu.SemaphoreType.DMA((LAST_COPIES,)),
+        ]
+    )
     return pl.pallas_call(
         last_kernel,
-        out_shape=(
-            jax.ShapeDtypeStruct((4, 4, 16, PIECE), jnp.bfloat16),
-            jax.ShapeDtypeStruct((4, 4, 16, PIECE), jnp.bfloat16),
-            jax.ShapeDtypeStruct((4, 4, 16, TAIL), jnp.bfloat16),
+        out_shape=[jax.ShapeDtypeStruct((UNITS,) + unit, low) for unit in SHAPES]
+        + [jax.ShapeDtypeStruct((16, 1024), low)],
+        in_specs=[pl.BlockSpec(memory_space=pl.ANY)] * 8,
+        out_specs=[pl.BlockSpec(memory_space=pl.ANY)] * 4,
+        scratch_shapes=scratch,
+        compiler_params=pltpu.CompilerParams(
+            collective_id=collective, has_side_effects=True, vmem_limit_bytes=48 << 20
         ),
-        in_specs=[pl.BlockSpec(memory_space=pltpu.VMEM)] * 3,
-        out_specs=[pl.BlockSpec(memory_space=pl.ANY)] * 3,
-        scratch_shapes=[
-            pltpu.VMEM((3, 2, 16, PIECE), jnp.bfloat16),
-            pltpu.VMEM((3, 2, 16, PIECE), jnp.bfloat16),
-            pltpu.VMEM((3, 2, 16, TAIL), jnp.bfloat16),
-            pltpu.VMEM((2, 16, 2 * PIECE + TAIL), jnp.bfloat16),
-            pltpu.VMEM((3, 16, 2 * PIECE + TAIL), jnp.bfloat16),
-            pltpu.VMEM((16, 2 * PIECE + TAIL), jnp.bfloat16),
-            pltpu.SemaphoreType.DMA((3,)),
-            pltpu.SemaphoreType.DMA((LAST_COPIES,)),
-            pltpu.SemaphoreType.DMA((LAST_COPIES,)),
-        ],
-        compiler_params=pltpu.CompilerParams(
-            collective_id=collective, has_side_effects=True, vmem_limit_bytes=40 << 20
-        ),
-        cost_estimate=pl.CostEstimate(flops=0, bytes_accessed=16 << 20, transcendentals=0),
-    )(tz, tx, td)
-
-
-def flat_units(parts):
-    lead = parts[0].shape[:-2]
-    down = parts[3].reshape(lead + (4, 16, 1088))
-    down = jnp.moveaxis(down, -3, -2).reshape(lead + (16, 4352))
-    return jnp.concatenate([parts[0], parts[1], parts[2], down], axis=-1)
-
-
-def wide_units(flat):
-    lead = flat.shape[:-2]
-    down = flat[..., 8704:].reshape(lead + (16, 4, 1088))
-    down = jnp.moveaxis(down, -2, -3).reshape(lead + (64, 1088))
-    return flat[..., :3264], flat[..., 3264:4352], flat[..., 4352:8704], down
-
-
-def reduce_grads(parts, small, collective):
-    z, x, y_low, y_high, core = places()
-    parts = [part.reshape(2, UNITS, part.shape[1] // UNITS, part.shape[2]) for part in parts]
-    last = flat_units([part[:, 16] for part in parts])
-    extra = jnp.pad(small, ((0, 0), (0, 16 * 1280 - small.shape[1]))).reshape(2, 16, 1280)
-    tail = jnp.concatenate([last, extra.astype(jnp.bfloat16)], axis=-1)
+        cost_estimate=pl.CostEstimate(flops=0, bytes_accessed=40 << 20, transcendentals=0),
+    )(*terms, tail, *far_z, *far_x)
+
+
+def reduce_grads(terms, small, far_z, far_x, collective):
+    down = terms[2][:, 16].reshape(2, 4, 16, 1088)
+    down = jnp.pad(down, ((0, 0), (0, 0), (0, 0), (0, 64)))
+    down = jnp.transpose(down, (0, 2, 1, 3)).reshape(2, 16, 4608)
+    extra = jnp.pad(small, ((0, 0), (0, 16 * 1024 - small.shape[1]))).reshape(2, 16, 1024)
+    tail = jnp.concatenate(
+        [terms[0][:, 16], terms[1][:, 16], down, extra.astype(jnp.bfloat16)], axis=-1
+    )
     tail = jnp.transpose(tail.reshape(2, 16, 4, 4, TAIL), (0, 2, 3, 1, 4))
-    by_z, by_x, by_tail = first_exchange(parts, tail, collective)
-
-    def added(own, others):
-        total = own.astype(jnp.float32)
-        for step in range(3):
-            total = total + others[step].astype(jnp.float32)
-        return total.astype(jnp.bfloat16)
-
-    def first_sum(start, others):
-        sums = []
-        for part, other in zip(parts, others):
-            size = (2, 2) + part.shape[2:]
-            sums.append(added(lax.dynamic_slice(part, (0, start, 0, 0), size), other))
-        flat = flat_units(sums).reshape(2, 2, 16, 2, PIECE)
-        return jnp.transpose(flat, (1, 3, 0, 2, 4)).reshape(4, 2, 16, PIECE)
-
-    tz = first_sum(2 * z, by_z)
-    tx = first_sum(8 + 2 * x, by_x)
-    td = added(lax.dynamic_index_in_dim(tail, z, 1, keepdims=False), by_tail)
-    gz, gx, gd = last_exchange(tz, tx, jnp.transpose(td, (1, 0, 2, 3)), collective + 1)
-
-    def units(whole):
-        turned = jnp.transpose(whole.reshape(8, 2, 16, PIECE), (0, 2, 1, 3))
-        return turned.reshape(8, 16, 2 * PIECE)
-
-    tail_all = jnp.transpose(gd, (2, 0, 1, 3)).reshape(1, 16, 16 * TAIL)
-    flat = jnp.concatenate([units(gz), units(gx), tail_all[:, :, : 2 * PIECE]], axis=0)
-    outs = wide_units(flat)
-    widths = [(272, 3264), (272, 1088), (272, 4352), (1088, 1088)]
-    outs = [out.reshape(shape).astype(jnp.float32) for out, shape in zip(outs, widths)]
-    extras = tail_all[0, :, 2 * PIECE :].reshape(-1)[:3264].astype(jnp.float32)
-    return outs, extras
+    joint, fc, down, small = last_exchange(terms, tail, far_z, far_x, collective)
+    joint = joint.reshape(272, 4352)
+    outs = (
+        joint[:, :3264].astype(jnp.float32),
+        joint[:, 3264:].astype(jnp.float32),
+        fc.reshape(272, 4352).astype(jnp.float32),
+        down.reshape(1088, 1088).astype(jnp.float32),
+    )
+    return outs, small.reshape(-1)[:3264].astype(jnp.float32)
 
 
 def norm_rows(values, gain_vec, offset):
@@ -867,7 +988,7 @@
             (((0,), (0,)), ((), ())),
             preferred_element_type=jnp.float32,
         ).astype(jnp.bfloat16)
-        return terms.reshape(2, terms.shape[0] // 2, terms.shape[1])
+        return terms.reshape(2, UNITS, terms.shape[0] // (2 * UNITS), terms.shape[1])
 
     scale_one = g_scale1.astype(jnp.float32)
     shift_one = g_shift1.astype(jnp.float32)
@@ -920,7 +1041,9 @@
         "te,de->td", grad_branch, full_out, preferred_element_type=jnp.float32
     ).astype(jnp.bfloat16)
     grad_rows = spread_heads(pack_heads(grad_attended, jnp.zeros_like(grad_attended)), ctx_count, 3)
-    joint_rows_grad = run_backward(head_rows, grad_rows, wide_out, lse_rows)
+    joint_rows_grad, far_z, far_x = run_backward(
+        head_rows, grad_rows, wide_out, lse_rows, d_fc, d_down, 7
+    )
     packed_grads = collect_heads(joint_rows_grad, ctx_count, 4)
     grad_q16 = unpack_heads(packed_grads, 0)
     grad_k16 = unpack_heads(packed_grads, 1)
@@ -936,7 +1059,9 @@
     sums = jnp.concatenate([vector.reshape(4, -1) for vector in narrow], axis=1)
     keep, give = split(sums.reshape(1, -1))
     sums = (keep + swap(give)).reshape(2, 3264)
-    (t_qkv, t_out, t_fc, t_down), extras = reduce_grads((d_qkv, d_out, d_fc, d_down), sums, 6)
+    (t_qkv, t_out, t_fc, t_down), extras = reduce_grads(
+        (jnp.concatenate([d_qkv, d_out], axis=-1), d_fc, d_down), sums, far_z, far_x, 6
+    )
     (t_scale1, t_shift1, t_bq, t_bv, t_bout, t_scale2, t_shift2, t_bdown) = [
         extras[at * 272 : (at + 1) * 272] for at in range(8)
     ]

time: 779 us -> 533 us (0.68)
  Pallas kernels: 569 us -> 347 us
  local copies, waits for them, and re-layouts: 101 us -> 77.2 us
    pallas_call x1, Pallas kernels: 228 us -> 58.1 us  [gather_weights(): pl.pallas_call(gather_kernel, out_shape=shapes, in_specs=[pl.BlockSpec(me...]
    pallas_call x3 -> x2, Pallas kernels: 223 us -> 171 us  [the longest x1 117 us: last_exchange(): pl.pallas_call(last_kernel, out_shape=[jax.ShapeDtypeStruct((UNITS,) + un...]
    reshape x12 -> x1, local copies, waits for them, and re-layouts: 33 us -> 0.85 us  [reduce_grads(): down = jnp.transpose(down, (0, 2, 1, 3)).reshape(2, 16, 4608)]
    convert_element_type x2 -> x0, local copies, waits for them, and re-layouts: 12.1 us -> none  [reduce_grads(): out.reshape(shape).astype(jnp.float32)]
    convert_element_type x9 -> x5, other arithmetic: 21.2 us -> 11.5 us  [the longest x1 3.7 us: reduce_grads(): joint[:, :3264].astype(jnp.float32)]
    unnamed x116 -> x101, local copies, waits for them, and re-layouts: 14.9 us -> 23.6 us
  transfers between devices with their start and end apart: 9 -> 9, of which waited for: 1 -> 0; matrix products, arithmetic and copies ran while one was open for 7% -> 16% of each run, Pallas kernels for 11% -> 19%
where the time goes in v3:
time: 533 us; the launch traced here: 525 us
  Pallas kernels  347 us (65%)
  local copies, waits for them, and re-layouts  77.2 us (14%)
  matrix products  61.3 us (12%)
  other arithmetic  34.9 us (7%)
    pallas_call x1, Pallas kernels, last_exchange(): pl.pallas_call(last_kernel, out_shape=[jax.ShapeDtypeStruct((UNITS,) + un...  117 us
    pallas_call x1, Pallas kernels, gather_weights(): pl.pallas_call(gather_kernel, out_shape=shapes, in_specs=[pl.BlockSpec(me...  58.1 us
    pallas_call x1, Pallas kernels, run_backward(): pl.pallas_call(attend_backward, out_shape=[jax.ShapeDtypeStruct((length,...  53.6 us
    pallas_call x2, Pallas kernels, spread_heads(): pl.pallas_call(functools.partial(spread_kernel, count), out_shape=jax.Sha...  51.8 us
    pallas_call x2, Pallas kernels, collect_heads(): pl.pallas_call(functools.partial(collect_kernel, count), out_shape=jax.Sh...  41 us
    pallas_call x1, Pallas kernels, run_forward(): pl.pallas_call(attend_forward, out_shape=(jax.ShapeDtypeStruct((length, 1...  25.4 us
    unnamed x101, local copies, waits for them, and re-layouts  23.6 us
    dot_general x4, matrix products, weight_terms(): lax.dot_general(left_rows(left), right_rows(right), (((0,), (0,)), ((), (...  15.7 us
  transfers between devices with their start and end apart: 9, of which 0 were waited for; matrix products, arithmetic and copies ran while one was open for 16% of the time, Pallas kernels for 19%

profile of v3, /device:TPU:8, one launch (start us, length us, event | category | flops | bytes accessed | tf_op | source)
XLA Modules:
  0.0 524.8 jit_solution(7453627720099678338)
XLA Ops:
  0.6 6.3 %concatenate.64 = bf16[3264]{0:T(1024)(128)(2,1)S(1)} concatenate(bf16[272]{0:T(512)(128)(2,1)} %param.17, bf16[272]{0:T(512)(128)(2,1)} %param.18, bf16[272]{0:T(512)(128)(2,1)} %param.20, bf16[272]{0:T(512)(128)(2,1)} %param.21, bf16[272]{0:T(512)(128)(2,1)} %param.23, bf16[272]{0:T(512)(128)(2,1)} %param.24, bf16[272]{0:T(512)(128)(2,1)} %param.25, bf16[272]{0:T(512)(128)(2,1)} %param.29, ...), dimensions={0} | concatenate | bytes 13056 | tf_op jit(solution)/shard_map/concatenate | solution.py:948
  12.9 58.1 %shard_map.262 = (bf16[4,17,16,3264]{3,2,1,0:T(8,128)(2,1)S(1)}, bf16[4,17,16,1088]{3,2,1,0:T(8,128)(2,1)S(1)}, bf16[4,17,16,4352]{3,2,1,0:T(8,128)(2,1)S(1)}, b...) custom-call(bf16[17,16,3264]{2,1,0:T(8,128)(2,1)S(1)} %bitcast.185, bf16[17,16,1088]{2,1,0:T(8,128)(2,1)S(1)} %bitcast.186, ...), custom_call_target="tpu_custom_call" | custom-call | bytes 62914560 | tf_op jit(solution)/shard_map/pallas_call | solution.py:626
  71.1 3.6 copy-done
  74.7 3.0 copy-done.1
  79.7 6.4 %fusion.38 = f32[128,3264]{0,1:T(8,128)S(1)} fusion(bf16[1088,3264]{1,0:T(8,128)(2,1)} %bitcast.178, bf16[1,128,1088]{1,2,0:T(8,128)(2,1)S(1)} %copy-done.17, f32[1088]{0:T(1024)S(1)} %reshape.481, f32[1088]{0:T(1024)S(1)} %reshape.480, f32[128]{0:T(128)S(1)} %fusion.61, f32[128]{0:T(128)S(1)} %broadcast_multiply_fusion.1), kind=kOutput, calls=%fused_computation.96 | convolution fusion | flops 909950976 | bytes 9061888 | tf_op jit(solution)/shard_map/dot_general | solution.py:1000
  93.4 2.8 maximum_bitcast_fusion.x_ref
  96.2 31.2 %shard_map.263.x_ref = bf16[4096,256]{1,0:T(8,128)(2,1)} custom-call(bf16[17,128,256]{2,1,0:T(8,128)(2,1)} %maximum_bitcast_fusion.x_ref), custom_call_target="tpu_custom_call" | custom-call | bytes 4194304 | tf_op jit(solution)/shard_map/pallas_call | solution.py:174
  129.0 25.4 %shard_map.264 = (bf16[4096,128]{1,0:T(8,128)(2,1)S(1)}, f32[64,4096]{1,0:T(8,128)S(1)}, f32[1,4096]{1,0:T(1,128)S(1)}) custom-call(bf16[4096,256]{1,0:T(8,128)(2,1)S(1)} %copy-done.4), custom_call_target="tpu_custom_call" | custom-call | flops 2147483648 | bytes 4194304 | tf_op jit(solution)/shard_map/pallas_call | solution.py:365
  156.4 13.9 %shard_map.265 = bf16[17,128,128]{2,1,0:T(8,128)(2,1)} custom-call(bf16[4096,128]{1,0:T(8,128)(2,1)} %copy-done.12), custom_call_target="tpu_custom_call" | custom-call | bytes 4194304 | tf_op jit(solution)/shard_map/pallas_call | solution.py:191
  175.4 7.1 %multiply_convert_fusion = (bf16[128,4352]{1,0:T(8,128)(2,1)}, f32[128,4352]{1,0:T(8,128)S(1)}) fusion(f32[4352]{0:T(1024)S(1)} %reshape.487, bf16[128,1088]{0,1:T(8,128)(2,1)S(1)} %add_convert_fusion, bf16[1088,4352]{1,0:T(8,128)(2,1)} %bitcast.176), kind=kOutput, calls=%fused_computation.32 | convolution fusion | flops 1217724416 | bytes 13108224 | tf_op jit(solution)/shard_map/dot_general | solution.py:1015
  182.5 7.2 %convert_reduce_fusion = (f32[4352]{0:T(1024)}, bf16[128,4352]{1,0:T(8,128)(2,1)}) fusion(f32[128,4352]{1,0:T(8,128)S(1)} %get-tuple-element.93, bf16[4352,1088]{1,0:T(8,128)(2,1)S(1)} %bitcast.201, bf16[1,128,1088]{1,2,0:T(8,128)(2,1)} %param.16), kind=kOutput, calls=%fused_computation.31 | convolution fusion | flops 1226632960 | bytes 13108224 | tf_op jit(solution)/shard_map/td,fd->tf/dot_general | solution.py:1028
  195.5 6.8 %multiply_reduce_fusion = (f32[1088]{0:T(1024)S(1)}, f32[128]{0:T(128)S(1)}, f32[1088]{0:T(1024)S(1)}, f32[128,1088]{0,1:T(8,128)S(1)}) fusion(f32[128,1088]{0,1:T(8,128)S(1)} %get-tuple-element.91, f32[128]{0:T(128)S(1)} %fusion.62, f32[128]{0:T(128)S(1)} %broadcast_multiply_fusion, f32[1088]{0:T(1024)S(1)} %reshape.485, ...), kind=kOutput, calls=%fused_computation.74 | convolution fusion | flops 1213265664 | bytes 11712768 | tf_op jit(solution)/shard_map/tf,df->td/dot_general | solution.py:1034
  210.2 8.0 %fusion.3 = bf16[1,128,1088]{1,2,0:T(8,128)(2,1)} fusion(f32[128,1088]{0,1:T(8,128)S(1)} %get-tuple-element.91, bf16[128,4352]{1,0:T(8,128)(2,1)} %get-tuple-element.92, bf16[4352,1088]{1,0:T(8,128)(2,1)} %bitcast.198, f32[1088]{0:T(1024)S(1)} %reshape.488), kind=kOutput, calls=%fused_computation.21 | convolution fusion | flops 1212571648 | bytes 11424000 | tf_op jit(solution)/shard_map/dot_general | solution.py:1020
  221.1 20.5 %shard_map.266.g_ref = bf16[4096,128]{1,0:T(8,128)(2,1)} custom-call(bf16[17,128,128]{2,1,0:T(8,128)(2,1)} %pad_bitcast_fusion.x_ref), custom_call_target="tpu_custom_call" | custom-call | bytes 4194304 | tf_op jit(solution)/shard_map/pallas_call | solution.py:174
  248.4 4.9 convolution_convert_fusion
  253.3 8.2 %copy.49 = bf16[2176,1088]{1,0:T(8,128)(2,1)} copy(bf16[2176,1088]{0,1:T(8,128)(2,1)} %convolution_convert_fusion) | data formatting | bytes 9469952 | tf_op jit(solution)/shard_map/convert_element_type | solution.py:990
  263.7 5.3 %convolution_convert_fusion.1 = bf16[544,4352]{1,0:T(8,128)(2,1)} fusion(bf16[128,4352]{1,0:T(8,128)(2,1)} %collective-permute-done.1, bf16[128,4352]{1,0:T(8,128)(2,1)} %get-tuple-element.97, bf16[128,544]{0,1:T(8,128)(2,1)S(1)} %collective-permute-done, bf16[128,544]{0,1:T(8,128)(2,1)S(1)} %bitcast.225), kind=kOutput, calls=%fused_computation.1 | convolution fusion | flops 1219534848 | bytes 7241728 | tf_op jit(solution)/shard_map/dot_general | solution.py:985
  269.0 53.6 %shard_map.267 = (bf16[4096,256]{1,0:T(8,128)(2,1)S(1)}, bf16[3,2,2,16,4352]{4,3,2,1,0:T(8,128)(2,1)S(1)}, bf16[3,2,2,64,1088]{4,3,2,1,0:T(8,128)(2,1)S(1)}, bf1...) custom-call(bf16[4096,256]{1,0:T(8,128)(2,1)S(1)} %copy-done.5, bf16[4096,128]{1,0:T(8,128)(2,1)S(1)} %copy-done.11, ...), custom_call_target="tpu_custom_call" | custom-call | flops 5368709120 | bytes 6291456 | tf_op jit(solution)/shard_map/pallas_call | solution.py:394
  326.5 27.2 %shard_map.268 = bf16[17,128,256]{2,1,0:T(8,128)(2,1)} custom-call(bf16[4096,256]{1,0:T(8,128)(2,1)} %copy-done.6), custom_call_target="tpu_custom_call" | custom-call | bytes 4194304 | tf_op jit(solution)/shard_map/pallas_call | solution.py:191
  362.4 5.5 %fusion.69 = (f32[1088]{0:T(1024)S(1)}, f32[128]{0:T(128)S(1)}, f32[128,1088]{0,1:T(8,128)S(1)}) fusion(f32[1088]{0:T(1024)S(1)} %reshape.480, f32[128]{0:T(128)S(1)} %broadcast_multiply_fusion.1, bf16[1,128,1088]{1,2,0:T(8,128)(2,1)} %param.15, bf16[1088,3264]{1,0:T(8,128)(2,1)} %bitcast.179, bf16[128,1088]{0,1:T(8,128)(2,1)} %bitcast.213, ...), kind=kOutput, calls=%fused_computation.165 | convolution fusion | flops 912456512 | bytes 8783360 | tf_op jit(solution)/shard_map/te,de->td/dot_general | solution.py:1055
  384.6 2.9 pad_maximum_fusion.refs_0_
  389.6 3.2 reshape.477
  394.5 117.3 %shard_map.269 = (bf16[17,16,4352]{2,1,0:T(8,128)(2,1)}, bf16[17,16,4352]{2,1,0:T(8,128)(2,1)}, bf16[17,64,1088]{2,1,0:T(8,128)(2,1)}, bf16[16,1024]{1,0:T(8,128)(2,1)S(1)}) custom-call(bf16[2,17,16,4352]{3,2,1,0:T(8,128)(2,1)} %pad_maximum_fusion.refs_0_, bf16[2,17,16,4352]{3,2,1,0:T(8,128)(2,1)} %bitcast.191, bf16[2,17,64,1088]{3,2,1,0:T(8,128)(2,1)} %bitcast.194, ...), custom_call_target="tpu_custom_call" | custom-call | bytes 41943040 | tf_op jit(solution)/shard_map/pallas_call | solution.py:870
  511.8 3.7 slice_convert_fusion
  (219 shorter events, 91.0 us)
Async XLA Ops:
  12.9 65.7 %copy-start.17 = (bf16[1,128,1088]{1,2,0:T(8,128)(2,1)S(1)}, bf16[1,128,1088]{1,2,0:T(8,128)(2,1)}, u32[]{:S(2)}) copy-start(bf16[1,128,1088]{1,2,0:T(8,128)(2,1)} %param.15) | copy-start | bytes 835588
  78.8 291.1 %copy-start.39 = (f32[128]{0:T(128)}, f32[128]{0:T(128)S(1)}, u32[]{:S(2)}) copy-start(f32[128]{0:T(128)S(1)} %broadcast_multiply_fusion.1) | copy-start | bytes 1540
  79.5 138.9 %copy-start.40 = (f32[128]{0:T(128)}, f32[128]{0:T(128)S(1)}, u32[]{:S(2)}) copy-start(f32[128]{0:T(128)S(1)} %fusion.61) | copy-start | bytes 1540
  172.5 9.9 %slice-start = ((s8[10027008]{0:T(1024)(128)(4,1)}), s8[4194304]{0:T(1024)(128)(4,1)S(1)}, s32[]{:S(2)}) async-start(s8[10027008]{0:T(1024)(128)(4,1)} %bitcast.199), calls=%async_computation | async-start | bytes 8388608
  175.3 7.1 %copy-start.23 = (bf16[128,1088]{0,1:T(8,128)(2,1)}, bf16[128,1088]{0,1:T(8,128)(2,1)S(1)}, u32[]{:S(2)}) copy-start(bf16[128,1088]{0,1:T(8,128)(2,1)S(1)} %add_convert_fusion) | copy-start | bytes 835588
  175.3 7.1 %slice-start.1 = ((s8[10027008]{0:T(1024)(128)(4,1)}), s8[4194304]{0:T(1024)(128)(4,1)S(1)}, s32[]{:S(2)}) async-start(s8[10027008]{0:T(1024)(128)(4,1)} %bitcast.199), calls=%async_computation.1 | async-start | bytes 8388608
  175.4 7.1 %slice-start.2 = ((s8[10027008]{0:T(1024)(128)(4,1)}), s8[1638400]{0:T(1024)(128)(4,1)S(1)}, s32[]{:S(2)}) async-start(s8[10027008]{0:T(1024)(128)(4,1)} %bitcast.199), calls=%async_computation.2 | async-start | bytes 3276800
  189.6 74.0 %collective-permute-start.1 = (bf16[128,4352]{1,0:T(8,128)(2,1)}, bf16[128,4352]{1,0:T(8,128)(2,1)}, u32[]{:S(2)}, u32[]{:S(2)}) collective-permute-start(bf16[128,4352]{1,0:T(8,128)(2,1)} %get-tuple-element.97), channel_id=1, source_target_pairs={{0,1},{1,0},{2,3},{3,2},{4,5},{5,4},{6,7},{7,6},{8,9},{9,8},{10,11... | collective-permute-start | bytes 3342344 | tf_op jit(solution)/shard_map/ppermute | solution.py:966
  195.0 53.4 %collective-permute-start.2 = (bf16[128,2176]{0,1:T(8,128)(2,1)}, bf16[128,2176]{0,1:T(8,128)(2,1)}, u32[]{:S(2)}, u32[]{:S(2)}) collective-permute-start(bf16[128,2176]{0,1:T(8,128)(2,1)} %bitcast.31), channel_id=1, source_target_pairs={{0,1},{1,0},{2,3},{3,2},{4,5},{5,4},{6,7},{7,6},{8,9},{9,8},{10,11... | collective-permute-start | bytes 1671176 | tf_op jit(solution)/shard_map/ppermute | solution.py:966
  195.5 52.9 %collective-permute-start.3 = (bf16[128,1088]{0,1:T(8,128)(2,1)}, bf16[128,1088]{0,1:T(8,128)(2,1)}, u32[]{:S(2)}, u32[]{:S(2)}) collective-permute-start(bf16[128,1088]{0,1:T(8,128)(2,1)} %bitcast.17), channel_id=1, source_target_pairs={{0,1},{1,0},{2,3},{3,2},{4,5},{5,4},{6,7},{7,6},{8,9},{9,8},{10,11... | collective-permute-start | bytes 835592 | tf_op jit(solution)/shard_map/ppermute | solution.py:966
  205.7 39.5 %collective-permute-start.7 = (bf16[128,1088]{0,1:T(8,128)(2,1)}, bf16[128,1088]{0,1:T(8,128)(2,1)}, u32[]{:S(2)}, u32[]{:S(2)}) collective-permute-start(bf16[128,1088]{0,1:T(8,128)(2,1)} %get-tuple-element.59), channel_id=1, source_target_pairs={{0,1},{1,0},{2,3},{3,2},{4,5},{5,4},{6,7},{7,6},{8,9},{9,8},{10,11... | collective-permute-start | bytes 835592 | tf_op jit(solution)/shard_map/ppermute | solution.py:966
  206.3 38.9 %collective-permute-start.6 = (bf16[128,544]{0,1:T(8,128)(2,1)S(1)}, bf16[128,544]{0,1:T(8,128)(2,1)}, u32[]{:S(2)}, u32[]{:S(2)}) collective-permute-start(bf16[128,544]{0,1:T(8,128)(2,1)S(1)} %bitcast.231), channel_id=1, source_target_pairs={{0,1},{1,0},{2,3},{3,2},{4,5},{5,4},{6,7},{7,6},{8,9},{9,8},{10,11... | collective-permute-start | bytes 417800 | tf_op jit(solution)/shard_map/ppermute | solution.py:966
  210.2 8.0 %copy-start.24 = (bf16[128,1088]{0,1:T(8,128)(2,1)S(1)}, bf16[128,1088]{0,1:T(8,128)(2,1)}, u32[]{:S(2)}) copy-start(bf16[128,1088]{0,1:T(8,128)(2,1)} %copy-done.23) | copy-start | bytes 835588
  210.2 8.1 %copy-start.27 = (bf16[128,2,1088]{0,2,1:T(8,128)(2,1)S(1)}, bf16[128,2,1088]{0,2,1:T(8,128)(2,1)}, u32[]{:S(2)}) copy-start(bf16[128,2,1088]{0,2,1:T(8,128)(2,1)} %get-tuple-element.67) | copy-start | bytes 1671172
  219.1 22.6 %copy-start.35 = (f32[1088]{0:T(1024)S(1)}, f32[1088]{0:T(1024)}, u32[]{:S(2)}) copy-start(f32[1088]{0:T(1024)} %get-tuple-element.58) | copy-start | bytes 13060
  219.1 25.3 %copy-start.38 = (f32[4352]{0:T(1024)S(1)}, f32[4352]{0:T(1024)}, u32[]{:S(2)}) copy-start(f32[4352]{0:T(1024)} %get-tuple-element.96) | copy-start | bytes 52228
  245.2 18.5 %collective-permute-start = (bf16[128,544]{0,1:T(8,128)(2,1)S(1)}, bf16[128,544]{0,1:T(8,128)(2,1)S(1)}, u32[]{:S(2)}, u32[]{:S(2)}) collective-permute-start(bf16[128,544]{0,1:T(8,128)(2,1)S(1)} %bitcast.230), channel_id=1, source_target_pairs={{0,1},{1,0},{2,3},{3,2},{4,5},{5,4},{6,7},{7,6},{8,9},{9,8},{10,11... | collective-permute-start | bytes 417800 | tf_op jit(solution)/shard_map/ppermute | solution.py:966
  245.2 136.6 %collective-permute-start.4 = (bf16[128,544]{0,1:T(8,128)(2,1)}, bf16[128,544]{0,1:T(8,128)(2,1)}, u32[]{:S(2)}, u32[]{:S(2)}) collective-permute-start(bf16[128,544]{0,1:T(8,128)(2,1)} %bitcast.44), channel_id=1, source_target_pairs={{0,1},{1,0},{2,3},{3,2},{4,5},{5,4},{6,7},{7,6},{8,9},{9,8},{10,11... | collective-permute-start | bytes 417800 | tf_op jit(solution)/shard_map/ppermute | solution.py:966
  362.4 5.5 %copy-start.30 = (bf16[128,17,64]{0,2,1:T(8,128)(2,1)S(1)}, bf16[128,17,64]{0,2,1:T(8,128)(2,1)}, u32[]{:S(2)}) copy-start(bf16[128,17,64]{0,2,1:T(8,128)(2,1)} %copy.52) | copy-start | bytes 835588
  362.4 5.5 %copy-start.31 = (bf16[128,17,64]{0,2,1:T(8,128)(2,1)S(1)}, bf16[128,17,64]{0,2,1:T(8,128)(2,1)}, u32[]{:S(2)}) copy-start(bf16[128,17,64]{0,2,1:T(8,128)(2,1)} %copy.51) | copy-start | bytes 835588
  362.4 5.5 %copy-start.32 = (bf16[128,17,64]{0,2,1:T(8,128)(2,1)S(1)}, bf16[128,17,64]{0,2,1:T(8,128)(2,1)}, u32[]{:S(2)}) copy-start(bf16[128,17,64]{0,2,1:T(8,128)(2,1)} %copy.50) | copy-start | bytes 835588
  376.8 5.0 collective-permute-start.5
  377.6 3.2 collective-permute-start.8
  511.8 7.4 %copy-start.26 = (bf16[17,16,4352]{2,1,0:T(8,128)(2,1)S(1)}, bf16[17,16,4352]{2,1,0:T(8,128)(2,1)}, u32[]{:S(2)}) copy-start(bf16[17,16,4352]{2,1,0:T(8,128)(2,1)} %get-tuple-element.47) | copy-start | bytes 7102468
  (34 other events, 81.3 us)

commit v4 on v3

--- a/solution.py
+++ b/solution.py
@@ -1,5 +1,4 @@
 import functools
-import math
 
 import jax
 import jax.numpy as jnp
@@ -219,9 +218,19 @@
     return keys <= asks
 
 
-def attend_forward(x_ref, out_ref, wide_ref, lse_ref, q_ref, k_ref, vt_ref):
+def attend_forward(*refs):
+    x_ref, sources = refs[0], refs[1:4]
+    out_ref, wide_ref, lse_ref = refs[4:7]
+    targets = refs[7:10]
+    q_ref, k_ref, vt_ref = refs[10:13]
+    holds = refs[13:16]
+    own_sem, send_sem, recv_sem = refs[16:19]
     has, _ = held_head(lax.axis_index("ctx"), lax.rem(lax.axis_index("fsdp"), 2))
     blocks = x_ref.shape[0] // STEP
+    greet(gather_peers())
+    sender = Sender(send_sem, recv_sem)
+    steps = gather_steps(sources, targets, holds, Mover(own_sem), sender)
+    next(steps)
 
     @pl.when(has)
     def _():
@@ -234,39 +243,44 @@
 
         lax.fori_loop(0, blocks, prepare, 0)
 
-        def one_block(at, carry):
-            asks = pl.ds(pl.multiple_of(at * STEP, STEP), STEP)
-            query = q_ref[asks, :]
-
-            def update(state, place, masked):
-                top, total, accum = state
-                keys = pl.ds(pl.multiple_of(place * STEP, STEP), STEP)
-                scores = dot_nt(k_ref[keys, :], query)
-                if masked:
-                    scores = jnp.where(causal(scores), scores, -1e30)
-                new_top = jnp.maximum(top, jnp.max(scores, axis=0, keepdims=True))
-                factor = jnp.exp(top - new_top)
-                weights = jnp.exp(scores - new_top)
-                total = total * factor + jnp.sum(weights, axis=0, keepdims=True)
-                accum = accum * factor + dot_nn(vt_ref[:, keys], weights.astype(jnp.bfloat16))
-                return new_top, total, accum
-
-            state = (
-                jnp.full((1, STEP), -1e30, jnp.float32),
-                jnp.zeros((1, STEP), jnp.float32),
-                jnp.zeros((64, STEP), jnp.float32),
-            )
-            state = update(state, at, True)
-            state = lax.fori_loop(0, at, lambda place, held: update(held, place, False), state)
+    def one_block(at):
+        asks = pl.ds(at * STEP, STEP)
+        query = q_ref[asks, :]
+
+        def update(state, place, masked):
             top, total, accum = state
-            result = accum / total
-            wide_ref[:, asks] = result
-            lse_ref[:, asks] = top + jnp.log(total)
-            full = jnp.concatenate([result, jnp.zeros_like(result)], axis=0)
-            out_ref[asks, :] = full.T.astype(jnp.bfloat16)
-            return carry
-
-        lax.fori_loop(0, blocks, one_block, 0)
+            keys = pl.ds(pl.multiple_of(place * STEP, STEP), STEP)
+            scores = dot_nt(k_ref[keys, :], query)
+            if masked:
+                scores = jnp.where(causal(scores), scores, -1e30)
+            new_top = jnp.maximum(top, jnp.max(scores, axis=0, keepdims=True))
+            factor = jnp.exp(top - new_top)
+            weights = jnp.exp(scores - new_top)
+            total = total * factor + jnp.sum(weights, axis=0, keepdims=True)
+            accum = accum * factor + dot_nn(vt_ref[:, keys], weights.astype(jnp.bfloat16))
+            return new_top, total, accum
+
+        state = (
+            jnp.full((1, STEP), -1e30, jnp.float32),
+            jnp.zeros((1, STEP), jnp.float32),
+            jnp.zeros((64, STEP), jnp.float32),
+        )
+        state = update(state, at, True)
+        state = lax.fori_loop(0, at, lambda place, held: update(held, place, False), state)
+        top, total, accum = state
+        result = accum / total
+        wide_ref[:, asks] = result
+        lse_ref[:, asks] = top + jnp.log(total)
+        full = jnp.concatenate([result, jnp.zeros_like(result)], axis=0)
+        out_ref[asks, :] = full.T.astype(jnp.bfloat16)
+
+    for at in range(blocks):
+        pl.when(has)(functools.partial(one_block, at))
+        if at >= 3:
+            next(steps, None)
+    for _ in steps:
+        pass
+    sender.finish()
 
 
 def attend_backward(
@@ -360,27 +374,41 @@
     sender.finish()
 
 
-def run_forward(rows):
+def run_forward(rows, weights, collective):
     length = rows.shape[0]
-    return pl.pallas_call(
+    inside = pl.BlockSpec(memory_space=pltpu.VMEM)
+    outside = pl.BlockSpec(memory_space=pl.ANY)
+    results = pl.pallas_call(
         attend_forward,
-        out_shape=(
+        out_shape=[
             jax.ShapeDtypeStruct((length, 128), jnp.bfloat16),
             jax.ShapeDtypeStruct((64, length), jnp.float32),
             jax.ShapeDtypeStruct((1, length), jnp.float32),
-        ),
+        ]
+        + [jax.ShapeDtypeStruct((4,) + weight.shape, weight.dtype) for weight in weights],
+        in_specs=[inside] + [outside] * 3,
+        out_specs=[inside] * 3 + [outside] * 3,
         scratch_shapes=[
             pltpu.VMEM((length, 64), jnp.bfloat16),
             pltpu.VMEM((length, 64), jnp.bfloat16),
             pltpu.VMEM((64, length), jnp.bfloat16),
+        ]
+        + [pltpu.VMEM(weight.shape, weight.dtype) for weight in weights]
+        + [
+            pltpu.SemaphoreType.DMA((6,)),
+            pltpu.SemaphoreType.DMA((3 * GATHER_COPIES,)),
+            pltpu.SemaphoreType.DMA((3 * GATHER_COPIES,)),
         ],
-        compiler_params=pltpu.CompilerParams(vmem_limit_bytes=40 << 20),
+        compiler_params=pltpu.CompilerParams(
+            collective_id=collective, has_side_effects=True, vmem_limit_bytes=56 << 20
+        ),
         cost_estimate=pl.CostEstimate(
             flops=2 * length * length * 64,
             bytes_accessed=length * 512 * 2,
             transcendentals=length * length // 2,
         ),
-    )(rows)
+    )(rows, *weights)
+    return results[0:3], results[3:6]
 
 
 def run_backward(rows, grads, wide, lse, fc, down, collective):
@@ -419,19 +447,6 @@
     return results[0], results[1:3], results[3:5]
 
 
-def pack_heads(*parts):
-    rows = parts[0].shape[0]
-    turned = [part.reshape(rows, HEADS, HEAD_DIM) for part in parts]
-    if len(parts) % 2:
-        turned.append(jnp.zeros((rows, HEADS, HEAD_DIM), parts[0].dtype))
-    return jnp.transpose(jnp.concatenate(turned, axis=2), (1, 0, 2))
-
-
-def unpack_heads(packed, at):
-    part = packed[:, :, at * HEAD_DIM : (at + 1) * HEAD_DIM]
-    return jnp.transpose(part, (1, 0, 2)).reshape(part.shape[1], HEADS * HEAD_DIM)
-
-
 UNITS = 17
 TAIL = 896
 SHAPES = ((16, 4352), (16, 4352), (64, 1088))
@@ -532,44 +547,36 @@
         return copy
 
 
-GATHER_COPIES = 4 * 35 + 3
-
-
-def gather_kernel(*refs):
-    sources, small = refs[0:4], refs[4]
-    targets, small_out = refs[5:9], refs[9]
-    holds, small_hold = refs[10:14], refs[14]
-    own_sem, send_sem, recv_sem = refs[15:18]
+GATHER_COPIES = 35
+
+
+def gather_peers():
+    return ring_peers() + [near_peer(), cross_peer(), twin_peer()]
+
+
+def gather_steps(sources, targets, holds, mover, sender):
     z, x, y_low, y_high, core = places()
     mine = y_high * 2 + core
     cross = (1 - y_high) * 2 + core
-    mover = Mover(own_sem)
-    loads = [mover.move(sources[at], holds[at]) for at in range(4)]
-    loads.append(mover.move(small, small_hold))
-    greet(ring_peers() + [near_peer(), cross_peer(), far_peer(), twin_peer(), far_twin()])
-    sender = Sender(send_sem, recv_sem)
+    count = len(sources)
     firsts = (2 * z + y_low, 8 + 2 * x + y_low, 16)
     others = (2 * z + 1 - y_low, 8 + 2 * x + 1 - y_low)
-    arrivals = [
-        sender.push(small, small_out.at[mine], twin_peer()),
-        sender.push(small, small_out.at[mine], far_peer()),
-        sender.push(small, small_out.at[mine], far_twin()),
-    ]
     crossed = [
         [
             sender.push(sources[at].at[unit], targets[at].at[mine, unit], cross_peer())
             for unit in others + (16,)
         ]
-        for at in range(4)
+        for at in range(count)
     ]
-    for at in range(4):
-        arrivals.append(sender.push(sources[at], targets[at].at[mine], twin_peer()))
+    loads = [mover.move(sources[at], holds[at]) for at in range(count)]
+    arrivals = [
+        sender.push(sources[at], targets[at].at[mine], twin_peer()) for at in range(count)
+    ]
+    yield
     owns = []
-    for at in range(4):
+    for at in range(count):
         loads[at].wait()
         owns.append(mover.move(holds[at], targets[at].at[mine]))
-    loads[4].wait()
-    owns.append(mover.move(small_hold, small_out.at[mine]))
 
     def ring(at, part, unit, kept):
         piece = targets[at].at[cross, unit]
@@ -587,7 +594,7 @@
             arrivals.append(sender.push(piece, piece, twin_peer()))
 
     waiting = None
-    for at in range(4):
+    for at in range(count):
         nears = []
         for part in range(3):
             crossed[at][part].wait_recv()
@@ -596,12 +603,13 @@
                 nears.append(sender.push(piece, piece, near_peer()))
                 ring(at, part, firsts[part], first_ring)
             arrivals.append(sender.push(piece, piece, twin_peer()))
+        yield
         if waiting is not None:
             second(*waiting)
         waiting = (at, nears)
     second(*waiting)
-
-    for at in range(4):
+    yield
+    for at in range(count):
         for kept, base in ((first_ring, y_low), (second_ring, 1 - y_low)):
             for where, part, step, copy in kept:
                 if where != at:
@@ -617,28 +625,88 @@
         copy.wait_recv()
     for own in owns:
         own.wait()
+
+
+def gather_kernel(source, small, target, small_out, hold, small_hold, own_sem, send_sem, recv_sem):
+    z, x, y_low, y_high, core = places()
+    mine = y_high * 2 + core
+    mover = Mover(own_sem)
+    load = mover.move(small, small_hold)
+    greet(gather_peers() + [far_peer(), far_twin()])
+    sender = Sender(send_sem, recv_sem)
+    arrivals = [
+        sender.push(small, small_out.at[mine], twin_peer()),
+        sender.push(small, small_out.at[mine], far_peer()),
+        sender.push(small, small_out.at[mine], far_twin()),
+    ]
+    load.wait()
+    own = mover.move(small_hold, small_out.at[mine])
+    for _ in gather_steps([source], [target], [hold], mover, sender):
+        pass
+    for copy in arrivals:
+        copy.wait_recv()
+    own.wait()
     sender.finish()
 
 
-def gather_weights(parts, small, collective):
-    whole = list(parts) + [small]
-    shapes = [jax.ShapeDtypeStruct((4,) + part.shape, part.dtype) for part in whole]
+def gather_weights(part, small, collective):
+    whole = [part, small]
+    shapes = [jax.ShapeDtypeStruct((4,) + each.shape, each.dtype) for each in whole]
     return pl.pallas_call(
         gather_kernel,
         out_shape=shapes,
-        in_specs=[pl.BlockSpec(memory_space=pl.ANY)] * 5,
-        out_specs=[pl.BlockSpec(memory_space=pl.ANY)] * 5,
-        scratch_shapes=[pltpu.VMEM(part.shape, part.dtype) for part in whole]
+        in_specs=[pl.BlockSpec(memory_space=pl.ANY)] * 2,
+        out_specs=[pl.BlockSpec(memory_space=pl.ANY)] * 2,
+        scratch_shapes=[pltpu.VMEM(each.shape, each.dtype) for each in whole]
         + [
-            pltpu.SemaphoreType.DMA((10,)),
-            pltpu.SemaphoreType.DMA((GATHER_COPIES,)),
-            pltpu.SemaphoreType.DMA((GATHER_COPIES,)),
+            pltpu.SemaphoreType.DMA((4,)),
+            pltpu.SemaphoreType.DMA((GATHER_COPIES + 3,)),
+            pltpu.SemaphoreType.DMA((GATHER_COPIES + 3,)),
         ],
         compiler_params=pltpu.CompilerParams(
-            collective_id=collective, has_side_effects=True, vmem_limit_bytes=24 << 20
+            collective_id=collective, has_side_effects=True, vmem_limit_bytes=58 << 20
         ),
-        cost_estimate=pl.CostEstimate(flops=0, bytes_accessed=60 << 20, transcendentals=0),
+        cost_estimate=pl.CostEstimate(flops=0, bytes_accessed=20 << 20, transcendentals=0),
     )(*whole)
+
+
+def product_kernel(cut, *refs):
+    out = refs[-1]
+    products = []
+    for at in range(0, len(refs) - 1, 4):
+        left = jnp.concatenate([refs[at][...], refs[at + 1][...]], axis=1)
+        right = jnp.concatenate([refs[at + 2][...], refs[at + 3][...]], axis=0)
+        products.append((left, right))
+    if cut is None:
+        out[...] = dot_nn(*products[0]).astype(jnp.bfloat16)
+        return
+    (left, right), (other_left, other_right) = products
+    out[:, 0:cut] = dot_nn(left, right[:, 0:cut]).astype(jnp.bfloat16)
+    shared = dot_nn(left, right[:, cut : cut + 128]) + dot_nn(other_left, other_right[:, 0:128])
+    out[:, cut : cut + 128] = shared.astype(jnp.bfloat16)
+    out[:, cut + 128 :] = dot_nn(other_left, other_right[:, 128:]).astype(jnp.bfloat16)
+
+
+def weight_products(operands, width, cut=None):
+    size = operands[0][0].shape[0]
+    block = 272
+    specs, flat = [], []
+    for left, other_left, right, other_right in operands:
+        specs += [pl.BlockSpec((block, left.shape[1]), lambda step: (step, 0))] * 2
+        specs += [pl.BlockSpec(right.shape, lambda step: (0, 0))] * 2
+        flat += [left, other_left, right, other_right]
+    terms = pl.pallas_call(
+        functools.partial(product_kernel, cut),
+        grid=(size // block,),
+        out_shape=jax.ShapeDtypeStruct((size, width), jnp.bfloat16),
+        in_specs=specs,
+        out_specs=pl.BlockSpec((block, width), lambda step: (step, 0)),
+        compiler_params=pltpu.CompilerParams(vmem_limit_bytes=40 << 20),
+        cost_estimate=pl.CostEstimate(
+            flops=512 * size * width, bytes_accessed=2 * size * width, transcendentals=0
+        ),
+    )(*flat)
+    return terms.reshape(2, UNITS, size // (2 * UNITS), width)
 
 
 def push_rings(sender, terms, by_z, by_x):
@@ -901,18 +969,235 @@
     return outs, small.reshape(-1)[:3264].astype(jnp.float32)
 
 
-def norm_rows(values, gain_vec, offset):
-    centre = values - jnp.mean(values, axis=-1, keepdims=True)
-    spread = jnp.mean(centre * centre, axis=-1, keepdims=True)
-    return centre * lax.rsqrt(spread + 1e-05) * gain_vec + offset
-
-
-def gelu_tanh(values):
-    return (
-        0.5
-        * values
-        * (1.0 + jnp.tanh(0.7978845608028654 * (values + 0.044715 * values * values * values)))
-    )
+def mean_rows(values):
+    return jnp.sum(values, axis=-1, keepdims=True) * (1.0 / values.shape[-1])
+
+
+def normal_rows(values):
+    centre = values - mean_rows(values)
+    scale = lax.rsqrt(mean_rows(centre * centre) + 1e-05)
+    return centre * scale, scale
+
+
+def norm_back(grads, gain, unit, scale):
+    scaled = grads * gain
+    return scale * (scaled - mean_rows(scaled) - unit * mean_rows(scaled * unit))
+
+
+def column_sums(values):
+    return jnp.sum(values, axis=0, keepdims=True)
+
+
+def turned(values):
+    rows, width = values.shape
+    full = jnp.concatenate([values, jnp.zeros((rows, 1152 - width), values.dtype)], axis=1)
+    return full.T[0:width, :]
+
+
+def before_kernel(tokens, gain, offset, weight, bias, packed, turned_ref, joint):
+    unit, _ = normal_rows(widen(tokens[...]))
+    normed = (unit * widen(gain[...]) + widen(offset[...])).astype(jnp.bfloat16)
+    turned_ref[...] = turned(normed)
+    joint[...] = (dot_nn(normed, weight[...]) + widen(bias[...])).astype(jnp.bfloat16)
+    blank = jnp.zeros((joint.shape[0], HEAD_DIM), jnp.bfloat16)
+    for head in range(HEADS):
+        parts = [
+            joint[:, 1088 * part + 64 * head : 1088 * part + 64 * head + 64] for part in range(3)
+        ]
+        packed[head] = jnp.concatenate(parts + [blank], axis=1)
+
+
+def run_before(tokens, gain, offset, weight, bias):
+    rows = tokens.shape[0]
+    return pl.pallas_call(
+        before_kernel,
+        out_shape=(
+            jax.ShapeDtypeStruct((HEADS, rows, 256), jnp.bfloat16),
+            jax.ShapeDtypeStruct((1088, rows), jnp.bfloat16),
+        ),
+        scratch_shapes=[pltpu.VMEM((rows, 3264), jnp.bfloat16)],
+        compiler_params=pltpu.CompilerParams(vmem_limit_bytes=40 << 20),
+        cost_estimate=pl.CostEstimate(
+            flops=2 * rows * 1088 * 3264, bytes_accessed=8 << 20, transcendentals=0
+        ),
+    )(tokens, gain, offset, weight, bias)
+
+
+def middle_kernel(
+    heads,
+    tokens,
+    cotangent,
+    w_out,
+    b_out,
+    gain,
+    offset,
+    b_down,
+    fc,
+    b_fc,
+    down,
+    result,
+    grad_middle,
+    grad_heads,
+    attended_t,
+    normed_t,
+    grad_branch,
+    active_t,
+    grad_hidden,
+    d_fc,
+    sums,
+    attended,
+    normed,
+    unit,
+    scale,
+    total,
+    grads,
+):
+    at = pl.program_id(0)
+
+    @pl.when(at == 0)
+    def _():
+        for head in range(HEADS):
+            attended[:, 64 * head : 64 * head + 64] = heads[head, :, 0:64]
+        attended_t[...] = turned(attended[...])
+        middle = widen(tokens[...]) + (dot_nn(attended[...], w_out[...]) + widen(b_out[...]))
+        unit[...], scale[...] = normal_rows(middle)
+        normed[...] = (unit[...] * widen(gain[...]) + widen(offset[...])).astype(jnp.bfloat16)
+        normed_t[...] = turned(normed[...])
+        total[...] = middle + widen(b_down[...])
+        grads[...] = jnp.zeros_like(grads)
+
+    hidden = dot_nn(normed[...], fc[...]) + widen(b_fc[...])
+    square = hidden * hidden
+    bend = jnp.tanh(0.7978845608028654 * (hidden + 0.044715 * square * hidden))
+    active = (0.5 * hidden * (1.0 + bend)).astype(jnp.bfloat16)
+    slope = 0.5 * (1.0 + bend) + 0.5 * hidden * (1.0 - bend * bend) * (
+        0.7978845608028654 * (1.0 + 3.0 * 0.044715 * square)
+    )
+    back = (dot_nt(cotangent[...], down[...]) * slope).astype(jnp.bfloat16)
+    active_t[...] = active.T
+    grad_hidden[...] = back
+    d_fc[...] = column_sums(widen(back))
+    total[...] += dot_nn(active, down[...])
+    grads[...] += dot_nt(back, fc[...])
+
+    @pl.when(at == pl.num_programs(0) - 1)
+    def _():
+        result[...] = total[...].astype(jnp.bfloat16)
+        arrived = widen(cotangent[...])
+        whole = grads[...]
+        grad = arrived + norm_back(whole, widen(gain[...]), unit[...], scale[...])
+        grad_middle[...] = grad
+        low = grad.astype(jnp.bfloat16)
+        grad_branch[:, 0:64] = jnp.zeros((low.shape[0], 64), jnp.bfloat16)
+        grad_branch[:, 64:1152] = low
+        sums[0:1, :] = column_sums(widen(low))
+        sums[1:2, :] = column_sums(whole * unit[...])
+        sums[2:3, :] = column_sums(whole)
+        sums[3:4, :] = column_sums(arrived)
+        attended[...] = dot_nt(low, w_out[...]).astype(jnp.bfloat16)
+        blank = jnp.zeros((low.shape[0], HEAD_DIM), jnp.bfloat16)
+        for head in range(HEADS):
+            piece = attended[:, 64 * head : 64 * head + 64]
+            grad_heads[head] = jnp.concatenate([piece, blank], axis=1)
+
+
+def run_middle(heads, tokens, cotangent, w_out, b_out, gain, offset, b_down, fc, b_fc, down):
+    rows = tokens.shape[0]
+    low, wide = jnp.bfloat16, jnp.float32
+    block = 256
+
+    def fixed(shape):
+        return pl.BlockSpec(shape, lambda step: (0,) * len(shape))
+
+    vector = fixed((1, 1088))
+    square = fixed((rows, 1088))
+    across = pl.BlockSpec((rows, block), lambda step: (0, step))
+    line = pl.BlockSpec((1, block), lambda step: (0, step))
+    return pl.pallas_call(
+        middle_kernel,
+        grid=(4352 // block,),
+        in_specs=[
+            fixed((HEADS, rows, 128)),
+            square,
+            square,
+            fixed((1088, 1088)),
+            vector,
+            vector,
+            vector,
+            vector,
+            pl.BlockSpec((1088, block), lambda step: (0, step)),
+            line,
+            pl.BlockSpec((block, 1088), lambda step: (step, 0)),
+        ],
+        out_specs=[
+            square,
+            square,
+            fixed((HEADS, rows, 128)),
+            fixed((1088, rows)),
+            fixed((1088, rows)),
+            fixed((rows, 1152)),
+            pl.BlockSpec((block, rows), lambda step: (step, 0)),
+            across,
+            line,
+            fixed((4, 1088)),
+        ],
+        out_shape=[
+            jax.ShapeDtypeStruct((rows, 1088), low),
+            jax.ShapeDtypeStruct((rows, 1088), wide),
+            jax.ShapeDtypeStruct((HEADS, rows, 128), low),
+            jax.ShapeDtypeStruct((1088, rows), low),
+            jax.ShapeDtypeStruct((1088, rows), low),
+            jax.ShapeDtypeStruct((rows, 1152), low),
+            jax.ShapeDtypeStruct((4352, rows), low),
+            jax.ShapeDtypeStruct((rows, 4352), low),
+            jax.ShapeDtypeStruct((1, 4352), wide),
+            jax.ShapeDtypeStruct((4, 1088), wide),
+        ],
+        scratch_shapes=[
+            pltpu.VMEM((rows, 1088), low),
+            pltpu.VMEM((rows, 1088), low),
+            pltpu.VMEM((rows, 1088), wide),
+            pltpu.VMEM((rows, 1), wide),
+            pltpu.VMEM((rows, 1088), wide),
+            pltpu.VMEM((rows, 1088), wide),
+        ],
+        compiler_params=pltpu.CompilerParams(vmem_limit_bytes=48 << 20),
+        cost_estimate=pl.CostEstimate(
+            flops=8 * rows * 1088 * 4352, bytes_accessed=24 << 20, transcendentals=rows * 4352
+        ),
+    )(heads, tokens, cotangent, w_out, b_out, gain, offset, b_down, fc, b_fc, down)
+
+
+def after_kernel(packed, weight, tokens, gain, grad_middle, joint, grad_tokens, sums, line):
+    for head in range(HEADS):
+        for part in range(3):
+            start = 1088 * part + 64 * head
+            joint[:, start : start + 64] = packed[head, :, 64 * part : 64 * part + 64]
+    joint[:, 3264:3328] = jnp.zeros((joint.shape[0], 64), jnp.bfloat16)
+    unit, scale = normal_rows(widen(tokens[...]))
+    grads = dot_nt(joint[:, 0:3264], weight[...])
+    back = norm_back(grads, widen(gain[...]), unit, scale)
+    grad_tokens[...] = grad_middle[...] + back
+    sums[0:1, :] = column_sums(grads * unit)
+    sums[1:2, :] = column_sums(grads)
+    line[...] = column_sums(widen(joint[:, 0:3264]))
+
+
+def run_after(packed, weight, tokens, gain, grad_middle):
+    rows = tokens.shape[0]
+    return pl.pallas_call(
+        after_kernel,
+        out_shape=(
+            jax.ShapeDtypeStruct((rows, 3328), jnp.bfloat16),
+            jax.ShapeDtypeStruct((rows, 1088), jnp.float32),
+            jax.ShapeDtypeStruct((2, 1088), jnp.float32),
+            jax.ShapeDtypeStruct((1, 3264), jnp.float32),
+        ),
+        compiler_params=pltpu.CompilerParams(vmem_limit_bytes=40 << 20),
+        cost_estimate=pl.CostEstimate(
+            flops=2 * rows * 1088 * 3264, bytes_accessed=10 << 20, transcendentals=0
+        ),
+    )(packed, weight, tokens, gain, grad_middle)
 
 
 def local(
@@ -933,7 +1218,6 @@
     bias_down,
 ):
     ctx_count = lax.axis_size("ctx")
-    model_width = tokens.shape[2]
     vectors = (
         ln1_scale,
         ln1_bias,
@@ -945,122 +1229,92 @@
         bias_down,
         bias_fc,
     )
-    small = jnp.pad(jnp.concatenate(vectors), (0, 4096 - 3264)).reshape(16, 256)
+    small = jnp.concatenate(
+        [jnp.stack(vectors[:8]), bias_fc.reshape(4, 272), jnp.zeros((4, 272), jnp.bfloat16)]
+    )
     own_parts = [
         part.reshape(UNITS, part.shape[0] // UNITS, part.shape[1])
         for part in (w_qkv, w_out, w_fc, w_down)
     ]
-    full_qkv, full_out, full_fc, full_down, full_small = gather_weights(own_parts, small, 5)
+    full_qkv, full_small = gather_weights(own_parts[0], small, 5)
     full_qkv = full_qkv.reshape(1088, 3264)
+    lines = [full_small[:, at].reshape(1, 1088) for at in range(8)]
+    (line_scale1, line_shift1, line_bq, line_bv, line_bout, line_scale2, line_shift2) = lines[:7]
+    line_bdown = lines[7]
+    line_bfc = full_small[:, 8:12].reshape(1, 4352)
+    z, x, y_low, y_high, core = places()
+
+    def swap(values):
+        return lax.ppermute(values, "fsdp", [(0, 1), (1, 0), (2, 3), (3, 2)])
+
+    def split(quarters):
+        first, second = quarters[:, 0], quarters[:, 1]
+        keep = jnp.where(core == 0, first, second)
+        give = jnp.where(core == 0, second, first)
+        keep = jnp.where(y_high == 0, keep, keep[::-1])
+        give = jnp.where(y_high == 0, give, give[::-1])
+        return keep, give
+
+    def products(left, right):
+        width, rows = left.shape
+        keep, give = split(left.reshape(2, 2, width // 4, rows))
+        keep, give = keep.reshape(width // 2, rows), give.reshape(width // 2, rows)
+        return keep, swap(give), right, swap(right)
+
+    bias_joint = jnp.concatenate([line_bq, jnp.zeros_like(line_bq), line_bv], axis=1)
+    packed, normed_t = run_before(tokens[0], line_scale1, line_shift1, full_qkv, bias_joint)
+    head_rows = spread_heads(packed, ctx_count, 1)
+    (out_rows, wide_out, lse_rows), (full_out, full_fc, full_down) = run_forward(
+        head_rows, own_parts[1:], 8
+    )
     full_out = full_out.reshape(1088, 1088)
     full_fc = full_fc.reshape(1088, 4352)
     full_down = full_down.reshape(4352, 1088)
-    full_small = full_small.reshape(4, 4096)
-    (g_scale1, g_shift1, full_bq, full_bv, full_bout, g_scale2, g_shift2, full_bdown) = [
-        full_small[:, at * 272 : (at + 1) * 272].reshape(1088) for at in range(8)
-    ]
-    full_bfc = full_small[:, 2176:3264].reshape(4352)
-    z, x, y_low, y_high, core = places()
-
-    def swap(values):
-        return lax.ppermute(values, "fsdp", [(0, 1), (1, 0), (2, 3), (3, 2)])
-
-    def split(values):
-        quarters = values.reshape(values.shape[0], 2, 2, -1)
-        first, second = quarters[:, :, 0], quarters[:, :, 1]
-        keep = jnp.where(core == 0, first, second)
-        give = jnp.where(core == 0, second, first)
-        keep = jnp.where(y_high == 0, keep, keep[:, ::-1])
-        give = jnp.where(y_high == 0, give, give[:, ::-1])
-        return keep.reshape(values.shape[0], -1), give.reshape(values.shape[0], -1)
-
-    def left_rows(values):
-        keep, give = split(values)
-        return jnp.concatenate([keep, swap(give)], axis=0)
-
-    def right_rows(values):
-        return jnp.concatenate([values, swap(values)], axis=0)
-
-    def weight_terms(left, right):
-        terms = lax.dot_general(
-            left_rows(left),
-            right_rows(right),
-            (((0,), (0,)), ((), ())),
-            preferred_element_type=jnp.float32,
-        ).astype(jnp.bfloat16)
-        return terms.reshape(2, UNITS, terms.shape[0] // (2 * UNITS), terms.shape[1])
-
-    scale_one = g_scale1.astype(jnp.float32)
-    shift_one = g_shift1.astype(jnp.float32)
-    scale_two = g_scale2.astype(jnp.float32)
-    shift_two = g_shift2.astype(jnp.float32)
-    inputs32 = tokens[0].astype(jnp.float32)
-    norm_one, norm_one_pull = jax.vjp(norm_rows, inputs32, scale_one, shift_one)
-    normed = norm_one.astype(jnp.bfloat16)
-    joint_rows = jnp.dot(normed, full_qkv, preferred_element_type=jnp.float32)
-    queries = (joint_rows[:, :model_width] + full_bq.astype(jnp.float32)).astype(jnp.bfloat16)
-    key_rows = joint_rows[:, model_width : 2 * model_width].astype(jnp.bfloat16)
-    value_rows = (joint_rows[:, 2 * model_width :] + full_bv.astype(jnp.float32)).astype(
-        jnp.bfloat16
-    )
-    head_rows = spread_heads(pack_heads(queries, key_rows, value_rows), ctx_count, 1)
-    out_rows, wide_out, lse_rows = run_forward(head_rows)
-    attended = unpack_heads(collect_heads(out_rows, ctx_count, 2), 0)
-    branch = jnp.dot(attended, full_out, preferred_element_type=jnp.float32) + full_bout.astype(
-        jnp.float32
-    )
-    middle = inputs32 + branch
-    norm_two, norm_two_pull = jax.vjp(norm_rows, middle, scale_two, shift_two)
-    normed2 = norm_two.astype(jnp.bfloat16)
-    hidden_pre = jnp.dot(normed2, full_fc, preferred_element_type=jnp.float32) + full_bfc.astype(
-        jnp.float32
-    )
-    gelu_value, gelu_pull = jax.vjp(gelu_tanh, hidden_pre)
-    active = gelu_value.astype(jnp.bfloat16)
-    out_branch = jnp.dot(active, full_down, preferred_element_type=jnp.float32) + full_bdown.astype(
-        jnp.float32
-    )
-    result = (middle + out_branch).astype(jnp.bfloat16)
-    upstream = cotangent[0].astype(jnp.float32)
-    grad_branch2 = cotangent[0]
-    d_down = weight_terms(active, grad_branch2)
-    d_bdown = jnp.sum(upstream, axis=0)
-    grad_active = jnp.einsum(
-        "td,fd->tf", grad_branch2, full_down, preferred_element_type=jnp.float32
-    )
-    grad_hidden = gelu_pull(grad_active)[0].astype(jnp.bfloat16)
-    d_fc = weight_terms(normed2, grad_hidden)
-    d_bfc = jnp.sum(grad_hidden.astype(jnp.float32), axis=0)
-    grad_normed2 = jnp.einsum("tf,df->td", grad_hidden, full_fc, preferred_element_type=jnp.float32)
-    grad_mid_part, d_scale2, d_shift2 = norm_two_pull(grad_normed2)
-    grad_middle = upstream + grad_mid_part
-    grad_branch = grad_middle.astype(jnp.bfloat16)
-    d_out = weight_terms(attended, grad_branch)
-    d_bout = jnp.sum(grad_branch.astype(jnp.float32), axis=0)
-    grad_attended = jnp.einsum(
-        "te,de->td", grad_branch, full_out, preferred_element_type=jnp.float32
-    ).astype(jnp.bfloat16)
-    grad_rows = spread_heads(pack_heads(grad_attended, jnp.zeros_like(grad_attended)), ctx_count, 3)
+    (
+        result,
+        grad_middle,
+        grad_heads,
+        attended_t,
+        normed2_t,
+        grad_branch,
+        active_t,
+        grad_hidden,
+        line_fc,
+        sums_middle,
+    ) = run_middle(
+        collect_heads(out_rows, ctx_count, 2),
+        tokens[0],
+        cotangent[0],
+        full_out,
+        line_bout,
+        line_scale2,
+        line_shift2,
+        line_bdown,
+        full_fc,
+        line_bfc,
+        full_down,
+    )
+    d_down = weight_products([products(active_t, cotangent[0])], 1088)
+    d_fc = weight_products([products(normed2_t, grad_hidden)], 4352)
+    out_products = products(attended_t, grad_branch)
+    grad_rows = spread_heads(grad_heads, ctx_count, 3)
     joint_rows_grad, far_z, far_x = run_backward(
         head_rows, grad_rows, wide_out, lse_rows, d_fc, d_down, 7
     )
     packed_grads = collect_heads(joint_rows_grad, ctx_count, 4)
-    grad_q16 = unpack_heads(packed_grads, 0)
-    grad_k16 = unpack_heads(packed_grads, 1)
-    grad_v16 = unpack_heads(packed_grads, 2)
-    grad_joint = jnp.concatenate([grad_q16, grad_k16, grad_v16], axis=1)
-    d_qkv = weight_terms(normed, grad_joint)
-    d_bq = jnp.sum(grad_q16.astype(jnp.float32), axis=0)
-    d_bv = jnp.sum(grad_v16.astype(jnp.float32), axis=0)
-    grad_normed = jnp.einsum("te,de->td", grad_joint, full_qkv, preferred_element_type=jnp.float32)
-    grad_in_part, d_scale1, d_shift1 = norm_one_pull(grad_normed)
-    grad_inputs = grad_middle + grad_in_part
+    grad_joint, grad_inputs, sums_after, line_joint = run_after(
+        packed_grads, full_qkv, tokens[0], line_scale1, grad_middle
+    )
+    d_joint = weight_products([products(normed_t, grad_joint), out_products], 4352, 3200)
+    d_bout, d_scale2, d_shift2, d_bdown = [sums_middle[at] for at in range(4)]
+    d_scale1, d_shift1 = sums_after[0], sums_after[1]
+    d_bq, d_bv, d_bfc = line_joint[0, :1088], line_joint[0, 2176:], line_fc[0]
     narrow = (d_scale1, d_shift1, d_bq, d_bv, d_bout, d_scale2, d_shift2, d_bdown, d_bfc)
     sums = jnp.concatenate([vector.reshape(4, -1) for vector in narrow], axis=1)
-    keep, give = split(sums.reshape(1, -1))
-    sums = (keep + swap(give)).reshape(2, 3264)
+    keep, give = split(sums.reshape(2, 2, 3264))
+    sums = keep + swap(give)
     (t_qkv, t_out, t_fc, t_down), extras = reduce_grads(
-        (jnp.concatenate([d_qkv, d_out], axis=-1), d_fc, d_down), sums, far_z, far_x, 6
+        (d_joint, d_fc, d_down), sums, far_z, far_x, 6
     )
     (t_scale1, t_shift1, t_bq, t_bv, t_bout, t_scale2, t_shift2, t_bdown) = [
         extras[at * 272 : (at + 1) * 272] for at in range(8)

time: 533 us -> 462 us (0.87); the launches traced: 525 us -> 460 us
  matrix products: 61.3 us -> 0 us
  Pallas kernels: 347 us -> 381 us
  local copies, waits for them, and re-layouts: 77.2 us -> 57.3 us
  other arithmetic: 34.9 us -> 18.6 us
    dot_general x12 -> x0, matrix products: 61.3 us -> none  [the longest x4 15.7 us: weight_terms(): lax.dot_general(left_rows(left), right_rows(right), (((0,), (0,)), ((), (...]
    pallas_call x1 -> x7, Pallas kernels: 25.4 us -> 85 us  [the longest x1 47.5 us: run_forward(): pl.pallas_call(attend_forward, out_shape=[jax.ShapeDtypeStruct((length, 1...]
    pallas_call x1, Pallas kernels: 58.1 us -> 27.2 us  [gather_weights(): pl.pallas_call(gather_kernel, out_shape=shapes, in_specs=[pl.BlockSpec(me...]
    convert_element_type x15 -> x0, local copies, waits for them, and re-layouts: 12 us -> none  [the longest x1 8.24 us: weight_terms(): terms = lax.dot_general(left_rows(left), right_rows(right), (((0,), (0,))...]
    transpose x7 -> x0, local copies, waits for them, and re-layouts: 11.7 us -> none  [the longest x6 10.8 us: unpack_heads(): jnp.transpose(part, (1, 0, 2)).reshape(part.shape[1], HEADS * HEAD_DIM)]
    unnamed x101 -> x79, local copies, waits for them, and re-layouts: 23.6 us -> 31.9 us
    another operation x1 -> x16, local copies, waits for them, and re-layouts: 0.01 us -> 6.15 us  [the longest x8 5.46 us: local(): jnp.stack(vectors[:8])]
    reshape x8 -> x2, local copies, waits for them, and re-layouts: 6.55 us -> 0.88 us  [the longest x1 0.77 us: local(): bias_fc.reshape(4, 272)]
  transfers between devices with their start and end apart: 9 -> 9, of which waited for: 0 -> 0; matrix products, arithmetic and copies ran while one was open for 16% -> 7% of each run, Pallas kernels for 19% -> 56%
where the time goes in v4:
time: 462 us; the launch traced here: 460 us
  Pallas kernels  381 us (82%)
  local copies, waits for them, and re-layouts  57.3 us (12%)
  other arithmetic  18.6 us (4%)
    pallas_call x1, Pallas kernels, last_exchange(): pl.pallas_call(last_kernel, out_shape=[jax.ShapeDtypeStruct((UNITS,) + un...  118 us
    pallas_call x1, Pallas kernels, run_backward(): pl.pallas_call(attend_backward, out_shape=[jax.ShapeDtypeStruct((length,...  53.7 us
    pallas_call x2, Pallas kernels, spread_heads(): pl.pallas_call(functools.partial(spread_kernel, count), out_shape=jax.Sha...  50.4 us
    pallas_call x1, Pallas kernels, run_forward(): pl.pallas_call(attend_forward, out_shape=[jax.ShapeDtypeStruct((length, 1...  47.5 us
    pallas_call x2, Pallas kernels, collect_heads(): pl.pallas_call(functools.partial(collect_kernel, count), out_shape=jax.Sh...  46.4 us
    unnamed x79, local copies, waits for them, and re-layouts  31.9 us
    pallas_call x1, Pallas kernels, gather_weights(): pl.pallas_call(gather_kernel, out_shape=shapes, in_specs=[pl.BlockSpec(me...  27.2 us
    pallas_call x1, Pallas kernels, run_middle(): pl.pallas_call(middle_kernel, grid=(4352 // block,), in_specs=[fixed((HEA...  21.8 us
  transfers between devices with their start and end apart: 9, of which 0 were waited for; matrix products, arithmetic and copies ran while one was open for 7% of the time, Pallas kernels for 56%

profile of v4, /device:TPU:8, one launch (start us, length us, event | category | flops | bytes accessed | tf_op | source)
XLA Modules:
  0.0 460.3 jit_solution(9788213835829320454)
XLA Ops:
  9.4 27.2 %shard_map.262 = (bf16[4,17,16,3264]{3,2,1,0:T(8,128)(2,1)}, bf16[4,16,272]{2,1,0:T(8,128)(2,1)}) custom-call(bf16[17,16,3264]{2,1,0:T(8,128)(2,1)} %bitcast.154, bf16[16,272]{1,0:T(8,128)(2,1)} %concatenate.31.small), custom_call_target="tpu_custom_call" | custom-call | bytes 20971520 | tf_op jit(solution)/shard_map/pallas_call | solution.py:655
  39.4 3.1 copy-done
  42.4 1.7 shard_map.263
  45.8 30.5 %shard_map.264.refs_0_.x_ref = bf16[4096,256]{1,0:T(8,128)(2,1)} custom-call(bf16[17,128,256]{2,1,0:T(8,128)(2,1)} %copy-done.14), custom_call_target="tpu_custom_call" | custom-call | bytes 4194304 | tf_op jit(solution)/shard_map/pallas_call | solution.py:173
  76.3 47.5 %shard_map.265 = (bf16[4096,128]{1,0:T(8,128)(2,1)}, f32[64,4096]{1,0:T(8,128)}, f32[1,4096]{1,0:T(1,128)}, bf16[4,17,16,1088]{3,2,1,0:T(8,128)(2,1)}, bf16[4,17...) custom-call(bf16[4096,256]{1,0:T(8,128)(2,1)} %shard_map.264.refs_0_.x_ref, bf16[17,16,1088]{2,1,0:T(8,128)(2,1)} %bitcast.163, ...), custom_call_target="tpu_custom_call" | custom-call | flops 2147483648 | bytes 4194304 | tf_op jit(solution)/shard_map/pallas_call | solution.py:381
  123.8 18.3 %shard_map.266.heads = bf16[17,128,128]{2,1,0:T(8,128)(2,1)} custom-call(bf16[4096,128]{1,0:T(8,128)(2,1)} %get-tuple-element.51.y_ref), custom_call_target="tpu_custom_call" | custom-call | bytes 4194304 | tf_op jit(solution)/shard_map/pallas_call | solution.py:190
  143.7 21.8 %shard_map.267 = (bf16[128,1088]{1,0:T(8,128)(2,1)S(1)}, f32[128,1088]{1,0:T(8,128)S(1)}, bf16[17,128,128]{2,1,0:T(8,128)(2,1)S(1)}, bf16[1088,128]{1,0:T(8,128)...) custom-call(bf16[17,128,128]{2,1,0:T(8,128)(2,1)S(1)} %copy-done.6, ...), custom_call_target="tpu_custom_call" | custom-call | flops 4848615424 | bytes 25165824 | tf_op jit(solution)/shard_map/pallas_call | solution.py:1116
  171.9 19.9 %shard_map.268.g_ref = bf16[4096,128]{1,0:T(8,128)(2,1)} custom-call(bf16[17,128,128]{2,1,0:T(8,128)(2,1)} %copy-done.19), custom_call_target="tpu_custom_call" | custom-call | bytes 4194304 | tf_op jit(solution)/shard_map/pallas_call | solution.py:173
  198.0 1.8 copy.62
  202.0 5.5 %shard_map.270 = bf16[2176,1088]{1,0:T(8,128)(2,1)S(1)} custom-call(bf16[2176,128]{1,0:T(8,128)(2,1)S(1)} %bitcast.138, bf16[2176,128]{1,0:T(8,128)(2,1)} %collective-permute-done.2.refs_1_, bf16[128,1088]{1,0:T(8,128)(2,1)S(1)} %bitcast.137, bf16[128,1088]{1,0:T(8,128)(2,1)} %collective-permute-done.3.refs_3_), custom_call_target="tpu_custom_call" | custom-call | flops 1212153856 | bytes 4734976 | tf_op jit(solution)/shard_map/pallas_call | solution.py:698
  207.5 2.3 copy-done.2
  211.0 2.7 shard_map.269
  215.9 53.7 %shard_map.271 = (bf16[4096,256]{1,0:T(8,128)(2,1)S(1)}, bf16[3,2,2,16,4352]{4,3,2,1,0:T(8,128)(2,1)S(1)}, bf16[3,2,2,64,1088]{4,3,2,1,0:T(8,128)(2,1)S(1)}, bf1...) custom-call(bf16[4096,256]{1,0:T(8,128)(2,1)S(1)} %copy-done.7, bf16[4096,128]{1,0:T(8,128)(2,1)S(1)} %copy-done.15, ...), custom_call_target="tpu_custom_call" | custom-call | flops 5368709120 | bytes 6291456 | tf_op jit(solution)/shard_map/pallas_call | solution.py:422
  274.6 28.1 %shard_map.272.packed = bf16[17,128,256]{2,1,0:T(8,128)(2,1)} custom-call(bf16[4096,256]{1,0:T(8,128)(2,1)} %copy-done.8), custom_call_target="tpu_custom_call" | custom-call | bytes 4194304 | tf_op jit(solution)/shard_map/pallas_call | solution.py:190
  302.7 3.0 copy-done.1
  307.0 2.8 shard_map.273
  314.0 2.1 copy.63
  318.1 3.1 shard_map.274
  321.2 2.1 copy-done.4
  329.4 118.1 %shard_map.275 = (bf16[17,16,4352]{2,1,0:T(8,128)(2,1)}, bf16[17,16,4352]{2,1,0:T(8,128)(2,1)}, bf16[17,64,1088]{2,1,0:T(8,128)(2,1)}, bf16[16,1024]{1,0:T(8,128)(2,1)S(1)}) custom-call(bf16[2,17,16,4352]{3,2,1,0:T(8,128)(2,1)} %bitcast.130, bf16[2,17,16,4352]{3,2,1,0:T(8,128)(2,1)} %bitcast.128, bf16[2,17,64,1088]{3,2,1,0:T(8,128)(2,1)} %bitcast.125, ...), custom_call_target="tpu_custom_call" | custom-call | bytes 41943040 | tf_op jit(solution)/shard_map/pallas_call | solution.py:938
  447.5 3.7 slice_convert_fusion
  451.2 2.4 slice_convert_fusion.1
  454.8 2.8 bitcast_convert_fusion
  457.6 2.6 bitcast_convert_fusion.1
  (158 shorter events, 52.3 us)
Async XLA Ops:
  0.6 38.4 %copy-start.33 = (bf16[1,128,1088]{1,2,0:T(8,128)(2,1)S(1)}, bf16[1,128,1088]{1,2,0:T(8,128)(2,1)}, u32[]{:S(2)}) copy-start(bf16[1,128,1088]{1,2,0:T(8,128)(2,1)} %param.15) | copy-start | bytes 835588
  1.9 199.6 %collective-permute-start.3 = (bf16[128,1088]{1,0:T(8,128)(2,1)S(1)}, bf16[128,1088]{1,0:T(8,128)(2,1)}, u32[]{:S(2)}, u32[]{:S(2)}) collective-permute-start(bf16[128,1088]{1,0:T(8,128)(2,1)S(1)} %bitcast.135), channel_id=1, source_target_pairs={{0,1},{1,0},{2,3},{3,2},{4,5},{5,4},{6,7},{7,6},{8,9},{9,8},{10,11... | collective-permute-start | bytes 835592 | tf_op jit(solution)/shard_map/ppermute | solution.py:1248
  165.5 4.3 copy-start.22
  165.5 4.3 copy-start.23
  166.5 35.0 %collective-permute-start.2 = (bf16[2176,128]{1,0:T(8,128)(2,1)}, bf16[2176,128]{1,0:T(8,128)(2,1)}, u32[]{:S(2)}, u32[]{:S(2)}) collective-permute-start(bf16[2176,128]{1,0:T(8,128)(2,1)} %bitcast.21), channel_id=1, source_target_pairs={{0,1},{1,0},{2,3},{3,2},{4,5},{5,4},{6,7},{7,6},{8,9},{9,8},{10,11... | collective-permute-start | bytes 1671176 | tf_op jit(solution)/shard_map/ppermute | solution.py:1248
  167.3 43.7 %collective-permute-start = (bf16[544,128]{1,0:T(8,128)(2,1)}, bf16[544,128]{1,0:T(8,128)(2,1)}, u32[]{:S(2)}, u32[]{:S(2)}) collective-permute-start(bf16[544,128]{1,0:T(8,128)(2,1)} %bitcast.15), channel_id=1, source_target_pairs={{0,1},{1,0},{2,3},{3,2},{4,5},{5,4},{6,7},{7,6},{8,9},{9,8},{10,11... | collective-permute-start | bytes 417800 | tf_op jit(solution)/shard_map/ppermute | solution.py:1248
  167.8 43.2 %collective-permute-start.1 = (bf16[128,4352]{1,0:T(8,128)(2,1)S(1)}, bf16[128,4352]{1,0:T(8,128)(2,1)S(1)}, u32[]{:S(2)}, u32[]{:S(2)}) collective-permute-start(bf16[128,4352]{1,0:T(8,128)(2,1)S(1)} %get-tuple-element.60.refs_2_), channel_id=1, source_target_pairs={{0,1},{1,0},{2,3},{3,2},{4,5},{5,4},{6,7},{7,6},{8,9},{9,8},{10,11... | collective-permute-start | bytes 3342344 | tf_op jit(solution)/shard_map/ppermute | solution.py:1248
  169.2 147.1 %collective-permute-start.4 = (bf16[544,128]{1,0:T(8,128)(2,1)}, bf16[544,128]{1,0:T(8,128)(2,1)}, u32[]{:S(2)}, u32[]{:S(2)}) collective-permute-start(bf16[544,128]{1,0:T(8,128)(2,1)} %bitcast.28), channel_id=1, source_target_pairs={{0,1},{1,0},{2,3},{3,2},{4,5},{5,4},{6,7},{7,6},{8,9},{9,8},{10,11... | collective-permute-start | bytes 417800 | tf_op jit(solution)/shard_map/ppermute | solution.py:1248
  201.5 114.8 %collective-permute-start.6 = (bf16[544,128]{1,0:T(8,128)(2,1)}, bf16[544,128]{1,0:T(8,128)(2,1)}, u32[]{:S(2)}, u32[]{:S(2)}) collective-permute-start(bf16[544,128]{1,0:T(8,128)(2,1)} %bitcast.158), channel_id=1, source_target_pairs={{0,1},{1,0},{2,3},{3,2},{4,5},{5,4},{6,7},{7,6},{8,9},{9,8},{10,11... | collective-permute-start | bytes 417800 | tf_op jit(solution)/shard_map/ppermute | solution.py:1248
  201.5 114.8 %collective-permute-start.7 = (bf16[128,1152]{1,0:T(8,128)(2,1)}, bf16[128,1152]{1,0:T(8,128)(2,1)}, u32[]{:S(2)}, u32[]{:S(2)}) collective-permute-start(bf16[128,1152]{1,0:T(8,128)(2,1)} %copy-done.23), channel_id=1, source_target_pairs={{0,1},{1,0},{2,3},{3,2},{4,5},{5,4},{6,7},{7,6},{8,9},{9,8},{10,11... | collective-permute-start | bytes 884744 | tf_op jit(solution)/shard_map/ppermute | solution.py:1248
  211.0 5.0 %copy-start.7 = (bf16[4096,256]{1,0:T(8,128)(2,1)S(1)}, bf16[4096,256]{1,0:T(8,128)(2,1)}, u32[]{:S(2)}) copy-start(bf16[4096,256]{1,0:T(8,128)(2,1)} %shard_map.264.refs_0_.x_ref) | copy-start | bytes 6291460
  211.0 5.0 %copy-start.15 = (bf16[4096,128]{1,0:T(8,128)(2,1)S(1)}, bf16[4096,128]{1,0:T(8,128)(2,1)}, u32[]{:S(2)}) copy-start(bf16[4096,128]{1,0:T(8,128)(2,1)} %shard_map.268.g_ref) | copy-start | bytes 3145732
  211.0 5.0 %copy-start.27 = (f32[64,4096]{1,0:T(8,128)S(1)}, f32[64,4096]{1,0:T(8,128)}, u32[]{:S(2)}) copy-start(f32[64,4096]{1,0:T(8,128)} %get-tuple-element.57.wide_ref) | copy-start | bytes 3145732
  211.0 5.0 %copy-start.28 = (f32[1,4096]{1,0:T(1,128)S(1)}, f32[1,4096]{1,0:T(1,128)}, u32[]{:S(2)}) copy-start(f32[1,4096]{1,0:T(1,128)} %get-tuple-element.58.lse_ref) | copy-start | bytes 49156
  274.6 28.1 %copy-start.17 = (f32[128,1088]{1,0:T(8,128)S(1)}, f32[128,1088]{1,0:T(8,128)}, u32[]{:S(2)}) copy-start(f32[128,1088]{1,0:T(8,128)} %copy-done.16) | copy-start | bytes 1671172
  302.7 3.1 copy-start.1
  307.0 4.1 copy-start.34
  307.0 4.1 copy-start.35
  310.7 5.6 %copy-start.24 = (bf16[128,1152]{1,0:T(8,128)(2,1)S(1)}, bf16[128,1152]{1,0:T(8,128)(2,1)}, u32[]{:S(2)}) copy-start(bf16[128,1152]{1,0:T(8,128)(2,1)} %copy-done.23) | copy-start | bytes 884740
  312.7 3.4 collective-permute-start.8
  313.5 2.8 collective-permute-start.5
  318.1 5.3 %copy-start.31 = (bf16[2,16,4608]{2,1,0:T(8,128)(2,1)S(1)}, bf16[2,16,4608]{2,1,0:T(8,128)(2,1)}, u32[]{:S(2)}) copy-start(bf16[2,16,4608]{2,1,0:T(8,128)(2,1)} %reshape.189) | copy-start | bytes 884740
  318.1 5.3 %copy-start.32 = (bf16[2,16,4352]{2,1,0:T(8,128)(2,1)S(1)}, bf16[2,16,4352]{2,1,0:T(8,128)(2,1)}, u32[]{:S(2)}) copy-start(bf16[2,16,4352]{2,1,0:T(8,128)(2,1)} %slice_bitcast_fusion.2) | copy-start | bytes 835588
  447.4 7.4 %copy-start.29 = (bf16[17,64,1088]{2,1,0:T(8,128)(2,1)S(1)}, bf16[17,64,1088]{2,1,0:T(8,128)(2,1)}, u32[]{:S(2)}) copy-start(bf16[17,64,1088]{2,1,0:T(8,128)(2,1)} %get-tuple-element.80) | copy-start | bytes 7102468
  (21 other events, 35.3 us)

commit v5 on v4

--- a/solution.py
+++ b/solution.py
@@ -37,45 +37,35 @@
     pl.semaphore_wait(barrier, count - 1)
 
 
-def rows_of(place, half, count):
-    block = place if half == 0 else 2 * count - 1 - place
-    return pl.ds(pl.multiple_of(block * BLOCK, BLOCK), BLOCK)
-
-
 def spread_kernel(count, x_ref, out_ref, send_sem, recv_sem, own_sem):
     me = lax.axis_index("ctx")
     core = lax.rem(lax.axis_index("fsdp"), 2)
     has, _ = held_head(me, core)
     greet_ctx(me, count)
 
-    def remote(head, source, half):
+    def remote(head, source):
         return pltpu.make_async_remote_copy(
-            src_ref=x_ref.at[head, pl.ds(half * BLOCK, BLOCK)],
-            dst_ref=out_ref.at[rows_of(source, half, count)],
-            send_sem=send_sem.at[head, half],
-            recv_sem=recv_sem.at[source, half],
+            src_ref=x_ref.at[head],
+            dst_ref=out_ref.at[source],
+            send_sem=send_sem.at[head],
+            recv_sem=recv_sem.at[source],
             device_id={"ctx": head_place(head, core)},
             device_id_type=MESH,
         )
 
-    def own(head, half):
-        return pltpu.make_async_copy(
-            x_ref.at[head, pl.ds(half * BLOCK, BLOCK)],
-            out_ref.at[rows_of(me, half, count)],
-            own_sem.at[half],
-        )
+    def own(head):
+        return pltpu.make_async_copy(x_ref.at[head], out_ref.at[me], own_sem.at[0])
 
     def send(head, carry):
         target = head_place(head, core)
-        for half in range(2):
-
-            @pl.when(target != me)
-            def _():
-                remote(head, me, half).start()
-
-            @pl.when(target == me)
-            def _():
-                own(head, half).start()
+
+        @pl.when(target != me)
+        def _():
+            remote(head, me).start()
+
+        @pl.when(target == me)
+        def _():
+            own(head).start()
 
         return carry
 
@@ -83,15 +73,14 @@
 
     def sent(head, carry):
         target = head_place(head, core)
-        for half in range(2):
-
-            @pl.when(target != me)
-            def _():
-                remote(head, me, half).wait_send()
-
-            @pl.when(target == me)
-            def _():
-                own(head, half).wait()
+
+        @pl.when(target != me)
+        def _():
+            remote(head, me).wait_send()
+
+        @pl.when(target == me)
+        def _():
+            own(head).wait()
 
         return carry
 
@@ -100,11 +89,9 @@
     @pl.when(has)
     def _():
         def arrived(source, carry):
-            for half in range(2):
-
-                @pl.when(source != me)
-                def _():
-                    remote(0, source, half).wait_recv()
+            @pl.when(source != me)
+            def _():
+                remote(0, source).wait_recv()
 
             return carry
 
@@ -117,51 +104,37 @@
     has, mine = held_head(me, core)
     greet_ctx(me, count)
 
-    def remote(head, target, half):
+    def remote(head, target):
         return pltpu.make_async_remote_copy(
-            src_ref=y_ref.at[rows_of(target, half, count)],
-            dst_ref=out_ref.at[head, pl.ds(half * BLOCK, BLOCK)],
-            send_sem=send_sem.at[target, half],
-            recv_sem=recv_sem.at[head, half],
+            src_ref=y_ref.at[target],
+            dst_ref=out_ref.at[head],
+            send_sem=send_sem.at[target],
+            recv_sem=recv_sem.at[head],
             device_id={"ctx": target},
             device_id_type=MESH,
         )
 
-    def own(half):
-        return pltpu.make_async_copy(
-            y_ref.at[rows_of(me, half, count)],
-            out_ref.at[mine, pl.ds(half * BLOCK, BLOCK)],
-            own_sem.at[half],
-        )
-
     @pl.when(has)
     def _():
         def send(step, carry):
-            target = lax.rem(me + step, count)
-            for half in range(2):
-                remote(mine, target, half).start()
+            remote(mine, lax.rem(me + 11 * step, count)).start()
             return carry
 
         lax.fori_loop(1, count, send, 0)
-        for half in range(2):
-            own(half).start()
+        own = pltpu.make_async_copy(y_ref.at[me], out_ref.at[mine], own_sem.at[0])
+        own.start()
 
         def sent(step, carry):
-            target = lax.rem(me + step, count)
-            for half in range(2):
-                remote(mine, target, half).wait_send()
+            remote(mine, lax.rem(me + 11 * step, count)).wait_send()
             return carry
 
         lax.fori_loop(1, count, sent, 0)
-        for half in range(2):
-            own(half).wait()
+        own.wait()
 
     def arrived(head, carry):
-        for half in range(2):
-
-            @pl.when(head_place(head, core) != me)
-            def _():
-                remote(head, 0, half).wait_recv()
+        @pl.when(head_place(head, core) != me)
+        def _():
+            remote(head, 0).wait_recv()
 
         return carry
 
@@ -169,37 +142,70 @@
 
 
 def spread_heads(packed, count, collective):
-    width = packed.shape[2]
     return pl.pallas_call(
         functools.partial(spread_kernel, count),
-        out_shape=jax.ShapeDtypeStruct((2 * BLOCK * count, width), packed.dtype),
-        in_specs=[pl.BlockSpec(memory_space=pl.ANY)],
-        out_specs=pl.BlockSpec(memory_space=pl.ANY),
+        out_shape=jax.ShapeDtypeStruct((count,) + packed.shape[1:], packed.dtype),
+        in_specs=[pl.BlockSpec(memory_space=pltpu.VMEM)],
+        out_specs=pl.BlockSpec(memory_space=pltpu.VMEM),
         scratch_shapes=[
-            pltpu.SemaphoreType.DMA((HEADS, 2)),
-            pltpu.SemaphoreType.DMA((count, 2)),
-            pltpu.SemaphoreType.DMA((2,)),
+            pltpu.SemaphoreType.DMA((HEADS,)),
+            pltpu.SemaphoreType.DMA((count,)),
+            pltpu.SemaphoreType.DMA((1,)),
         ],
-        compiler_params=pltpu.CompilerParams(collective_id=collective, has_side_effects=True),
+        compiler_params=pltpu.CompilerParams(
+            collective_id=collective, has_side_effects=True, vmem_limit_bytes=24 << 20
+        ),
         cost_estimate=pl.CostEstimate(flops=0, bytes_accessed=4 << 20, transcendentals=0),
     )(packed)
 
 
-def collect_heads(rows, count, collective):
-    width = rows.shape[1]
+def collect_heads(pieces, count, collective):
     return pl.pallas_call(
         functools.partial(collect_kernel, count),
-        out_shape=jax.ShapeDtypeStruct((HEADS, 2 * BLOCK, width), rows.dtype),
-        in_specs=[pl.BlockSpec(memory_space=pl.ANY)],
-        out_specs=pl.BlockSpec(memory_space=pl.ANY),
+        out_shape=jax.ShapeDtypeStruct((HEADS,) + pieces.shape[1:], pieces.dtype),
+        in_specs=[pl.BlockSpec(memory_space=pltpu.VMEM)],
+        out_specs=pl.BlockSpec(memory_space=pltpu.VMEM),
         scratch_shapes=[
-            pltpu.SemaphoreType.DMA((count, 2)),
-            pltpu.SemaphoreType.DMA((HEADS, 2)),
-            pltpu.SemaphoreType.DMA((2,)),
+            pltpu.SemaphoreType.DMA((count,)),
+            pltpu.SemaphoreType.DMA((HEADS,)),
+            pltpu.SemaphoreType.DMA((1,)),
         ],
-        compiler_params=pltpu.CompilerParams(collective_id=collective, has_side_effects=True),
+        compiler_params=pltpu.CompilerParams(
+            collective_id=collective, has_side_effects=True, vmem_limit_bytes=24 << 20
+        ),
         cost_estimate=pl.CostEstimate(flops=0, bytes_accessed=4 << 20, transcendentals=0),
-    )(rows)
+    )(pieces)
+
+
+TILES = 32
+
+
+def tile_span(at):
+    return pl.ds(pl.multiple_of(at * 128, 128), 128)
+
+
+def each_tile(visit):
+    def low(at, carry):
+        visit(at, 2 * at, 2 * at + 1, 0)
+        return carry
+
+    def high(at, carry):
+        visit(TILES // 2 + at, TILES - 1 - 2 * at, TILES - 2 - 2 * at, 64)
+        return carry
+
+    lax.fori_loop(0, TILES // 2, low, 0)
+    lax.fori_loop(0, TILES // 2, high, 0)
+
+
+def take_tile(ref, first, second, lane):
+    return jnp.concatenate(
+        [ref[first, :, lane : lane + 64], ref[second, :, lane : lane + 64]], axis=1
+    )
+
+
+def put_tile(ref, first, second, lane, tile):
+    ref[first, :, lane : lane + 64] = tile[:, 0:64]
+    ref[second, :, lane : lane + 64] = tile[:, 64:128]
 
 
 def dot_nt(left, right):
@@ -226,7 +232,7 @@
     holds = refs[13:16]
     own_sem, send_sem, recv_sem = refs[16:19]
     has, _ = held_head(lax.axis_index("ctx"), lax.rem(lax.axis_index("fsdp"), 2))
-    blocks = x_ref.shape[0] // STEP
+    blocks = lse_ref.shape[1] // STEP
     greet(gather_peers())
     sender = Sender(send_sem, recv_sem)
     steps = gather_steps(sources, targets, holds, Mover(own_sem), sender)
@@ -234,23 +240,22 @@
 
     @pl.when(has)
     def _():
-        def prepare(at, carry):
-            rows = pl.ds(pl.multiple_of(at * STEP, STEP), STEP)
-            q_ref[rows, :] = x_ref[rows, 0:64] * jnp.bfloat16(0.125)
-            k_ref[rows, :] = x_ref[rows, 64:128]
-            vt_ref[:, rows] = x_ref[rows, 128:256].T[0:64, :]
-            return carry
-
-        lax.fori_loop(0, blocks, prepare, 0)
+        def prepare(at, first, second, lane):
+            tile = take_tile(x_ref, first, second, lane)
+            q_ref[:, tile_span(at)] = tile[0:64] * jnp.bfloat16(0.125)
+            k_ref[tile_span(at), :] = tile[64:192].T[:, 0:64]
+            vt_ref[:, tile_span(at)] = tile[128:192]
+
+        each_tile(prepare)
 
     def one_block(at):
         asks = pl.ds(at * STEP, STEP)
-        query = q_ref[asks, :]
+        query = q_ref[:, asks]
 
         def update(state, place, masked):
             top, total, accum = state
             keys = pl.ds(pl.multiple_of(place * STEP, STEP), STEP)
-            scores = dot_nt(k_ref[keys, :], query)
+            scores = dot_nn(k_ref[keys, :], query)
             if masked:
                 scores = jnp.where(causal(scores), scores, -1e30)
             new_top = jnp.maximum(top, jnp.max(scores, axis=0, keepdims=True))
@@ -271,8 +276,15 @@
         result = accum / total
         wide_ref[:, asks] = result
         lse_ref[:, asks] = top + jnp.log(total)
-        full = jnp.concatenate([result, jnp.zeros_like(result)], axis=0)
-        out_ref[asks, :] = full.T.astype(jnp.bfloat16)
+        low = result.astype(jnp.bfloat16)
+        for part in range(4):
+            tile = low[:, 128 * part : 128 * part + 128]
+            index = 4 * at + part
+            if index < TILES // 2:
+                put_tile(out_ref, 2 * index, 2 * index + 1, 0, tile)
+            else:
+                rest = 2 * (index - TILES // 2)
+                put_tile(out_ref, TILES - 1 - rest, TILES - 2 - rest, 64, tile)
 
     for at in range(blocks):
         pl.when(has)(functools.partial(one_block, at))
@@ -302,11 +314,12 @@
     go_ref,
     dq_ref,
     delta_ref,
+    grad_ref,
     send_sem,
     recv_sem,
 ):
     has, _ = held_head(lax.axis_index("ctx"), lax.rem(lax.axis_index("fsdp"), 2))
-    blocks = x_ref.shape[0] // STEP
+    blocks = lse_ref.shape[1] // STEP
     greet(ring_peers())
     sender = Sender(send_sem, recv_sem)
     push_rings(sender, down_ref, down_z_ref, down_x_ref)
@@ -314,19 +327,24 @@
 
     @pl.when(has)
     def _():
-        def prepare(at, carry):
-            rows = pl.ds(pl.multiple_of(at * STEP, STEP), STEP)
-            q_ref[rows, :] = x_ref[rows, 0:64] * jnp.bfloat16(0.125)
-            k_ref[rows, :] = x_ref[rows, 64:128]
-            kt_ref[:, rows] = x_ref[rows, 0:128].T[64:128, :]
-            v_ref[rows, :] = x_ref[rows, 128:192]
-            go_ref[rows, :] = g_ref[rows, 0:64]
-            turned = g_ref[rows, :].T[0:64, :].astype(jnp.float32)
-            delta_ref[:, rows] = jnp.sum(turned * wide_ref[:, rows], axis=0, keepdims=True)
-            dq_ref[:, rows] = jnp.zeros((64, STEP), jnp.float32)
-            return carry
-
-        lax.fori_loop(0, blocks, prepare, 0)
+        blank = jnp.zeros((64, 128), jnp.bfloat16)
+
+        def prepare(at, first, second, lane):
+            span = tile_span(at)
+            tile = take_tile(x_ref, first, second, lane)
+            rows = jnp.concatenate([tile, blank], axis=0).T
+            q_ref[span, :] = rows[:, 0:64] * jnp.bfloat16(0.125)
+            k_ref[span, :] = rows[:, 64:128]
+            kt_ref[:, span] = tile[64:128]
+            v_ref[span, :] = rows[:, 128:192]
+            grad = take_tile(g_ref, first, second, lane)
+            go_ref[span, :] = jnp.concatenate([grad, blank], axis=0).T[:, 0:64]
+            delta_ref[:, span] = jnp.sum(
+                grad.astype(jnp.float32) * wide_ref[:, span], axis=0, keepdims=True
+            )
+            dq_ref[:, span] = jnp.zeros((64, 128), jnp.float32)
+
+        each_tile(prepare)
 
         def one_block(place, carry):
             keys = pl.ds(pl.multiple_of(place * STEP, STEP), STEP)
@@ -354,20 +372,20 @@
             grad_key, grad_value = lax.fori_loop(
                 place + 1, blocks, lambda at, held: update(held, at, False), state
             )
-            out_ref[keys, 64:128] = grad_key.astype(jnp.bfloat16)
-            out_ref[keys, 128:192] = grad_value.astype(jnp.bfloat16)
+            grad_ref[64:192, keys] = (
+                jnp.concatenate([grad_key, grad_value], axis=1).T.astype(jnp.bfloat16)
+            )
             return carry
 
         lax.fori_loop(0, blocks, one_block, 0)
 
-        def finish(at, carry):
-            rows = pl.ds(pl.multiple_of(at * STEP, STEP), STEP)
-            half = dq_ref[:, rows] * 0.125
-            full = jnp.concatenate([half, jnp.zeros_like(half)], axis=0).T
-            out_ref[rows, 0:64] = full[:, 0:64].astype(jnp.bfloat16)
-            return carry
-
-        lax.fori_loop(0, blocks, finish, 0)
+        def finish(at, first, second, lane):
+            span = tile_span(at)
+            query_part = (dq_ref[:, span] * 0.125).astype(jnp.bfloat16)
+            tile = jnp.concatenate([query_part, grad_ref[64:192, span]], axis=0)
+            put_tile(out_ref, first, second, lane, tile)
+
+        each_tile(finish)
 
     for copy in sender.started:
         copy.wait_recv()
@@ -375,13 +393,13 @@
 
 
 def run_forward(rows, weights, collective):
-    length = rows.shape[0]
+    length = rows.shape[0] * rows.shape[2]
     inside = pl.BlockSpec(memory_space=pltpu.VMEM)
     outside = pl.BlockSpec(memory_space=pl.ANY)
     results = pl.pallas_call(
         attend_forward,
         out_shape=[
-            jax.ShapeDtypeStruct((length, 128), jnp.bfloat16),
+            jax.ShapeDtypeStruct((TILES, 64, 128), jnp.bfloat16),
             jax.ShapeDtypeStruct((64, length), jnp.float32),
             jax.ShapeDtypeStruct((1, length), jnp.float32),
         ]
@@ -389,7 +407,7 @@
         in_specs=[inside] + [outside] * 3,
         out_specs=[inside] * 3 + [outside] * 3,
         scratch_shapes=[
-            pltpu.VMEM((length, 64), jnp.bfloat16),
+            pltpu.VMEM((64, length), jnp.bfloat16),
             pltpu.VMEM((length, 64), jnp.bfloat16),
             pltpu.VMEM((64, length), jnp.bfloat16),
         ]
@@ -412,7 +430,7 @@
 
 
 def run_backward(rows, grads, wide, lse, fc, down, collective):
-    length = rows.shape[0]
+    length = rows.shape[0] * rows.shape[2]
     inside = pl.BlockSpec(memory_space=pltpu.VMEM)
     outside = pl.BlockSpec(memory_space=pl.ANY)
     received = [
@@ -421,7 +439,7 @@
     ]
     results = pl.pallas_call(
         attend_backward,
-        out_shape=[jax.ShapeDtypeStruct((length, 256), jnp.bfloat16)] + received,
+        out_shape=[jax.ShapeDtypeStruct(rows.shape, jnp.bfloat16)] + received,
         in_specs=[inside] * 4 + [outside] * 2,
         out_specs=[inside] + [outside] * 4,
         scratch_shapes=[
@@ -432,11 +450,12 @@
             pltpu.VMEM((length, 64), jnp.bfloat16),
             pltpu.VMEM((64, length), jnp.float32),
             pltpu.VMEM((1, length), jnp.float32),
+            pltpu.VMEM((192, length), jnp.bfloat16),
             pltpu.SemaphoreType.DMA((12,)),
             pltpu.SemaphoreType.DMA((12,)),
         ],
         compiler_params=pltpu.CompilerParams(
-            collective_id=collective, has_side_effects=True, vmem_limit_bytes=40 << 20
+            collective_id=collective, has_side_effects=True, vmem_limit_bytes=58 << 20
         ),
         cost_estimate=pl.CostEstimate(
             flops=5 * length * length * 64,
@@ -701,7 +720,7 @@
         out_shape=jax.ShapeDtypeStruct((size, width), jnp.bfloat16),
         in_specs=specs,
         out_specs=pl.BlockSpec((block, width), lambda step: (step, 0)),
-        compiler_params=pltpu.CompilerParams(vmem_limit_bytes=40 << 20),
+        compiler_params=pltpu.CompilerParams(vmem_limit_bytes=58 << 20),
         cost_estimate=pl.CostEstimate(
             flops=512 * size * width, bytes_accessed=2 * size * width, transcendentals=0
         ),
@@ -994,17 +1013,17 @@
     return full.T[0:width, :]
 
 
-def before_kernel(tokens, gain, offset, weight, bias, packed, turned_ref, joint):
+def before_kernel(tokens, gain, offset, weight, bias, packed, turned_ref, joint, joint_t):
     unit, _ = normal_rows(widen(tokens[...]))
     normed = (unit * widen(gain[...]) + widen(offset[...])).astype(jnp.bfloat16)
     turned_ref[...] = turned(normed)
     joint[...] = (dot_nn(normed, weight[...]) + widen(bias[...])).astype(jnp.bfloat16)
-    blank = jnp.zeros((joint.shape[0], HEAD_DIM), jnp.bfloat16)
+    blank = jnp.zeros((joint.shape[0], 64), jnp.bfloat16)
+    joint_t[...] = jnp.concatenate([joint[...], blank], axis=1).T
     for head in range(HEADS):
-        parts = [
-            joint[:, 1088 * part + 64 * head : 1088 * part + 64 * head + 64] for part in range(3)
-        ]
-        packed[head] = jnp.concatenate(parts + [blank], axis=1)
+        for part in range(3):
+            start = 1088 * part + 64 * head
+            packed[head, 64 * part : 64 * part + 64] = joint_t[start : start + 64]
 
 
 def run_before(tokens, gain, offset, weight, bias):
@@ -1012,10 +1031,13 @@
     return pl.pallas_call(
         before_kernel,
         out_shape=(
-            jax.ShapeDtypeStruct((HEADS, rows, 256), jnp.bfloat16),
+            jax.ShapeDtypeStruct((HEADS, 192, rows), jnp.bfloat16),
             jax.ShapeDtypeStruct((1088, rows), jnp.bfloat16),
         ),
-        scratch_shapes=[pltpu.VMEM((rows, 3264), jnp.bfloat16)],
+        scratch_shapes=[
+            pltpu.VMEM((rows, 3264), jnp.bfloat16),
+            pltpu.VMEM((3328, rows), jnp.bfloat16),
+        ],
         compiler_params=pltpu.CompilerParams(vmem_limit_bytes=40 << 20),
         cost_estimate=pl.CostEstimate(
             flops=2 * rows * 1088 * 3264, bytes_accessed=8 << 20, transcendentals=0
@@ -1038,7 +1060,6 @@
     result,
     grad_middle,
     grad_heads,
-    attended_t,
     normed_t,
     grad_branch,
     active_t,
@@ -1056,9 +1077,8 @@
 
     @pl.when(at == 0)
     def _():
-        for head in range(HEADS):
-            attended[:, 64 * head : 64 * head + 64] = heads[head, :, 0:64]
-        attended_t[...] = turned(attended[...])
+        filler = jnp.zeros((64, heads.shape[1]), jnp.bfloat16)
+        attended[...] = jnp.concatenate([heads[...], filler], axis=0).T[:, 0:1088]
         middle = widen(tokens[...]) + (dot_nn(attended[...], w_out[...]) + widen(b_out[...]))
         unit[...], scale[...] = normal_rows(middle)
         normed[...] = (unit[...] * widen(gain[...]) + widen(offset[...])).astype(jnp.bfloat16)
@@ -1095,10 +1115,7 @@
         sums[2:3, :] = column_sums(whole)
         sums[3:4, :] = column_sums(arrived)
         attended[...] = dot_nt(low, w_out[...]).astype(jnp.bfloat16)
-        blank = jnp.zeros((low.shape[0], HEAD_DIM), jnp.bfloat16)
-        for head in range(HEADS):
-            piece = attended[:, 64 * head : 64 * head + 64]
-            grad_heads[head] = jnp.concatenate([piece, blank], axis=1)
+        grad_heads[...] = turned(attended[...])
 
 
 def run_middle(heads, tokens, cotangent, w_out, b_out, gain, offset, b_down, fc, b_fc, down):
@@ -1117,7 +1134,7 @@
         middle_kernel,
         grid=(4352 // block,),
         in_specs=[
-            fixed((HEADS, rows, 128)),
+            fixed((1088, rows)),
             square,
             square,
             fixed((1088, 1088)),
@@ -1132,7 +1149,6 @@
         out_specs=[
             square,
             square,
-            fixed((HEADS, rows, 128)),
             fixed((1088, rows)),
             fixed((1088, rows)),
             fixed((rows, 1152)),
@@ -1144,7 +1160,6 @@
         out_shape=[
             jax.ShapeDtypeStruct((rows, 1088), low),
             jax.ShapeDtypeStruct((rows, 1088), wide),
-            jax.ShapeDtypeStruct((HEADS, rows, 128), low),
             jax.ShapeDtypeStruct((1088, rows), low),
             jax.ShapeDtypeStruct((1088, rows), low),
             jax.ShapeDtypeStruct((rows, 1152), low),
@@ -1168,12 +1183,13 @@
     )(heads, tokens, cotangent, w_out, b_out, gain, offset, b_down, fc, b_fc, down)
 
 
-def after_kernel(packed, weight, tokens, gain, grad_middle, joint, grad_tokens, sums, line):
+def after_kernel(packed, weight, tokens, gain, grad_middle, joint, grad_tokens, sums, line, joint_t):
     for head in range(HEADS):
         for part in range(3):
             start = 1088 * part + 64 * head
-            joint[:, start : start + 64] = packed[head, :, 64 * part : 64 * part + 64]
-    joint[:, 3264:3328] = jnp.zeros((joint.shape[0], 64), jnp.bfloat16)
+            joint_t[start : start + 64] = packed[head, 64 * part : 64 * part + 64]
+    joint_t[3264:3328] = jnp.zeros((64, joint.shape[0]), jnp.bfloat16)
+    joint[...] = joint_t[...].T
     unit, scale = normal_rows(widen(tokens[...]))
     grads = dot_nt(joint[:, 0:3264], weight[...])
     back = norm_back(grads, widen(gain[...]), unit, scale)
@@ -1193,6 +1209,7 @@
             jax.ShapeDtypeStruct((2, 1088), jnp.float32),
             jax.ShapeDtypeStruct((1, 3264), jnp.float32),
         ),
+        scratch_shapes=[pltpu.VMEM((3328, rows), jnp.bfloat16)],
         compiler_params=pltpu.CompilerParams(vmem_limit_bytes=40 << 20),
         cost_estimate=pl.CostEstimate(
             flops=2 * rows * 1088 * 3264, bytes_accessed=10 << 20, transcendentals=0
@@ -1270,11 +1287,11 @@
     full_out = full_out.reshape(1088, 1088)
     full_fc = full_fc.reshape(1088, 4352)
     full_down = full_down.reshape(4352, 1088)
+    attended_t = collect_heads(out_rows, ctx_count, 2).reshape(1088, -1)
     (
         result,
         grad_middle,
         grad_heads,
-        attended_t,
         normed2_t,
         grad_branch,
         active_t,
@@ -1282,7 +1299,7 @@
         line_fc,
         sums_middle,
     ) = run_middle(
-        collect_heads(out_rows, ctx_count, 2),
+        attended_t,
         tokens[0],
         cotangent[0],
         full_out,
@@ -1297,7 +1314,9 @@
     d_down = weight_products([products(active_t, cotangent[0])], 1088)
     d_fc = weight_products([products(normed2_t, grad_hidden)], 4352)
     out_products = products(attended_t, grad_branch)
-    grad_rows = spread_heads(grad_heads, ctx_count, 3)
+    grad_rows = spread_heads(
+        grad_heads.reshape(HEADS, HEAD_DIM, -1), ctx_count, 3
+    )
     joint_rows_grad, far_z, far_x = run_backward(
         head_rows, grad_rows, wide_out, lse_rows, d_fc, d_down, 7
     )

time: 462 us -> 427 us (0.924)
  local copies, waits for them, and re-layouts: 57.3 us -> 38.8 us
  Pallas kernels: 381 us -> 363 us
    unnamed x79 -> x45, local copies, waits for them, and re-layouts: 31.9 us -> 15 us
    pallas_call x2, Pallas kernels: 46.4 us -> 33.8 us  [collect_heads(): pl.pallas_call(functools.partial(collect_kernel, count), out_shape=jax.Sh...]
    pallas_call x2, Pallas kernels: 50.4 us -> 38.3 us  [spread_heads(): pl.pallas_call(functools.partial(spread_kernel, count), out_shape=jax.Sha...]
    concatenate x10, local copies, waits for them, and re-layouts: 6.79 us -> 0.89 us  [local(): sums = jnp.concatenate([vector.reshape(4, -1) for vector in narrow], axis=1)]
    pallas_call x3, Pallas kernels: 11.3 us -> 17.1 us  [weight_products(): pl.pallas_call(functools.partial(product_kernel, cut), grid=(size // bloc...]
  transfers between devices with their start and end apart: 9 -> 9, of which waited for: 0 -> 1; matrix products, arithmetic and copies ran while one was open for 7% -> 6% of each run, Pallas kernels for 56% -> 57%
where the time goes in v5:
time: 427 us; the launch traced here: 425 us
  Pallas kernels  363 us (85%)
  local copies, waits for them, and re-layouts  38.8 us (9%)
  other arithmetic  18.9 us (4%)
    pallas_call x1, Pallas kernels, last_exchange(): pl.pallas_call(last_kernel, out_shape=[jax.ShapeDtypeStruct((UNITS,) + un...  117 us
    pallas_call x1, Pallas kernels, run_backward(): pl.pallas_call(attend_backward, out_shape=[jax.ShapeDtypeStruct(rows.shap...  56.6 us
    pallas_call x1, Pallas kernels, run_forward(): pl.pallas_call(attend_forward, out_shape=[jax.ShapeDtypeStruct((TILES, 64...  47.5 us
    pallas_call x2, Pallas kernels, spread_heads(): pl.pallas_call(functools.partial(spread_kernel, count), out_shape=jax.Sha...  38.3 us
    pallas_call x2, Pallas kernels, collect_heads(): pl.pallas_call(functools.partial(collect_kernel, count), out_shape=jax.Sh...  33.8 us
    pallas_call x1, Pallas kernels, gather_weights(): pl.pallas_call(gather_kernel, out_shape=shapes, in_specs=[pl.BlockSpec(me...  27.1 us
    pallas_call x1, Pallas kernels, run_middle(): pl.pallas_call(middle_kernel, grid=(4352 // block,), in_specs=[fixed((108...  21.7 us
    pallas_call x3, Pallas kernels, weight_products(): pl.pallas_call(functools.partial(product_kernel, cut), grid=(size // bloc...  17.1 us
  transfers between devices with their start and end apart: 9, of which 1 were waited for; matrix products, arithmetic and copies ran while one was open for 6% of the time, Pallas kernels for 57%

profile of v5, /device:TPU:8, one launch (start us, length us, event | category | flops | bytes accessed | tf_op | source)
XLA Modules:
  0.0 425.3 jit_solution(15284270185223287516)
XLA Ops:
  9.5 27.1 %shard_map.262 = (bf16[4,17,16,3264]{3,2,1,0:T(8,128)(2,1)}, bf16[4,16,272]{2,1,0:T(8,128)(2,1)}) custom-call(bf16[17,16,3264]{2,1,0:T(8,128)(2,1)} %bitcast.155, bf16[16,272]{1,0:T(8,128)(2,1)} %concatenate.31.small), custom_call_target="tpu_custom_call" | custom-call | bytes 20971520 | tf_op jit(solution)/shard_map/pallas_call | solution.py:674
  39.3 3.1 copy-done
  42.4 1.6 shard_map.263
  44.0 25.3 %shard_map.264.refs_0_.x_ref = bf16[32,192,128]{2,1,0:T(8,128)(2,1)S(1)} custom-call(bf16[17,192,128]{2,1,0:T(8,128)(2,1)S(1)} %get-tuple-element.49.x_ref), custom_call_target="tpu_custom_call" | custom-call | bytes 4194304 | tf_op jit(solution)/shard_map/pallas_call | solution.py:145
  70.5 47.5 %shard_map.265 = (bf16[32,64,128]{2,1,0:T(8,128)(2,1)}, f32[64,4096]{1,0:T(8,128)}, f32[1,4096]{1,0:T(1,128)}, bf16[4,17,16,1088]{3,2,1,0:T(8,128)(2,1)}, bf16[4...) custom-call(bf16[32,192,128]{2,1,0:T(8,128)(2,1)} %copy-done.6, bf16[17,16,1088]{2,1,0:T(8,128)(2,1)} %bitcast.166, ...), custom_call_target="tpu_custom_call" | custom-call | flops 2147483648 | bytes 4194304 | tf_op jit(solution)/shard_map/pallas_call | solution.py:399
  119.0 12.2 %shard_map.266 = bf16[17,64,128]{2,1,0:T(8,128)(2,1)S(1)} custom-call(bf16[32,64,128]{2,1,0:T(8,128)(2,1)S(1)} %copy-done.11), custom_call_target="tpu_custom_call" | custom-call | bytes 4194304 | tf_op jit(solution)/shard_map/pallas_call | solution.py:163
  131.8 21.7 %shard_map.267 = (bf16[128,1088]{1,0:T(8,128)(2,1)S(1)}, f32[128,1088]{1,0:T(8,128)S(1)}, bf16[1088,128]{1,0:T(8,128)(2,1)S(1)}, bf16[1088,128]{1,0:T(8,128)(2,1...) custom-call(bf16[1088,128]{1,0:T(8,128)(2,1)S(1)} %bitcast.132, ...), custom_call_target="tpu_custom_call" | custom-call | flops 4848615424 | bytes 25165824 | tf_op jit(solution)/shard_map/pallas_call | solution.py:1133
  160.2 13.0 %shard_map.268.g_ref = bf16[32,64,128]{2,1,0:T(8,128)(2,1)S(1)} custom-call(bf16[17,64,128]{2,1,0:T(8,128)(2,1)S(1)} %bitcast.138), custom_call_target="tpu_custom_call" | custom-call | bytes 4194304 | tf_op jit(solution)/shard_map/pallas_call | solution.py:145
  176.5 7.5 %shard_map.270 = bf16[2176,1088]{1,0:T(8,128)(2,1)} custom-call(bf16[2176,128]{1,0:T(8,128)(2,1)} %bitcast.154, bf16[2176,128]{1,0:T(8,128)(2,1)} %collective-permute-done.2.refs_1_, bf16[128,1088]{1,0:T(8,128)(2,1)} %bitcast.131, bf16[128,1088]{1,0:T(8,128)(2,1)} %collective-permute-done.3.refs_3_), custom_call_target="tpu_custom_call" | custom-call | flops 1212153856 | bytes 4734976 | tf_op jit(solution)/shard_map/pallas_call | solution.py:717
  186.1 4.7 %shard_map.269 = bf16[544,4352]{1,0:T(8,128)(2,1)} custom-call(bf16[544,128]{1,0:T(8,128)(2,1)} %bitcast.157, bf16[544,128]{1,0:T(8,128)(2,1)} %collective-permute-done.refs_1_, bf16[128,4352]{1,0:T(8,128)(2,1)} %copy-done.8, bf16[128,4352]{1,0:T(8,128)(2,1)} %collective-permute-done.1.refs_3_), custom_call_target="tpu_custom_call" | custom-call | flops 1212153856 | bytes 4734976 | tf_op jit(solution)/shard_map/pallas_call | solution.py:717
  190.8 1.7 slice_bitcast_fusion.2
  192.5 56.6 %shard_map.271 = (bf16[32,192,128]{2,1,0:T(8,128)(2,1)}, bf16[3,2,2,16,4352]{4,3,2,1,0:T(8,128)(2,1)}, bf16[3,2,2,64,1088]{4,3,2,1,0:T(8,128)(2,1)}, bf16[3,2,2,...) custom-call(bf16[32,192,128]{2,1,0:T(8,128)(2,1)} %copy-done.6, bf16[32,64,128]{2,1,0:T(8,128)(2,1)} %copy-done.10, ...), custom_call_target="tpu_custom_call" | custom-call | flops 5368709120 | bytes 6291456 | tf_op jit(solution)/shard_map/pallas_call | solution.py:440
  249.1 1.4 copy-done.7
  250.5 21.5 %shard_map.272.packed = bf16[17,192,128]{2,1,0:T(8,128)(2,1)S(1)} custom-call(bf16[32,192,128]{2,1,0:T(8,128)(2,1)S(1)} %copy-done.7), custom_call_target="tpu_custom_call" | custom-call | bytes 4194304 | tf_op jit(solution)/shard_map/pallas_call | solution.py:163
  272.1 3.0 copy-done.1
  275.1 2.6 shard_map.273
  283.3 5.0 %shard_map.274 = bf16[544,4352]{1,0:T(8,128)(2,1)} custom-call(bf16[544,128]{1,0:T(8,128)(2,1)} %bitcast.158, bf16[544,128]{1,0:T(8,128)(2,1)} %collective-permute-done.4.refs_1_, bf16[128,3328]{1,0:T(8,128)(2,1)} %copy-done.9, bf16[128,3328]{1,0:T(8,128)(2,1)} %copy-done.17, bf16[544,128]{1,0:T(8,128)(2,1)} %bitcast.159, ...), custom_call_target="tpu_custom_call" | custom-call | flops 1212153856 | bytes 4734976 | tf_op jit(solution)/shard_map/pallas_call | solution.py:717
  290.3 3.6 reshape.194
  293.9 1.5 copy.85
  295.6 116.8 %shard_map.275 = (bf16[17,16,4352]{2,1,0:T(8,128)(2,1)}, bf16[17,16,4352]{2,1,0:T(8,128)(2,1)}, bf16[17,64,1088]{2,1,0:T(8,128)(2,1)}, bf16[16,1024]{1,0:T(8,128)(2,1)S(1)}) custom-call(bf16[2,17,16,4352]{3,2,1,0:T(8,128)(2,1)} %bitcast.148, bf16[2,17,16,4352]{3,2,1,0:T(8,128)(2,1)} %bitcast.146, bf16[2,17,64,1088]{3,2,1,0:T(8,128)(2,1)} %bitcast.143, ...), custom_call_target="tpu_custom_call" | custom-call | bytes 41943040 | tf_op jit(solution)/shard_map/pallas_call | solution.py:957
  412.5 3.7 slice_convert_fusion
  416.2 2.4 slice_convert_fusion.1
  419.8 2.8 bitcast_convert_fusion
  422.6 2.6 bitcast_convert_fusion.1
  (125 shorter events, 35.2 us)
Async XLA Ops:
  0.6 38.4 %copy-start.18 = (bf16[1,128,1088]{1,2,0:T(8,128)(2,1)S(1)}, bf16[1,128,1088]{1,2,0:T(8,128)(2,1)}, u32[]{:S(2)}) copy-start(bf16[1,128,1088]{1,2,0:T(8,128)(2,1)} %param.15) | copy-start | bytes 835588
  1.9 129.9 %copy-start.2 = (bf16[1,128,1088]{2,1,0:T(8,128)(2,1)}, bf16[1,128,1088]{2,1,0:T(8,128)(2,1)S(1)}, u32[]{:S(2)}) copy-start(bf16[1,128,1088]{2,1,0:T(8,128)(2,1)S(1)} %copy.47) | copy-start | bytes 835588
  1.9 174.2 %collective-permute-start.3 = (bf16[128,1088]{1,0:T(8,128)(2,1)S(1)}, bf16[128,1088]{1,0:T(8,128)(2,1)}, u32[]{:S(2)}, u32[]{:S(2)}) collective-permute-start(bf16[128,1088]{1,0:T(8,128)(2,1)S(1)} %bitcast.129), channel_id=1, source_target_pairs={{0,1},{1,0},{2,3},{3,2},{4,5},{5,4},{6,7},{7,6},{8,9},{9,8},{10,11... | collective-permute-start | bytes 835592 | tf_op jit(solution)/shard_map/ppermute | solution.py:1265
  39.3 3.1 copy-start
  153.5 2.5 copy-start.8
  153.5 22.5 %copy-start.12 = (bf16[128,1152]{1,0:T(8,128)(2,1)}, bf16[128,1152]{1,0:T(8,128)(2,1)S(1)}, u32[]{:S(2)}) copy-start(bf16[128,1152]{1,0:T(8,128)(2,1)S(1)} %get-tuple-element.66.refs_6_) | copy-start | bytes 884740
  154.7 21.3 %collective-permute-start.2 = (bf16[2176,128]{1,0:T(8,128)(2,1)}, bf16[2176,128]{1,0:T(8,128)(2,1)}, u32[]{:S(2)}, u32[]{:S(2)}) collective-permute-start(bf16[2176,128]{1,0:T(8,128)(2,1)} %bitcast.23), channel_id=1, source_target_pairs={{0,1},{1,0},{2,3},{3,2},{4,5},{5,4},{6,7},{7,6},{8,9},{9,8},{10,11... | collective-permute-start | bytes 1671176 | tf_op jit(solution)/shard_map/ppermute | solution.py:1265
  155.4 30.7 %collective-permute-start = (bf16[544,128]{1,0:T(8,128)(2,1)}, bf16[544,128]{1,0:T(8,128)(2,1)}, u32[]{:S(2)}, u32[]{:S(2)}) collective-permute-start(bf16[544,128]{1,0:T(8,128)(2,1)} %bitcast.17), channel_id=1, source_target_pairs={{0,1},{1,0},{2,3},{3,2},{4,5},{5,4},{6,7},{7,6},{8,9},{9,8},{10,11... | collective-permute-start | bytes 417800 | tf_op jit(solution)/shard_map/ppermute | solution.py:1265
  155.9 30.2 %collective-permute-start.1 = (bf16[128,4352]{1,0:T(8,128)(2,1)S(1)}, bf16[128,4352]{1,0:T(8,128)(2,1)}, u32[]{:S(2)}, u32[]{:S(2)}) collective-permute-start(bf16[128,4352]{1,0:T(8,128)(2,1)S(1)} %get-tuple-element.59.refs_2_), channel_id=1, source_target_pairs={{0,1},{1,0},{2,3},{3,2},{4,5},{5,4},{6,7},{7,6},{8,9},{9,8},{10,11... | collective-permute-start | bytes 3342344 | tf_op jit(solution)/shard_map/ppermute | solution.py:1265
  156.6 124.9 %collective-permute-start.4 = (bf16[544,128]{1,0:T(8,128)(2,1)}, bf16[544,128]{1,0:T(8,128)(2,1)}, u32[]{:S(2)}, u32[]{:S(2)}) collective-permute-start(bf16[544,128]{1,0:T(8,128)(2,1)} %bitcast.30), channel_id=1, source_target_pairs={{0,1},{1,0},{2,3},{3,2},{4,5},{5,4},{6,7},{7,6},{8,9},{9,8},{10,11... | collective-permute-start | bytes 417800 | tf_op jit(solution)/shard_map/ppermute | solution.py:1265
  176.0 105.5 %collective-permute-start.7 = (bf16[128,1152]{1,0:T(8,128)(2,1)S(1)}, bf16[128,1152]{1,0:T(8,128)(2,1)}, u32[]{:S(2)}, u32[]{:S(2)}) collective-permute-start(bf16[128,1152]{1,0:T(8,128)(2,1)S(1)} %get-tuple-element.66.refs_6_), channel_id=1, source_target_pairs={{0,1},{1,0},{2,3},{3,2},{4,5},{5,4},{6,7},{7,6},{8,9},{9,8},{10,11... | collective-permute-start | bytes 884744 | tf_op jit(solution)/shard_map/ppermute | solution.py:1265
  176.0 105.5 %collective-permute-start.6 = (bf16[544,128]{1,0:T(8,128)(2,1)}, bf16[544,128]{1,0:T(8,128)(2,1)}, u32[]{:S(2)}, u32[]{:S(2)}) collective-permute-start(bf16[544,128]{1,0:T(8,128)(2,1)} %bitcast.35), channel_id=1, source_target_pairs={{0,1},{1,0},{2,3},{3,2},{4,5},{5,4},{6,7},{7,6},{8,9},{9,8},{10,11... | collective-permute-start | bytes 417800 | tf_op jit(solution)/shard_map/ppermute | solution.py:1265
  249.1 1.4 copy-start.7
  272.1 3.1 copy-start.1
  277.7 4.7 %copy-start.9 = (bf16[128,3328]{1,0:T(8,128)(2,1)}, bf16[128,3328]{1,0:T(8,128)(2,1)S(1)}, u32[]{:S(2)}) copy-start(bf16[128,3328]{1,0:T(8,128)(2,1)S(1)} %get-tuple-element.65.refs_2_) | copy-start | bytes 2555908
  279.1 2.4 collective-permute-start.8
  279.8 2.6 collective-permute-start.5
  283.3 6.0 %copy-start.15 = (bf16[2,16,4608]{2,1,0:T(8,128)(2,1)S(1)}, bf16[2,16,4608]{2,1,0:T(8,128)(2,1)}, u32[]{:S(2)}) copy-start(bf16[2,16,4608]{2,1,0:T(8,128)(2,1)} %reshape.193) | copy-start | bytes 884740
  283.3 6.0 %copy-start.16 = (bf16[2,16,4352]{2,1,0:T(8,128)(2,1)S(1)}, bf16[2,16,4352]{2,1,0:T(8,128)(2,1)}, u32[]{:S(2)}) copy-start(bf16[2,16,4352]{2,1,0:T(8,128)(2,1)} %slice_bitcast_fusion.2) | copy-start | bytes 835588
  289.3 6.1 %copy-start.3 = (bf16[3,2,2,64,1088]{4,3,2,1,0:T(8,128)(2,1)S(1)}, bf16[3,2,2,64,1088]{4,3,2,1,0:T(8,128)(2,1)}, u32[]{:S(2)}) copy-start(bf16[3,2,2,64,1088]{4,3,2,1,0:T(8,128)(2,1)} %get-tuple-element.72.refs_5_) | copy-start | bytes 5013508
  289.3 6.1 %copy-start.4 = (bf16[3,2,2,16,4352]{4,3,2,1,0:T(8,128)(2,1)S(1)}, bf16[3,2,2,16,4352]{4,3,2,1,0:T(8,128)(2,1)}, u32[]{:S(2)}) copy-start(bf16[3,2,2,16,4352]{4,3,2,1,0:T(8,128)(2,1)} %get-tuple-element.71.refs_4_) | copy-start | bytes 5013508
  293.9 1.7 copy-start.5
  412.5 7.4 %copy-start.13 = (bf16[17,64,1088]{2,1,0:T(8,128)(2,1)S(1)}, bf16[17,64,1088]{2,1,0:T(8,128)(2,1)}, u32[]{:S(2)}) copy-start(bf16[17,64,1088]{2,1,0:T(8,128)(2,1)} %get-tuple-element.78) | copy-start | bytes 7102468
  419.8 2.8 copy-start.14
  (4 other events, 3.9 us)

commit v6 on v5

--- a/solution.py
+++ b/solution.py
@@ -752,7 +752,7 @@
     return values[:, 0:2176], values[:, 2176:4352]
 
 
-LAST_COPIES = 6 + 3 * (6 + 3 + 6 + 6 + 18) + 3 + 3 + 3 + 3 + 3 + 9
+LAST_COPIES = 6 + 3 * (6 + 3 + 6 + 16 + 16) + 3 + 3 + 3 + 3 + 3 + 9
 
 
 def last_kernel(*refs):
@@ -778,12 +778,16 @@
         if group > 0:
             loads[group].append(mover.move(far_z[group], by[group].at[0]))
             loads[group].append(mover.move(far_x[group], by[group].at[1]))
-    load_tail = mover.move(tail.at[:, z], own_t)
+
+    def tail_part(place):
+        return tail.at[:, :, pl.ds(pl.multiple_of(place * 4 * TAIL, 128), 4 * TAIL)]
+
+    load_tail = mover.move(tail_part(z), own_t)
     greet(ring_peers() + [near_peer(), cross_peer(), far_peer()])
     sender = Sender(send_sem, recv_sem)
     first = push_rings(sender, terms[0], by[0].at[0], by[0].at[1])
     first_t = [
-        sender.push(tail.at[:, lax.rem(z + step, 4)], by_t.at[step - 1], z_peer(step))
+        sender.push(tail_part(lax.rem(z + step, 4)), by_t.at[step - 1], z_peer(step))
         for step in (2, 1, 3)
     ]
 
@@ -816,9 +820,10 @@
     for copy in first_t:
         copy.wait_recv()
     for place in range(4):
-        total = widen(own_t[:, place])
+        columns = slice(TAIL * place, TAIL * (place + 1))
+        total = widen(own_t[:, :, columns])
         for step in range(3):
-            total = total + widen(by_t[step, :, place])
+            total = total + widen(by_t[step, :, :, columns])
         parted_t[place] = total.astype(jnp.bfloat16)
     second_t = [
         sender.push(parted_t.at[lax.rem(x + step, 4)], met_t.at[step - 1], x_peer(step))
@@ -850,14 +855,31 @@
     merged_t[...] = total.astype(jnp.bfloat16)
     third_t = across(merged_t, landed_t)
 
-    def spot(group, ring, at_z, at_x):
+    def spot(group, ring, at_z, at_x, side=None):
         unit = 2 * at_z + at_x // 2 if ring == 0 else 8 + 2 * at_x + at_z // 2
         half = lax.rem(at_x, 2) if ring == 0 else lax.rem(at_z, 2)
         if group == 2:
-            return totals[group].at[unit, pl.ds(pl.multiple_of(half * 32, 32), 32)]
-        return totals[group].at[unit, :, pl.ds(pl.multiple_of(half * 2176, 128), 2176)]
-
-    passed, ends, owns = [], [], []
+            start, size = ((0, 32), (0, 16), (16, 16))[0 if side is None else side + 1]
+            rows = pl.ds(pl.multiple_of(half * 32 + start, 16), size)
+            return totals[group].at[unit, rows]
+        start, size = ((0, 2176), (0, 1152), (1152, 1024))[0 if side is None else side + 1]
+        columns = pl.ds(pl.multiple_of(half * 2176 + start, 128), size)
+        return totals[group].at[unit, :, columns]
+
+    def step_on(ring, at_z, at_x, step):
+        if ring == 0:
+            return lax.rem(at_z + step, 4), at_x
+        return at_z, lax.rem(at_x + step, 4)
+
+    passed, ends, owns, nexts = [], [], [], []
+
+    def spread_on(group, ring, source, at_z, at_x):
+        place = spot(group, ring, at_z, at_x)
+        for step in (1, 3):
+            peer = z_peer(step) if ring == 0 else x_peer(step)
+            copy = sender.push(source, place, peer)
+            nexts.append((group, ring, step, at_z, at_x, copy))
+
     for group in order:
         for copy in third[group]:
             copy.wait_recv()
@@ -871,9 +893,7 @@
             for step in (1, 3, 2):
                 peer = x_peer(step) if ring == 0 else z_peer(step)
                 passed.append((group, ring, step, sender.push(piece, place, peer)))
-            for step in (1, 3, 2):
-                peer = z_peer(step) if ring == 0 else x_peer(step)
-                ends.append(sender.push(piece, place, peer))
+            spread_on(group, ring, piece, z, x)
     for copy in third_t:
         copy.wait_recv()
     near = widen(merged_t[0]) + widen(landed_t[0])
@@ -889,13 +909,17 @@
         copy.wait_recv()
         if group == 3:
             place = whole_t.at[z, lax.rem(x - step + 4, 4)]
-        elif ring == 0:
-            place = spot(group, ring, z, lax.rem(x - step + 4, 4))
-        else:
-            place = spot(group, ring, lax.rem(z - step + 4, 4), x)
-        for other in (1, 3, 2):
-            peer = z_peer(other) if ring == 0 else x_peer(other)
-            ends.append(sender.push(place, place, peer))
+            for other in (1, 3, 2):
+                ends.append(sender.push(place, place, z_peer(other)))
+            continue
+        at_z, at_x = step_on(1 - ring, z, x, 4 - step)
+        spread_on(group, ring, spot(group, ring, at_z, at_x), at_z, at_x)
+    for group, ring, step, at_z, at_x, copy in nexts:
+        copy.wait_recv()
+        from_z, from_x = step_on(ring, at_z, at_x, 4 - step)
+        piece = spot(group, ring, from_z, from_x, 0 if step == 1 else 1)
+        peer = z_peer(step) if ring == 0 else x_peer(step)
+        ends.append(sender.push(piece, piece, peer))
     for copy in ends:
         copy.wait_recv()
     for copy in owns:
@@ -937,8 +961,8 @@
         + each(lambda unit, piece: (3, 2) + piece)
         + each(lambda unit, piece: (2,) + piece)
         + [
-            pltpu.VMEM((2, 4, 16, TAIL), low),
-            pltpu.VMEM((3, 2, 4, 16, TAIL), low),
+            pltpu.VMEM((2, 16, 4 * TAIL), low),
+            pltpu.VMEM((3, 2, 16, 4 * TAIL), low),
             pltpu.VMEM((4, 2, 16, TAIL), low),
             pltpu.VMEM((3, 2, 16, TAIL), low),
             pltpu.VMEM((2, 16, TAIL), low),
@@ -976,7 +1000,6 @@
     tail = jnp.concatenate(
         [terms[0][:, 16], terms[1][:, 16], down, extra.astype(jnp.bfloat16)], axis=-1
     )
-    tail = jnp.transpose(tail.reshape(2, 16, 4, 4, TAIL), (0, 2, 3, 1, 4))
     joint, fc, down, small = last_exchange(terms, tail, far_z, far_x, collective)
     joint = joint.reshape(272, 4352)
     outs = (

time: 427 us -> 412 us (0.965)
  Pallas kernels: 363 us -> 355 us
  local copies, waits for them, and re-layouts: 38.8 us -> 32.5 us
    pallas_call x1, Pallas kernels: 117 us -> 109 us  [last_exchange(): pl.pallas_call(last_kernel, out_shape=[jax.ShapeDtypeStruct((UNITS,) + un...]
    reshape x2 -> x0, local copies, waits for them, and re-layouts: 5.05 us -> none  [reduce_grads(): tail = jnp.transpose(tail.reshape(2, 16, 4, 4, TAIL), (0, 2, 3, 1, 4))]
    unnamed x45 -> x40, local copies, waits for them, and re-layouts: 15 us -> 14.2 us
  transfers between devices with their start and end apart: 9 -> 9, of which waited for: 1 -> 1; matrix products, arithmetic and copies ran while one was open for 6% -> 6% of each run, Pallas kernels for 57% -> 59%
where the time goes in v6:
time: 412 us; the launch traced here: 410 us
  Pallas kernels  355 us (86%)
  local copies, waits for them, and re-layouts  32.5 us (8%)
  other arithmetic  18 us (4%)
    pallas_call x1, Pallas kernels, last_exchange(): pl.pallas_call(last_kernel, out_shape=[jax.ShapeDtypeStruct((UNITS,) + un...  109 us
    pallas_call x1, Pallas kernels, run_backward(): pl.pallas_call(attend_backward, out_shape=[jax.ShapeDtypeStruct(rows.shap...  56.6 us
    pallas_call x1, Pallas kernels, run_forward(): pl.pallas_call(attend_forward, out_shape=[jax.ShapeDtypeStruct((TILES, 64...  47.5 us
    pallas_call x2, Pallas kernels, spread_heads(): pl.pallas_call(functools.partial(spread_kernel, count), out_shape=jax.Sha...  38.3 us
    pallas_call x2, Pallas kernels, collect_heads(): pl.pallas_call(functools.partial(collect_kernel, count), out_shape=jax.Sh...  33.8 us
    pallas_call x1, Pallas kernels, gather_weights(): pl.pallas_call(gather_kernel, out_shape=shapes, in_specs=[pl.BlockSpec(me...  27.1 us
    pallas_call x1, Pallas kernels, run_middle(): pl.pallas_call(middle_kernel, grid=(4352 // block,), in_specs=[fixed((108...  21.7 us
    pallas_call x3, Pallas kernels, weight_products(): pl.pallas_call(functools.partial(product_kernel, cut), grid=(size // bloc...  17.2 us
  transfers between devices with their start and end apart: 9, of which 1 were waited for; matrix products, arithmetic and copies ran while one was open for 6% of the time, Pallas kernels for 59%

profile of v6, /device:TPU:8, one launch (start us, length us, event | category | flops | bytes accessed | tf_op | source)
XLA Modules:
  0.0 410.1 jit_solution(1829476384064089072)
XLA Ops:
  0.7 1.2 copy.56
  8.2 1.2 concatenate.31.small
  9.5 27.1 %shard_map.262 = (bf16[4,17,16,3264]{3,2,1,0:T(8,128)(2,1)}, bf16[4,16,272]{2,1,0:T(8,128)(2,1)}) custom-call(bf16[17,16,3264]{2,1,0:T(8,128)(2,1)} %bitcast.152, bf16[16,272]{1,0:T(8,128)(2,1)} %concatenate.31.small), custom_call_target="tpu_custom_call" | custom-call | bytes 20971520 | tf_op jit(solution)/shard_map/pallas_call | solution.py:674
  36.6 1.3 slice_reduce_fusion
  39.4 3.1 copy-done
  42.4 1.6 shard_map.263
  44.0 25.3 %shard_map.264.refs_0_.x_ref = bf16[32,192,128]{2,1,0:T(8,128)(2,1)S(1)} custom-call(bf16[17,192,128]{2,1,0:T(8,128)(2,1)S(1)} %get-tuple-element.49.x_ref), custom_call_target="tpu_custom_call" | custom-call | bytes 4194304 | tf_op jit(solution)/shard_map/pallas_call | solution.py:145
  70.5 47.5 %shard_map.265 = (bf16[32,64,128]{2,1,0:T(8,128)(2,1)}, f32[64,4096]{1,0:T(8,128)}, f32[1,4096]{1,0:T(1,128)}, bf16[4,17,16,1088]{3,2,1,0:T(8,128)(2,1)}, bf16[4...) custom-call(bf16[32,192,128]{2,1,0:T(8,128)(2,1)} %copy-done.6, bf16[17,16,1088]{2,1,0:T(8,128)(2,1)} %bitcast.162, ...), custom_call_target="tpu_custom_call" | custom-call | flops 2147483648 | bytes 4194304 | tf_op jit(solution)/shard_map/pallas_call | solution.py:399
  119.0 12.2 %shard_map.266 = bf16[17,64,128]{2,1,0:T(8,128)(2,1)S(1)} custom-call(bf16[32,64,128]{2,1,0:T(8,128)(2,1)S(1)} %copy-done.11), custom_call_target="tpu_custom_call" | custom-call | bytes 4194304 | tf_op jit(solution)/shard_map/pallas_call | solution.py:163
  131.8 21.7 %shard_map.267 = (bf16[128,1088]{1,0:T(8,128)(2,1)S(1)}, f32[128,1088]{1,0:T(8,128)S(1)}, bf16[1088,128]{1,0:T(8,128)(2,1)S(1)}, bf16[1088,128]{1,0:T(8,128)(2,1...) custom-call(bf16[1088,128]{1,0:T(8,128)(2,1)S(1)} %bitcast.129, ...), custom_call_target="tpu_custom_call" | custom-call | flops 4848615424 | bytes 25165824 | tf_op jit(solution)/shard_map/pallas_call | solution.py:1156
  160.2 13.0 %shard_map.268.g_ref = bf16[32,64,128]{2,1,0:T(8,128)(2,1)S(1)} custom-call(bf16[17,64,128]{2,1,0:T(8,128)(2,1)S(1)} %bitcast.135), custom_call_target="tpu_custom_call" | custom-call | bytes 4194304 | tf_op jit(solution)/shard_map/pallas_call | solution.py:145
  176.6 7.5 %shard_map.270 = bf16[2176,1088]{1,0:T(8,128)(2,1)} custom-call(bf16[2176,128]{1,0:T(8,128)(2,1)} %bitcast.151, bf16[2176,128]{1,0:T(8,128)(2,1)} %collective-permute-done.2.refs_1_, bf16[128,1088]{1,0:T(8,128)(2,1)} %bitcast.128, bf16[128,1088]{1,0:T(8,128)(2,1)} %collective-permute-done.3.refs_3_), custom_call_target="tpu_custom_call" | custom-call | flops 1212153856 | bytes 4734976 | tf_op jit(solution)/shard_map/pallas_call | solution.py:717
  186.2 4.7 %shard_map.269 = bf16[544,4352]{1,0:T(8,128)(2,1)} custom-call(bf16[544,128]{1,0:T(8,128)(2,1)} %bitcast.154, bf16[544,128]{1,0:T(8,128)(2,1)} %collective-permute-done.refs_1_, bf16[128,4352]{1,0:T(8,128)(2,1)} %copy-done.8, bf16[128,4352]{1,0:T(8,128)(2,1)} %collective-permute-done.1.refs_3_), custom_call_target="tpu_custom_call" | custom-call | flops 1212153856 | bytes 4734976 | tf_op jit(solution)/shard_map/pallas_call | solution.py:717
  190.9 56.6 %shard_map.271 = (bf16[32,192,128]{2,1,0:T(8,128)(2,1)}, bf16[3,2,2,16,4352]{4,3,2,1,0:T(8,128)(2,1)}, bf16[3,2,2,64,1088]{4,3,2,1,0:T(8,128)(2,1)}, bf16[3,2,2,...) custom-call(bf16[32,192,128]{2,1,0:T(8,128)(2,1)} %copy-done.6, bf16[32,64,128]{2,1,0:T(8,128)(2,1)} %copy-done.10, ...), custom_call_target="tpu_custom_call" | custom-call | flops 5368709120 | bytes 6291456 | tf_op jit(solution)/shard_map/pallas_call | solution.py:440
  247.5 1.4 copy-done.7
  248.9 21.5 %shard_map.272.packed = bf16[17,192,128]{2,1,0:T(8,128)(2,1)S(1)} custom-call(bf16[32,192,128]{2,1,0:T(8,128)(2,1)S(1)} %copy-done.7), custom_call_target="tpu_custom_call" | custom-call | bytes 4194304 | tf_op jit(solution)/shard_map/pallas_call | solution.py:163
  270.5 3.0 copy-done.1
  273.5 2.6 shard_map.273
  281.9 5.1 %shard_map.274 = bf16[544,4352]{1,0:T(8,128)(2,1)} custom-call(bf16[544,128]{1,0:T(8,128)(2,1)} %bitcast.155, bf16[544,128]{1,0:T(8,128)(2,1)} %collective-permute-done.4.refs_1_, bf16[128,3328]{1,0:T(8,128)(2,1)} %copy-done.9, bf16[128,3328]{1,0:T(8,128)(2,1)} %collective-permute-done.5.refs_3_, bf16[544,128]{1,0:T(8,128)(2,1)} %bitcast.156, ...), custom_call_target="tpu_custom_call" | custom-call | flops 1212153856 | bytes 4734976 | tf_op jit(solution)/shard_map/pallas_call | solution.py:717
  288.5 108.7 %shard_map.275 = (bf16[17,16,4352]{2,1,0:T(8,128)(2,1)}, bf16[17,16,4352]{2,1,0:T(8,128)(2,1)}, bf16[17,64,1088]{2,1,0:T(8,128)(2,1)}, bf16[16,1024]{1,0:T(8,128)(2,1)S(1)}) custom-call(bf16[2,17,16,4352]{3,2,1,0:T(8,128)(2,1)} %bitcast.145, bf16[2,17,16,4352]{3,2,1,0:T(8,128)(2,1)} %bitcast.143, bf16[2,17,64,1088]{3,2,1,0:T(8,128)(2,1)} %bitcast.140, ...), custom_call_target="tpu_custom_call" | custom-call | bytes 41943040 | tf_op jit(solution)/shard_map/pallas_call | solution.py:981
  397.3 3.7 slice_convert_fusion
  401.0 2.4 slice_convert_fusion.1
  404.6 2.8 bitcast_convert_fusion
  407.4 2.6 bitcast_convert_fusion.1
  (126 shorter events, 31.0 us)
Async XLA Ops:
  0.6 38.4 %copy-start.16 = (bf16[1,128,1088]{1,2,0:T(8,128)(2,1)S(1)}, bf16[1,128,1088]{1,2,0:T(8,128)(2,1)}, u32[]{:S(2)}) copy-start(bf16[1,128,1088]{1,2,0:T(8,128)(2,1)} %param.15) | copy-start | bytes 835588
  1.9 129.9 %copy-start.2 = (bf16[1,128,1088]{2,1,0:T(8,128)(2,1)}, bf16[1,128,1088]{2,1,0:T(8,128)(2,1)S(1)}, u32[]{:S(2)}) copy-start(bf16[1,128,1088]{2,1,0:T(8,128)(2,1)S(1)} %copy.56) | copy-start | bytes 835588
  1.9 174.2 %collective-permute-start.3 = (bf16[128,1088]{1,0:T(8,128)(2,1)S(1)}, bf16[128,1088]{1,0:T(8,128)(2,1)}, u32[]{:S(2)}, u32[]{:S(2)}) collective-permute-start(bf16[128,1088]{1,0:T(8,128)(2,1)S(1)} %bitcast.126), channel_id=1, source_target_pairs={{0,1},{1,0},{2,3},{3,2},{4,5},{5,4},{6,7},{7,6},{8,9},{9,8},{10,11... | collective-permute-start | bytes 835592 | tf_op jit(solution)/shard_map/ppermute | solution.py:1288
  39.3 3.1 copy-start
  69.3 1.1 copy-start.6
  153.5 2.5 copy-start.8
  153.5 22.6 %copy-start.12 = (bf16[128,1152]{1,0:T(8,128)(2,1)}, bf16[128,1152]{1,0:T(8,128)(2,1)S(1)}, u32[]{:S(2)}) copy-start(bf16[128,1152]{1,0:T(8,128)(2,1)S(1)} %get-tuple-element.66.refs_6_) | copy-start | bytes 884740
  154.7 21.4 %collective-permute-start.2 = (bf16[2176,128]{1,0:T(8,128)(2,1)}, bf16[2176,128]{1,0:T(8,128)(2,1)}, u32[]{:S(2)}, u32[]{:S(2)}) collective-permute-start(bf16[2176,128]{1,0:T(8,128)(2,1)} %bitcast.23), channel_id=1, source_target_pairs={{0,1},{1,0},{2,3},{3,2},{4,5},{5,4},{6,7},{7,6},{8,9},{9,8},{10,11... | collective-permute-start | bytes 1671176 | tf_op jit(solution)/shard_map/ppermute | solution.py:1288
  155.4 30.7 %collective-permute-start = (bf16[544,128]{1,0:T(8,128)(2,1)}, bf16[544,128]{1,0:T(8,128)(2,1)}, u32[]{:S(2)}, u32[]{:S(2)}) collective-permute-start(bf16[544,128]{1,0:T(8,128)(2,1)} %bitcast.17), channel_id=1, source_target_pairs={{0,1},{1,0},{2,3},{3,2},{4,5},{5,4},{6,7},{7,6},{8,9},{9,8},{10,11... | collective-permute-start | bytes 417800 | tf_op jit(solution)/shard_map/ppermute | solution.py:1288
  155.9 30.2 %collective-permute-start.1 = (bf16[128,4352]{1,0:T(8,128)(2,1)S(1)}, bf16[128,4352]{1,0:T(8,128)(2,1)}, u32[]{:S(2)}, u32[]{:S(2)}) collective-permute-start(bf16[128,4352]{1,0:T(8,128)(2,1)S(1)} %get-tuple-element.59.refs_2_), channel_id=1, source_target_pairs={{0,1},{1,0},{2,3},{3,2},{4,5},{5,4},{6,7},{7,6},{8,9},{9,8},{10,11... | collective-permute-start | bytes 3342344 | tf_op jit(solution)/shard_map/ppermute | solution.py:1288
  156.6 124.2 %collective-permute-start.4 = (bf16[544,128]{1,0:T(8,128)(2,1)}, bf16[544,128]{1,0:T(8,128)(2,1)}, u32[]{:S(2)}, u32[]{:S(2)}) collective-permute-start(bf16[544,128]{1,0:T(8,128)(2,1)} %bitcast.30), channel_id=1, source_target_pairs={{0,1},{1,0},{2,3},{3,2},{4,5},{5,4},{6,7},{7,6},{8,9},{9,8},{10,11... | collective-permute-start | bytes 417800 | tf_op jit(solution)/shard_map/ppermute | solution.py:1288
  176.1 104.8 %collective-permute-start.7 = (bf16[128,1152]{1,0:T(8,128)(2,1)S(1)}, bf16[128,1152]{1,0:T(8,128)(2,1)}, u32[]{:S(2)}, u32[]{:S(2)}) collective-permute-start(bf16[128,1152]{1,0:T(8,128)(2,1)S(1)} %get-tuple-element.66.refs_6_), channel_id=1, source_target_pairs={{0,1},{1,0},{2,3},{3,2},{4,5},{5,4},{6,7},{7,6},{8,9},{9,8},{10,11... | collective-permute-start | bytes 884744 | tf_op jit(solution)/shard_map/ppermute | solution.py:1288
  176.1 104.8 %collective-permute-start.6 = (bf16[544,128]{1,0:T(8,128)(2,1)}, bf16[544,128]{1,0:T(8,128)(2,1)}, u32[]{:S(2)}, u32[]{:S(2)}) collective-permute-start(bf16[544,128]{1,0:T(8,128)(2,1)} %bitcast.35), channel_id=1, source_target_pairs={{0,1},{1,0},{2,3},{3,2},{4,5},{5,4},{6,7},{7,6},{8,9},{9,8},{10,11... | collective-permute-start | bytes 417800 | tf_op jit(solution)/shard_map/ppermute | solution.py:1288
  247.5 1.4 copy-start.7
  270.5 3.1 copy-start.1
  276.1 5.8 %copy-start.9 = (bf16[128,3328]{1,0:T(8,128)(2,1)}, bf16[128,3328]{1,0:T(8,128)(2,1)S(1)}, u32[]{:S(2)}) copy-start(bf16[128,3328]{1,0:T(8,128)(2,1)S(1)} %get-tuple-element.65.refs_2_) | copy-start | bytes 2555908
  277.4 3.3 collective-permute-start.8
  279.2 2.7 collective-permute-start.5
  281.9 6.2 %copy-start.15 = (bf16[2,16,4608]{2,1,0:T(8,128)(2,1)S(1)}, bf16[2,16,4608]{2,1,0:T(8,128)(2,1)}, u32[]{:S(2)}) copy-start(bf16[2,16,4608]{2,1,0:T(8,128)(2,1)} %reshape.190) | copy-start | bytes 884740
  281.9 6.3 %copy-start.4 = (bf16[3,2,2,16,4352]{4,3,2,1,0:T(8,128)(2,1)S(1)}, bf16[3,2,2,16,4352]{4,3,2,1,0:T(8,128)(2,1)}, u32[]{:S(2)}) copy-start(bf16[3,2,2,16,4352]{4,3,2,1,0:T(8,128)(2,1)} %get-tuple-element.71.refs_4_) | copy-start | bytes 5013508
  281.9 6.3 %copy-start.5 = (bf16[3,2,2,16,4352]{4,3,2,1,0:T(8,128)(2,1)S(1)}, bf16[3,2,2,16,4352]{4,3,2,1,0:T(8,128)(2,1)}, u32[]{:S(2)}) copy-start(bf16[3,2,2,16,4352]{4,3,2,1,0:T(8,128)(2,1)} %get-tuple-element.73.refs_6_) | copy-start | bytes 5013508
  287.0 1.6 copy-start.3
  397.3 7.4 %copy-start.13 = (bf16[17,64,1088]{2,1,0:T(8,128)(2,1)S(1)}, bf16[17,64,1088]{2,1,0:T(8,128)(2,1)}, u32[]{:S(2)}) copy-start(bf16[17,64,1088]{2,1,0:T(8,128)(2,1)} %get-tuple-element.78) | copy-start | bytes 7102468
  404.6 2.8 copy-start.14
  (2 other events, 1.8 us)

commit v7 on v6

--- a/solution.py
+++ b/solution.py
@@ -288,7 +288,7 @@
 
     for at in range(blocks):
         pl.when(has)(functools.partial(one_block, at))
-        if at >= 3:
+        if at in (1, 4, 6, 7):
             next(steps, None)
     for _ in steps:
         pass

time: 412 us -> 414 us (level)
  no operation moved by 1% of the time
where the time goes in v7:
time: 414 us; the launch traced here: 412 us
  Pallas kernels  358 us (86%)
  local copies, waits for them, and re-layouts  32.5 us (8%)
  other arithmetic  18 us (4%)
    pallas_call x1, Pallas kernels, last_exchange(): pl.pallas_call(last_kernel, out_shape=[jax.ShapeDtypeStruct((UNITS,) + un...  109 us
    pallas_call x1, Pallas kernels, run_backward(): pl.pallas_call(attend_backward, out_shape=[jax.ShapeDtypeStruct(rows.shap...  56.6 us
    pallas_call x1, Pallas kernels, run_forward(): pl.pallas_call(attend_forward, out_shape=[jax.ShapeDtypeStruct((TILES, 64...  49.1 us
    pallas_call x2, Pallas kernels, spread_heads(): pl.pallas_call(functools.partial(spread_kernel, count), out_shape=jax.Sha...  38.3 us
    pallas_call x2, Pallas kernels, collect_heads(): pl.pallas_call(functools.partial(collect_kernel, count), out_shape=jax.Sh...  34.5 us
    pallas_call x1, Pallas kernels, gather_weights(): pl.pallas_call(gather_kernel, out_shape=shapes, in_specs=[pl.BlockSpec(me...  27.1 us
    pallas_call x1, Pallas kernels, run_middle(): pl.pallas_call(middle_kernel, grid=(4352 // block,), in_specs=[fixed((108...  21.7 us
    pallas_call x3, Pallas kernels, weight_products(): pl.pallas_call(functools.partial(product_kernel, cut), grid=(size // bloc...  17.2 us
  transfers between devices with their start and end apart: 9, of which 1 were waited for; matrix products, arithmetic and copies ran while one was open for 6% of the time, Pallas kernels for 59%

profile of v7, /device:TPU:8, one launch (start us, length us, event | category | flops | bytes accessed | tf_op | source)
XLA Modules:
  0.0 412.4 jit_solution(16048249763809009166)
XLA Ops:
  0.7 1.2 copy.56
  8.2 1.2 concatenate.31.small
  9.5 27.1 %shard_map.262 = (bf16[4,17,16,3264]{3,2,1,0:T(8,128)(2,1)}, bf16[4,16,272]{2,1,0:T(8,128)(2,1)}) custom-call(bf16[17,16,3264]{2,1,0:T(8,128)(2,1)} %bitcast.152, bf16[16,272]{1,0:T(8,128)(2,1)} %concatenate.31.small), custom_call_target="tpu_custom_call" | custom-call | bytes 20971520 | tf_op jit(solution)/shard_map/pallas_call | solution.py:674
  36.6 1.3 slice_reduce_fusion
  39.4 3.1 copy-done
  42.4 1.6 shard_map.263
  44.0 25.3 %shard_map.264.refs_0_.x_ref = bf16[32,192,128]{2,1,0:T(8,128)(2,1)S(1)} custom-call(bf16[17,192,128]{2,1,0:T(8,128)(2,1)S(1)} %get-tuple-element.49.x_ref), custom_call_target="tpu_custom_call" | custom-call | bytes 4194304 | tf_op jit(solution)/shard_map/pallas_call | solution.py:145
  70.5 49.1 %shard_map.265 = (bf16[32,64,128]{2,1,0:T(8,128)(2,1)}, f32[64,4096]{1,0:T(8,128)}, f32[1,4096]{1,0:T(1,128)}, bf16[4,17,16,1088]{3,2,1,0:T(8,128)(2,1)}, bf16[4...) custom-call(bf16[32,192,128]{2,1,0:T(8,128)(2,1)} %copy-done.6, bf16[17,16,1088]{2,1,0:T(8,128)(2,1)} %bitcast.162, ...), custom_call_target="tpu_custom_call" | custom-call | flops 2147483648 | bytes 4194304 | tf_op jit(solution)/shard_map/pallas_call | solution.py:399
  120.6 12.9 %shard_map.266 = bf16[17,64,128]{2,1,0:T(8,128)(2,1)S(1)} custom-call(bf16[32,64,128]{2,1,0:T(8,128)(2,1)S(1)} %copy-done.11), custom_call_target="tpu_custom_call" | custom-call | bytes 4194304 | tf_op jit(solution)/shard_map/pallas_call | solution.py:163
  134.1 21.7 %shard_map.267 = (bf16[128,1088]{1,0:T(8,128)(2,1)S(1)}, f32[128,1088]{1,0:T(8,128)S(1)}, bf16[1088,128]{1,0:T(8,128)(2,1)S(1)}, bf16[1088,128]{1,0:T(8,128)(2,1...) custom-call(bf16[1088,128]{1,0:T(8,128)(2,1)S(1)} %bitcast.129, ...), custom_call_target="tpu_custom_call" | custom-call | flops 4848615424 | bytes 25165824 | tf_op jit(solution)/shard_map/pallas_call | solution.py:1156
  162.5 13.0 %shard_map.268.g_ref = bf16[32,64,128]{2,1,0:T(8,128)(2,1)S(1)} custom-call(bf16[17,64,128]{2,1,0:T(8,128)(2,1)S(1)} %bitcast.135), custom_call_target="tpu_custom_call" | custom-call | bytes 4194304 | tf_op jit(solution)/shard_map/pallas_call | solution.py:145
  178.9 7.5 %shard_map.270 = bf16[2176,1088]{1,0:T(8,128)(2,1)} custom-call(bf16[2176,128]{1,0:T(8,128)(2,1)} %bitcast.151, bf16[2176,128]{1,0:T(8,128)(2,1)} %collective-permute-done.2.refs_1_, bf16[128,1088]{1,0:T(8,128)(2,1)} %bitcast.128, bf16[128,1088]{1,0:T(8,128)(2,1)} %collective-permute-done.3.refs_3_), custom_call_target="tpu_custom_call" | custom-call | flops 1212153856 | bytes 4734976 | tf_op jit(solution)/shard_map/pallas_call | solution.py:717
  188.5 4.7 %shard_map.269 = bf16[544,4352]{1,0:T(8,128)(2,1)} custom-call(bf16[544,128]{1,0:T(8,128)(2,1)} %bitcast.154, bf16[544,128]{1,0:T(8,128)(2,1)} %collective-permute-done.refs_1_, bf16[128,4352]{1,0:T(8,128)(2,1)} %copy-done.8, bf16[128,4352]{1,0:T(8,128)(2,1)} %collective-permute-done.1.refs_3_), custom_call_target="tpu_custom_call" | custom-call | flops 1212153856 | bytes 4734976 | tf_op jit(solution)/shard_map/pallas_call | solution.py:717
  193.2 56.6 %shard_map.271 = (bf16[32,192,128]{2,1,0:T(8,128)(2,1)}, bf16[3,2,2,16,4352]{4,3,2,1,0:T(8,128)(2,1)}, bf16[3,2,2,64,1088]{4,3,2,1,0:T(8,128)(2,1)}, bf16[3,2,2,...) custom-call(bf16[32,192,128]{2,1,0:T(8,128)(2,1)} %copy-done.6, bf16[32,64,128]{2,1,0:T(8,128)(2,1)} %copy-done.10, ...), custom_call_target="tpu_custom_call" | custom-call | flops 5368709120 | bytes 6291456 | tf_op jit(solution)/shard_map/pallas_call | solution.py:440
  249.9 1.4 copy-done.7
  251.3 21.5 %shard_map.272.packed = bf16[17,192,128]{2,1,0:T(8,128)(2,1)S(1)} custom-call(bf16[32,192,128]{2,1,0:T(8,128)(2,1)S(1)} %copy-done.7), custom_call_target="tpu_custom_call" | custom-call | bytes 4194304 | tf_op jit(solution)/shard_map/pallas_call | solution.py:163
  272.8 3.0 copy-done.1
  275.9 2.6 shard_map.273
  284.2 5.1 %shard_map.274 = bf16[544,4352]{1,0:T(8,128)(2,1)} custom-call(bf16[544,128]{1,0:T(8,128)(2,1)} %bitcast.155, bf16[544,128]{1,0:T(8,128)(2,1)} %collective-permute-done.4.refs_1_, bf16[128,3328]{1,0:T(8,128)(2,1)} %copy-done.9, bf16[128,3328]{1,0:T(8,128)(2,1)} %collective-permute-done.5.refs_3_, bf16[544,128]{1,0:T(8,128)(2,1)} %bitcast.156, ...), custom_call_target="tpu_custom_call" | custom-call | flops 1212153856 | bytes 4734976 | tf_op jit(solution)/shard_map/pallas_call | solution.py:717
  290.9 108.7 %shard_map.275 = (bf16[17,16,4352]{2,1,0:T(8,128)(2,1)}, bf16[17,16,4352]{2,1,0:T(8,128)(2,1)}, bf16[17,64,1088]{2,1,0:T(8,128)(2,1)}, bf16[16,1024]{1,0:T(8,128)(2,1)S(1)}) custom-call(bf16[2,17,16,4352]{3,2,1,0:T(8,128)(2,1)} %bitcast.145, bf16[2,17,16,4352]{3,2,1,0:T(8,128)(2,1)} %bitcast.143, bf16[2,17,64,1088]{3,2,1,0:T(8,128)(2,1)} %bitcast.140, ...), custom_call_target="tpu_custom_call" | custom-call | bytes 41943040 | tf_op jit(solution)/shard_map/pallas_call | solution.py:981
  399.6 3.7 slice_convert_fusion
  403.3 2.4 slice_convert_fusion.1
  406.9 2.8 bitcast_convert_fusion
  409.7 2.6 bitcast_convert_fusion.1
  (126 shorter events, 31.0 us)
Async XLA Ops:
  0.6 38.4 %copy-start.16 = (bf16[1,128,1088]{1,2,0:T(8,128)(2,1)S(1)}, bf16[1,128,1088]{1,2,0:T(8,128)(2,1)}, u32[]{:S(2)}) copy-start(bf16[1,128,1088]{1,2,0:T(8,128)(2,1)} %param.15) | copy-start | bytes 835588
  1.9 132.2 %copy-start.2 = (bf16[1,128,1088]{2,1,0:T(8,128)(2,1)}, bf16[1,128,1088]{2,1,0:T(8,128)(2,1)S(1)}, u32[]{:S(2)}) copy-start(bf16[1,128,1088]{2,1,0:T(8,128)(2,1)S(1)} %copy.56) | copy-start | bytes 835588
  1.9 176.6 %collective-permute-start.3 = (bf16[128,1088]{1,0:T(8,128)(2,1)S(1)}, bf16[128,1088]{1,0:T(8,128)(2,1)}, u32[]{:S(2)}, u32[]{:S(2)}) collective-permute-start(bf16[128,1088]{1,0:T(8,128)(2,1)S(1)} %bitcast.126), channel_id=1, source_target_pairs={{0,1},{1,0},{2,3},{3,2},{4,5},{5,4},{6,7},{7,6},{8,9},{9,8},{10,11... | collective-permute-start | bytes 835592 | tf_op jit(solution)/shard_map/ppermute | solution.py:1288
  39.3 3.1 copy-start
  69.3 1.1 copy-start.6
  155.8 2.5 copy-start.8
  155.8 22.6 %copy-start.12 = (bf16[128,1152]{1,0:T(8,128)(2,1)}, bf16[128,1152]{1,0:T(8,128)(2,1)S(1)}, u32[]{:S(2)}) copy-start(bf16[128,1152]{1,0:T(8,128)(2,1)S(1)} %get-tuple-element.66.refs_6_) | copy-start | bytes 884740
  157.0 21.4 %collective-permute-start.2 = (bf16[2176,128]{1,0:T(8,128)(2,1)}, bf16[2176,128]{1,0:T(8,128)(2,1)}, u32[]{:S(2)}, u32[]{:S(2)}) collective-permute-start(bf16[2176,128]{1,0:T(8,128)(2,1)} %bitcast.23), channel_id=1, source_target_pairs={{0,1},{1,0},{2,3},{3,2},{4,5},{5,4},{6,7},{7,6},{8,9},{9,8},{10,11... | collective-permute-start | bytes 1671176 | tf_op jit(solution)/shard_map/ppermute | solution.py:1288
  157.8 30.7 %collective-permute-start = (bf16[544,128]{1,0:T(8,128)(2,1)}, bf16[544,128]{1,0:T(8,128)(2,1)}, u32[]{:S(2)}, u32[]{:S(2)}) collective-permute-start(bf16[544,128]{1,0:T(8,128)(2,1)} %bitcast.17), channel_id=1, source_target_pairs={{0,1},{1,0},{2,3},{3,2},{4,5},{5,4},{6,7},{7,6},{8,9},{9,8},{10,11... | collective-permute-start | bytes 417800 | tf_op jit(solution)/shard_map/ppermute | solution.py:1288
  158.3 30.2 %collective-permute-start.1 = (bf16[128,4352]{1,0:T(8,128)(2,1)S(1)}, bf16[128,4352]{1,0:T(8,128)(2,1)}, u32[]{:S(2)}, u32[]{:S(2)}) collective-permute-start(bf16[128,4352]{1,0:T(8,128)(2,1)S(1)} %get-tuple-element.59.refs_2_), channel_id=1, source_target_pairs={{0,1},{1,0},{2,3},{3,2},{4,5},{5,4},{6,7},{7,6},{8,9},{9,8},{10,11... | collective-permute-start | bytes 3342344 | tf_op jit(solution)/shard_map/ppermute | solution.py:1288
  159.0 124.2 %collective-permute-start.4 = (bf16[544,128]{1,0:T(8,128)(2,1)}, bf16[544,128]{1,0:T(8,128)(2,1)}, u32[]{:S(2)}, u32[]{:S(2)}) collective-permute-start(bf16[544,128]{1,0:T(8,128)(2,1)} %bitcast.30), channel_id=1, source_target_pairs={{0,1},{1,0},{2,3},{3,2},{4,5},{5,4},{6,7},{7,6},{8,9},{9,8},{10,11... | collective-permute-start | bytes 417800 | tf_op jit(solution)/shard_map/ppermute | solution.py:1288
  178.4 104.8 %collective-permute-start.7 = (bf16[128,1152]{1,0:T(8,128)(2,1)S(1)}, bf16[128,1152]{1,0:T(8,128)(2,1)}, u32[]{:S(2)}, u32[]{:S(2)}) collective-permute-start(bf16[128,1152]{1,0:T(8,128)(2,1)S(1)} %get-tuple-element.66.refs_6_), channel_id=1, source_target_pairs={{0,1},{1,0},{2,3},{3,2},{4,5},{5,4},{6,7},{7,6},{8,9},{9,8},{10,11... | collective-permute-start | bytes 884744 | tf_op jit(solution)/shard_map/ppermute | solution.py:1288
  178.4 104.8 %collective-permute-start.6 = (bf16[544,128]{1,0:T(8,128)(2,1)}, bf16[544,128]{1,0:T(8,128)(2,1)}, u32[]{:S(2)}, u32[]{:S(2)}) collective-permute-start(bf16[544,128]{1,0:T(8,128)(2,1)} %bitcast.35), channel_id=1, source_target_pairs={{0,1},{1,0},{2,3},{3,2},{4,5},{5,4},{6,7},{7,6},{8,9},{9,8},{10,11... | collective-permute-start | bytes 417800 | tf_op jit(solution)/shard_map/ppermute | solution.py:1288
  249.8 1.4 copy-start.7
  272.8 3.1 copy-start.1
  278.5 5.8 %copy-start.9 = (bf16[128,3328]{1,0:T(8,128)(2,1)}, bf16[128,3328]{1,0:T(8,128)(2,1)S(1)}, u32[]{:S(2)}) copy-start(bf16[128,3328]{1,0:T(8,128)(2,1)S(1)} %get-tuple-element.65.refs_2_) | copy-start | bytes 2555908
  279.8 3.3 collective-permute-start.8
  281.5 2.7 collective-permute-start.5
  284.2 6.2 %copy-start.15 = (bf16[2,16,4608]{2,1,0:T(8,128)(2,1)S(1)}, bf16[2,16,4608]{2,1,0:T(8,128)(2,1)}, u32[]{:S(2)}) copy-start(bf16[2,16,4608]{2,1,0:T(8,128)(2,1)} %reshape.190) | copy-start | bytes 884740
  284.2 6.3 %copy-start.4 = (bf16[3,2,2,16,4352]{4,3,2,1,0:T(8,128)(2,1)S(1)}, bf16[3,2,2,16,4352]{4,3,2,1,0:T(8,128)(2,1)}, u32[]{:S(2)}) copy-start(bf16[3,2,2,16,4352]{4,3,2,1,0:T(8,128)(2,1)} %get-tuple-element.71.refs_4_) | copy-start | bytes 5013508
  284.2 6.3 %copy-start.5 = (bf16[3,2,2,16,4352]{4,3,2,1,0:T(8,128)(2,1)S(1)}, bf16[3,2,2,16,4352]{4,3,2,1,0:T(8,128)(2,1)}, u32[]{:S(2)}) copy-start(bf16[3,2,2,16,4352]{4,3,2,1,0:T(8,128)(2,1)} %get-tuple-element.73.refs_6_) | copy-start | bytes 5013508
  289.3 1.6 copy-start.3
  399.6 7.4 %copy-start.13 = (bf16[17,64,1088]{2,1,0:T(8,128)(2,1)S(1)}, bf16[17,64,1088]{2,1,0:T(8,128)(2,1)}, u32[]{:S(2)}) copy-start(bf16[17,64,1088]{2,1,0:T(8,128)(2,1)} %get-tuple-element.78) | copy-start | bytes 7102468
  406.9 2.8 copy-start.14
  (2 other events, 1.8 us)
